TPU v7x, 512 devices: a whole 4x8x8 slice. The times are simulated.
512 devices in a mesh: row: 32 (over y_hi, z), col: 16 (over y_lo, x, core).
Axes of the slice: x: 4, y: 8 (y_hi: 4, y_lo: 2; y = y_hi * 2 + y_lo), z: 8, core: 2. Of those that a mesh axis runs over, the one named last changes fastest.
Arguments:
- q_proj: bfloat16 [4096, 8192], P('row', 'col'), may hold values from -6 to 6
- k_proj: bfloat16 [4096, 8192], P('row', 'col'), may hold values from -6 to 6
- v_proj: bfloat16 [4096, 8192], P('row', 'col'), may hold values from -6 to 6
- filters: float32 [128, 512], P(None, 'col'), may hold values from -0.5 to 0.5
- w_out: bfloat16 [8192, 4096], P('col', 'row'), may hold values from -0.125 to 0.125
- cotangent: bfloat16 [4096, 4096], P('row', 'col'), may hold values from -1.5 to 1.5
Outputs:
- projected: bfloat16 [4096, 4096], P('row', 'col')
- grad_q: bfloat16 [4096, 8192], P('row', 'col')
- grad_k: bfloat16 [4096, 8192], P('row', 'col')
- grad_v: bfloat16 [4096, 8192], P('row', 'col')
- grad_filters: float32 [128, 512], P(None, 'col')
- grad_w: float32 [8192, 4096], P('col', 'row')
All inputs are finite; a program needn't handle non-finite values.
Results may differ from a plain program's by a relative error of at most 0.0058.
Values may be sent and summed in bfloat16 or wider, within the bound.
No kernel may reach another device: no remote copies, remote signals or barrier semaphores. Data moves between devices by JAX's collectives and lax.ppermute only.
A program may use at most 64 MiB of HBM per device.

v0:
```python
import math

import jax
import jax.numpy as jnp
from jax import lax
from jax.sharding import PartitionSpec as P


def from_behind(block, axis, distance):
    devices = range(lax.axis_size(axis))
    route = [(i - distance, i) for i in devices if i - distance in devices]
    return lax.ppermute(block, axis, route)


def toeplitz(block_taps, rows):
    taps, groups = block_taps.shape
    width = rows + taps - 1
    period = width + 1
    front = jnp.concatenate(
        [block_taps[::-1].T, jnp.zeros((groups, period - taps), jnp.float32)], 1
    )
    tiled = jnp.tile(front, (1, rows))[:, : rows * width]
    return tiled.reshape(groups, rows, width)


def filter_block(block_taps, extended):
    rows = extended.shape[0] - block_taps.shape[0] + 1
    matrix = toeplitz(block_taps, rows)
    return jnp.einsum("gts,sgc->tgc", matrix, extended, precision=lax.Precision.HIGHEST)


def filter_grads(block_taps, extended, upstream):
    rows = upstream.shape[0]
    matrix = toeplitz(block_taps, rows)
    grad_ext = jnp.einsum("gts,tgc->sgc", matrix, upstream, precision=lax.Precision.HIGHEST)
    grad_matrix = jnp.einsum("tgc,sgc->gts", upstream, extended, precision=lax.Precision.HIGHEST)
    unused, pullback = jax.vjp(lambda values: toeplitz(values, rows), block_taps)
    return (pullback(grad_matrix)[0], grad_ext)


def local(q_proj, k_proj, v_proj, filters, w_out, cotangent):
    tok_rows, features = q_proj.shape
    taps, local_groups = filters.shape
    group_width = features // local_groups
    block_size = math.gcd(local_groups, 8)
    blocks = local_groups // block_size
    span = tok_rows + taps - 1
    product = (k_proj.astype(jnp.float32) * v_proj.astype(jnp.float32)).astype(jnp.bfloat16)
    earlier = from_behind(product[tok_rows - (taps - 1) :], "row", 1)
    extended = jnp.concatenate([earlier, product], 0).astype(jnp.float32)
    ext_blocks = extended.reshape(span, blocks, block_size, group_width).transpose(1, 0, 2, 3)
    tap_blocks = filters.reshape(taps, blocks, block_size).transpose(1, 0, 2)
    conv_blocks = lax.map(lambda pair: filter_block(pair[0], pair[1]), (tap_blocks, ext_blocks))
    conv = conv_blocks.transpose(1, 0, 2, 3).reshape(tok_rows, features)
    mixed = (q_proj.astype(jnp.float32) * conv).astype(jnp.bfloat16)
    partial_value = jnp.dot(
        mixed, lax.all_gather(w_out, "row", axis=1, tiled=True), preferred_element_type=jnp.float32
    )
    projected = lax.psum_scatter(partial_value, "col", scatter_dimension=1, tiled=True).astype(
        jnp.bfloat16
    )
    cot_rows = lax.all_gather(cotangent, "col", axis=1, tiled=True)
    grad_mixed = lax.dot_general(
        cot_rows,
        lax.all_gather(w_out, "row", axis=1, tiled=True),
        (((1,), (1,)), ((), ())),
        preferred_element_type=jnp.float32,
    )
    grad_q = (grad_mixed * conv).astype(jnp.bfloat16)
    grad_conv = grad_mixed * q_proj.astype(jnp.float32)
    upstream = grad_conv.reshape(tok_rows, blocks, block_size, group_width).transpose(1, 0, 2, 3)
    grad_tap_blocks, grad_ext_blocks = lax.map(
        lambda triple: filter_grads(triple[0], triple[1], triple[2]),
        (tap_blocks, ext_blocks, upstream),
    )
    grad_taps = grad_tap_blocks.transpose(1, 0, 2).reshape(taps, local_groups)
    grad_filters = lax.psum(grad_taps, "row")
    grad_ext = grad_ext_blocks.transpose(1, 0, 2, 3).reshape(span, features)
    later = from_behind(grad_ext[: taps - 1], "row", -1)
    grad_product = grad_ext[taps - 1 :] + jnp.concatenate(
        [jnp.zeros((tok_rows - (taps - 1), features), jnp.float32), later], 0
    )
    grad_k = (grad_product * v_proj.astype(jnp.float32)).astype(jnp.bfloat16)
    grad_v = (grad_product * k_proj.astype(jnp.float32)).astype(jnp.bfloat16)
    cot_columns = lax.all_to_all(cot_rows, "row", split_axis=1, concat_axis=0, tiled=True)
    grad_w = lax.dot_general(
        lax.all_gather(mixed, "row", axis=0, tiled=True),
        cot_columns,
        (((0,), (0,)), ((), ())),
        preferred_element_type=jnp.float32,
    )
    return (projected, grad_q, grad_k, grad_v, grad_filters, grad_w)


def solution(mesh):
    placed = (
        P("row", "col"),
        P("row", "col"),
        P("row", "col"),
        P(None, "col"),
        P("col", "row"),
        P("row", "col"),
    )
    return jax.shard_map(
        local,
        mesh=mesh,
        in_specs=placed,
        out_specs=(
            P("row", "col"),
            P("row", "col"),
            P("row", "col"),
            P("row", "col"),
            P(None, "col"),
            P("col", "row"),
        ),
        check_vma=False,
    )
```

profile of v0, /device:TPU:4, one launch (start us, length us, event | category | flops | bytes accessed | tf_op | source)
XLA Modules:
  0.0 387.3 jit_solution(17585104031599551337)
XLA Ops:
  7.2 1.6 copy.28
  11.8 4.3 %collective-permute-start = (bf16[127,512]{0,1:T(8,128)(2,1)S(1)}, bf16[127,512]{0,1:T(8,128)(2,1)S(1)}, u32[]{:S(2)}, u32[]{:S(2)}) collective-permute-start(bf16[127,512]{0,1:T(8,128)(2,1)S(1)} %slice.28), channel_id=1, source_target_pairs={{0,16},{16,32},{32,48},{48,64},{64,80},{80,96},{96,112},{112,128},... | collective-permute-start | bytes 390152 | tf_op jit(solution)/shard_map/ppermute | solution.py:12
  16.1 2.7 collective-permute-done
  19.0 13.2 %while.22 = (s32[]{:T(128)}, f32[4,128,8,16]{1,3,2,0:T(8,128)S(1)}, f32[4,255,8,16]{1,3,2,0:T(8,128)S(1)}, f32[4,128,8]{1,2,0:T(8,128)}, s32[]{:T(128)}, /*index=5*/f32[]{:T(128)}) while((s32[]{:T(128)}, f32[4,128,8,16]{1,3,2,0:T(8,128)S(1)}, f32[4,255,8,16]{1,3,2,0:T(8,128)S(1)}, f32[4,128,8]{1,2,0:T(8,128)}, s32[]{:T(128)}, ...), condition=%wide.region_1.2_spmd, body=%wide.region_0.1_spmd.sunk | while | flops 50135040 | bytes 6509653 | solution.py:53
  20.0 1.4 reshape.61
  23.3 1.4 reshape.61
  26.6 1.4 reshape.61
  29.9 1.4 reshape.61
  32.4 19.8 %all-gather.6.cloned.1.call-done = bf16[128,4096]{0,1:T(8,128)(2,1)} async-done(((bf16[128,256]{0,1:T(8,128)(2,1)}), bf16[128,4096]{0,1:T(8,128)(2,1)}) %all-gather.6.cloned.1.call-update) | async-done | bytes 1048592 | tf_op jit(solution)/shard_map/all_gather | solution.py:62
  52.2 107.1 %all-gather.4.cloned.1.call-done = bf16[512,4096]{1,0:T(8,128)(2,1)} async-done(((bf16[512,128]{1,0:T(8,128)(2,1)}), bf16[512,4096]{1,0:T(8,128)(2,1)}) %all-gather.4.cloned.1.call-update) | async-done | bytes 4194320 | tf_op jit(solution)/shard_map/all_gather | solution.py:57
  159.3 4.7 %convert_multiply_fusion.3 = (f32[128,512]{1,0:T(8,128)S(1)}, bf16[128,512]{1,0:T(8,128)(2,1)}, bf16[128,512]{1,0:T(8,128)(2,1)S(1)}) fusion(bf16[128,512]{1,0:T(8,128)(2,1)S(1)} %copy-done.1, f32[128,512]{1,0:T(8,128)S(1)} %copy.27, bf16[128,4096]{0,1:T(8,128)(2,1)} %all-gather.6.cloned.1.call-done, bf16[512,4096]{1,0:T(8,128)(2,1)} %all-gather.4.cloned.1.call-done), kind=kOutput, calls=%fused_computation.24 | convolution fusion | flops 537264128 | bytes 6160384 | tf_op jit(solution)/shard_map/dot_general | solution.py:63
  164.0 4.3 %fusion.18 = f32[128,4096]{1,0:T(8,128)} fusion(bf16[128,512]{1,0:T(8,128)(2,1)S(1)} %get-tuple-element.100, bf16[512,4096]{1,0:T(8,128)(2,1)} %all-gather.4.cloned.1.call-done), kind=kOutput, calls=%fused_computation.32 | convolution fusion | flops 536870912 | bytes 6422528 | tf_op jit(solution)/shard_map/dot_general | solution.py:56
  168.9 6.6 %all-to-all-start = ((bf16[128,32,128]{0,2,1:T(8,128)(2,1)}), bf16[128,32,128]{0,2,1:T(8,128)(2,1)}, u32[]{:S(2)}, u32[]{:S(2)}) async-start(bf16[128,32,128]{0,2,1:T(8,128)(2,1)} %bitcast.32), calls=%async_computation.1 | async-start | bytes 2097152 | tf_op jit(solution)/shard_map/all_to_all | solution.py:85
  175.7 22.3 %while.23 = (s32[]{:T(128)}, f32[4,128,8]{1,2,0:T(8,128)S(1)}, f32[4,255,8,16]{1,3,2,0:T(8,128)}, f32[4,128,8,16]{1,3,2,0:T(8,128)S(1)}, f32[4,255,8,16]{1,3,2,0...) while((s32[]{:T(128)}, f32[4,128,8]{1,2,0:T(8,128)S(1)}, f32[4,255,8,16]{1,3,2,0:T(8,128)}, ...), condition=%wide.region_5.6_spmd, body=%wide.region_3.5_spmd.sunk | while | flops 100530176 | bytes 13015153 | solution.py:72
  178.6 1.4 reshape.63
  184.2 1.4 reshape.63
  189.7 1.4 reshape.63
  195.3 1.4 reshape.63
  199.0 1.3 collective-permute-start.1
  200.3 8.4 %all-to-all-done = bf16[128,32,128]{0,2,1:T(8,128)(2,1)} async-done(((bf16[128,32,128]{0,2,1:T(8,128)(2,1)}), bf16[128,32,128]{0,2,1:T(8,128)(2,1)}, u32[]{:S(2)}, u32[]{:S(2)}) %all-to-all-start) | async-done | bytes 1048608 | tf_op jit(solution)/shard_map/all_to_all | solution.py:85
  208.7 1.6 copy.31
  211.5 161.9 %psum.7 = f32[128,32]{0,1:T(8,128)} all-reduce(f32[128,32]{0,1:T(8,128)S(1)} %bitcast.119), channel_id=1, replica_groups=mesh['row'=32,'col'=16] {'row'}, use_global_device_ids=true, to_apply=%region_6.7 | all-reduce | flops 4096 | bytes 32768 | tf_op jit(solution)/shard_map/psum | solution.py:77
  375.0 1.5 convert_element_type.37
  376.6 4.2 %fusion.19 = f32[512,128]{1,0:T(8,128)} fusion(bf16[4096,512]{1,0:T(8,128)(2,1)} %all-gather.8.cloned.1.call-done, bf16[4096,128]{1,0:T(8,128)(2,1)S(1)} %bitcast.108), kind=kOutput, calls=%fused_computation.33 | convolution fusion | flops 536870912 | bytes 5505024 | tf_op jit(solution)/shard_map/dot_general | solution.py:86
  (106 shorter events, 31.8 us)
Async XLA Ops:
  7.2 45.1 %all-gather.6.cloned.1.call-start = ((), (), s32[]{:S(2)}) async-start(), calls=%async_computation.4 | async-start | bytes 1114112 | tf_op jit(solution)/shard_map/all_gather | solution.py:62
  8.8 150.5 %all-gather.4.cloned.1.call-start = ((), (), s32[]{:S(2)}) async-start(), calls=%async_computation.2 | async-start | bytes 4325376 | tf_op jit(solution)/shard_map/all_gather | solution.py:57
  9.6 365.5 %reduce-scatter.2.cloned.1.call-start = ((), (), s32[]{:S(2)}) async-start(), calls=%async_computation.3 | async-start | bytes 2228224 | tf_op jit(solution)/shard_map/reduce_scatter | solution.py:59
  11.8 7.0 %collective-permute-start = (bf16[127,512]{0,1:T(8,128)(2,1)S(1)}, bf16[127,512]{0,1:T(8,128)(2,1)S(1)}, u32[]{:S(2)}, u32[]{:S(2)}) collective-permute-start(bf16[127,512]{0,1:T(8,128)(2,1)S(1)} %slice.28), channel_id=1, source_target_pairs={{0,16},{16,32},{32,48},{48,64},{64,80},{80,96},{96,112},{112,128},... | collective-permute-start | bytes 390152 | tf_op jit(solution)/shard_map/ppermute | solution.py:12
  19.0 140.3 %copy-start.1 = (bf16[128,512]{1,0:T(8,128)(2,1)S(1)}, bf16[128,512]{1,0:T(8,128)(2,1)}, u32[]{:S(2)}) copy-start(bf16[128,512]{1,0:T(8,128)(2,1)} %param.10) | copy-start | bytes 393220
  164.0 4.3 %copy-start = (bf16[128,512]{1,0:T(8,128)(2,1)}, bf16[128,512]{1,0:T(8,128)(2,1)S(1)}, u32[]{:S(2)}) copy-start(bf16[128,512]{1,0:T(8,128)(2,1)S(1)} %get-tuple-element.100) | copy-start | bytes 393220
  168.3 208.2 %all-gather.8.cloned.1.call-start = ((), (), s32[]{:S(2)}) async-start(), calls=%async_computation.5 | async-start | bytes 4325376 | tf_op jit(solution)/shard_map/all_gather | solution.py:87
  168.9 39.7 %all-to-all-start = ((bf16[128,32,128]{0,2,1:T(8,128)(2,1)}), bf16[128,32,128]{0,2,1:T(8,128)(2,1)}, u32[]{:S(2)}, u32[]{:S(2)}) async-start(bf16[128,32,128]{0,2,1:T(8,128)(2,1)} %bitcast.32), calls=%async_computation.1 | async-start | bytes 2097152 | tf_op jit(solution)/shard_map/all_to_all | solution.py:85
  199.0 174.4 %collective-permute-start.1 = (f32[127,512]{0,1:T(8,128)S(1)}, f32[127,512]{0,1:T(8,128)S(1)}, u32[]{:S(2)}, u32[]{:S(2)}) collective-permute-start(f32[127,512]{0,1:T(8,128)S(1)} %bitcast.115), channel_id=1, source_target_pairs={{16,0},{32,16},{48,32},{64,48},{80,64},{96,80},{112,96},{128,112},... | collective-permute-start | bytes 780296 | tf_op jit(solution)/shard_map/ppermute | solution.py:12
Sparse Core Ops, SparseCore 0:
  10.7 41.4 all-gather.5
  55.3 103.9 all-gather.3
  168.5 67.9 reduce-scatter.1
  240.1 108.6 all-gather.7
where the time goes:
time: 388 us; the launch traced here: 387 us
  blocking collectives  162 us (42%)
  waiting for transfers between devices  139 us (36%)
  local copies, waits for them, and re-layouts  30.9 us (8%)
  matrix products  26.2 us (7%)
  between operations  13.9 us (4%)
  starting transfers between devices  12.4 us (3%)
    psum x1, blocking collectives, local(): grad_filters = lax.psum(grad_taps, 'row')  162 us
    all_gather x1, waiting for transfers between devices, local(): lax.all_gather(w_out, 'row', axis=1, tiled=True)  107 us
    all_gather x1, waiting for transfers between devices, local(): cot_rows = lax.all_gather(cotangent, 'col', axis=1, tiled=True)  19.8 us
    reshape x12, local copies, waits for them, and re-layouts, toeplitz(): return tiled.reshape(groups, rows, width)  13.6 us
    all_to_all x1, waiting for transfers between devices, local(): lax.all_to_all(cot_rows, 'row', split_axis=1, concat_axis=0, tiled=True)  8.42 us
  transfers between devices with their start and end apart: 7, of which 4 were waited for; matrix products, arithmetic and copies ran while one was open for 12% of the time, Pallas kernels for 0%

commit v1 on v0

v1 whole, which is shorter than its diff:
```python
import functools

import jax
import jax.numpy as jnp
from jax import lax
from jax.experimental import pallas as pl
from jax.experimental.pallas import tpu as pltpu
from jax.sharding import PartitionSpec as P

YS, ZS, COLS = 4, 8, 16
F32, BF16 = jnp.float32, jnp.bfloat16
NT = (((1,), (1,)), ((), ()))
TN = (((0,), (0,)), ((), ()))
NN = (((1,), (0,)), ((), ()))
Z_GROUPS = [[y * ZS + z for z in range(ZS)] for y in range(YS)]
Y_GROUPS = [[y * ZS + z for y in range(YS)] for z in range(ZS)]
CHIP_GROUPS = [[2 * i + core for i in range(8)] for core in range(2)]


def call(body, out_shape, args, scratch=(), flops=0, position=None, after=()):
    outs = out_shape if isinstance(out_shape, (list, tuple)) else [out_shape]
    size = sum(a.size * a.dtype.itemsize for a in args) + sum(
        o.size * jnp.dtype(o.dtype).itemsize for o in outs
    )
    specs = [pl.BlockSpec(memory_space=pltpu.VMEM)] * len(args)
    n_args = len(args)
    operands = list(args)
    if position is not None:
        specs = [pl.BlockSpec(memory_space=pltpu.SMEM)] + specs
        operands = [position] + operands
        n_args += 1
    specs += [pl.BlockSpec(memory_space=pl.ANY)] * len(after)
    operands += list(after)

    def run(*refs):
        body(*refs[:n_args], *refs[n_args + len(after) :])

    return pl.pallas_call(
        run,
        out_shape=out_shape,
        in_specs=specs,
        scratch_shapes=list(scratch),
        compiler_params=pltpu.CompilerParams(vmem_limit_bytes=40 * 1024 * 1024),
        cost_estimate=pl.CostEstimate(flops=flops, bytes_accessed=size, transcendentals=0),
    )(*operands)


def shaped(shape, dtype):
    return jax.ShapeDtypeStruct(shape, dtype)


def iotas(rows, cols):
    return (
        lax.broadcasted_iota(jnp.int32, (rows, cols), 0),
        lax.broadcasted_iota(jnp.int32, (rows, cols), 1),
    )


def circulant(row):
    size = row.shape[1]
    return pltpu.roll(jnp.broadcast_to(row, (size, size)), 0, axis=1, stride=1, stride_axis=0)


def apply_filters(first_rows, keep_own, own, other, stack, out, exact):
    size = own.shape[0]
    lanes = lax.broadcasted_iota(jnp.int32, (size, 128), 1) // 16
    for tile in range(own.shape[1] // 128):
        cols = slice(tile * 128, tile * 128 + 128)
        for g in range(8):
            c = circulant(first_rows[tile * 8 + g : tile * 8 + g + 1, :])
            rows = slice(g * size, (g + 1) * size)
            for part in range(2 if exact else 1):
                rounded = c.astype(BF16).astype(F32)
                at = 2 * size * part
                stack[rows, at : at + size] = jnp.where(keep_own, rounded, 0.0).astype(BF16)
                stack[rows, at + size : at + 2 * size] = jnp.where(keep_own, 0.0, rounded).astype(BF16)
                c = c - rounded
        both = jnp.concatenate([own[:, cols], other[:, cols]] * (2 if exact else 1), 0)
        r = lax.dot_general(stack[...], both, NN, preferred_element_type=F32)
        acc = r[:size]
        for g in range(1, 8):
            acc = jnp.where(lanes == g, r[g * size : (g + 1) * size], acc)
        out[:, cols] = acc


def conv_body(rows_ref, product_ref, halo_ref, q_ref, conv_ref, mixed_ref, stack):
    row, lane = iotas(128, 128)
    apply_filters(rows_ref, lane <= row, product_ref, halo_ref, stack, conv_ref, True)
    mixed_ref[...] = (q_ref[...].astype(F32) * conv_ref[...]).astype(BF16)


def spread_body(piece_ref, out_ref):
    for i in range(8):
        out_ref[i] = piece_ref[...]


def grad_mixed_body(at_ref, own_ref, pair_ref, w_ref, cot_ref, out_ref):
    core = at_ref[1]
    for i in range(8):
        cot_ref[2 * i + core] = own_ref[i]
        cot_ref[2 * i + 1 - core] = pair_ref[i]
    w = jnp.concatenate([w_ref[z] for z in range(ZS)], 1)
    for y in range(YS):
        lhs = jnp.concatenate([cot_ref[4 * y + k] for k in range(4)], 1)
        out_ref[y] = lax.dot_general(lhs, w, NT, preferred_element_type=F32).astype(BF16)


def projected_body(at_ref, m0_ref, m1_ref, m2_ref, m3_ref, w_ref, keep_ref, give_ref, total):
    y, core = at_ref[0], at_ref[1]
    mixed = jnp.concatenate([m[...] for m in (m0_ref, m1_ref, m2_ref, m3_ref)], 0)
    for k in range(4):
        w = jnp.concatenate([w_ref[2 * k], w_ref[2 * k + 1]], 1)
        r = lax.dot_general(mixed, w, NN, preferred_element_type=F32)
        for d in range(YS):
            total[4 * lax.rem(y + YS - d, YS) + k] = r[d * 128 : d * 128 + 128]
    for i in range(8):
        keep_ref[i] = total[2 * i + core]
        give_ref[i] = total[2 * i + 1 - core].astype(BF16)


def pair_body(keep_ref, got_ref, out_ref):
    for i in range(8):
        out_ref[i] = (keep_ref[i] + got_ref[i].astype(F32)).astype(BF16)


def taps_body(taps_ref, out_ref):
    taps = taps_ref[...].astype(BF16)
    for i in range(YS * ZS):
        out_ref[i] = taps


def grad_w_body(at_ref, m0_ref, m1_ref, m2_ref, m3_ref, cot_ref, out_ref):
    mixed = jnp.concatenate([m[...] for m in (m0_ref, m1_ref, m2_ref, m3_ref)], 0)
    for k in range(4):
        cot = jnp.concatenate([cot_ref[4 * lax.rem(at_ref[0] + YS - d, YS) + k] for d in range(YS)], 0)
        r = lax.dot_general(mixed, cot, TN, preferred_element_type=F32).astype(BF16)
        out_ref[2 * k] = r[:, :128]
        out_ref[2 * k + 1] = r[:, 128:]


def grad_conv_body(shares_ref, q_ref, conv_ref, grad_q_ref, grad_conv_ref):
    g = shares_ref[0].astype(F32)
    for y in range(1, YS):
        g = g + shares_ref[y].astype(F32)
    grad_q_ref[...] = (g * conv_ref[...]).astype(BF16)
    grad_conv_ref[...] = (g * q_ref[...].astype(F32)).astype(BF16)


def grad_filters_body(grad_conv_ref, product_ref, halo_ref, out_ref, own_stack, halo_stack):
    row, lane = iotas(128, 128)
    flip = jnp.where(row + lane == 127, 1.0, 0.0).astype(BF16)
    own_part = row + lane <= 127
    group = lane // 16
    for tile in range(4):
        cols = slice(tile * 128, tile * 128 + 128)
        reverse = lax.dot_general(
            flip, grad_conv_ref[:, cols], NN, preferred_element_type=F32
        ).astype(BF16)
        own = product_ref[:, cols].astype(F32)
        halo = halo_ref[:, cols].astype(F32)
        for g in range(8):
            own_stack[g * 128 : g * 128 + 128, :] = jnp.where(group == g, own, 0.0).astype(BF16)
            halo_stack[g * 128 : g * 128 + 128, :] = jnp.where(group == g, halo, 0.0).astype(BF16)
        m_own = lax.dot_general(own_stack[...], reverse, NT, preferred_element_type=F32)
        m_halo = lax.dot_general(halo_stack[...], reverse, NT, preferred_element_type=F32)
        for g in range(8):
            rows = slice(g * 128, g * 128 + 128)
            m = jnp.where(own_part, m_own[rows], m_halo[rows])
            m = pltpu.roll(m, 0, axis=1, stride=1, stride_axis=0)
            out_ref[tile * 8 + g : tile * 8 + g + 1, :] = jnp.sum(m, axis=0, keepdims=True)


def grad_kv_body(rows_ref, grad_conv_ref, next_ref, k_ref, v_ref, grad_k_ref, grad_v_ref, stack, total):
    row, lane = iotas(128, 128)
    apply_filters(rows_ref, lane >= row, grad_conv_ref, next_ref, stack, total, False)
    grad_k_ref[...] = (total[...] * v_ref[...].astype(F32)).astype(BF16)
    grad_v_ref[...] = (total[...] * k_ref[...].astype(F32)).astype(BF16)


def shift_row(block, distance):
    n = YS * ZS
    return lax.ppermute(
        block, "row", [(i, i + distance) for i in range(n) if 0 <= i + distance < n]
    )


def shift_y(block, distance):
    route = [
        (y * ZS + z, (y + distance) % YS * ZS + z) for y in range(YS) for z in range(ZS)
    ]
    return lax.ppermute(block, "row", route)


def other_core(block):
    return lax.ppermute(block, "col", [(i, i ^ 1) for i in range(COLS)])


def exchange(blocks, axis, groups):
    return lax.all_to_all(blocks, axis, 0, 0, axis_index_groups=groups, tiled=True)


def swap_pieces(piece):
    route = []
    for y in range(YS):
        for z in range(ZS):
            for other in range(YS):
                for k in range(4):
                    route.append(((y * ZS + z) * COLS + 4 * other + k, (other * ZS + z) * COLS + 4 * y + k))
    return lax.ppermute(piece, ("row", "col"), route)


def local(q_proj, k_proj, v_proj, filters, w_out, cotangent):
    at = jnp.stack([lax.axis_index("row") // ZS, lax.axis_index("col") % 2]).astype(jnp.int32)
    tile = shaped((128, 512), BF16)
    w8 = lax.all_gather(w_out, "row", axis_index_groups=Z_GROUPS)
    product = (k_proj.astype(F32) * v_proj.astype(F32)).astype(BF16)
    halo = shift_row(product, 1)
    piece = swap_pieces(cotangent)
    taps = filters.T
    forward_rows = jnp.roll(jnp.flip(taps, 1), 1, axis=1)
    conv, mixed = call(
        conv_body,
        [shaped((128, 512), F32), tile],
        (forward_rows, product, halo, q_proj),
        [pltpu.VMEM((1024, 512), BF16)],
        flops=2 * 4096 * 512 * 128 * 4,
    )
    own8 = call(spread_body, shaped((8, 128, 256), BF16), (piece,), after=(mixed,))
    own8 = exchange(own8, "col", CHIP_GROUPS)
    pair8 = other_core(own8)
    mixed4 = [mixed] + [shift_y(mixed, d) for d in (1, 2, 3)]

    cot16, shares = call(
        grad_mixed_body,
        [shaped((COLS, 128, 256), BF16), shaped((YS, 128, 512), BF16)],
        (own8, pair8, w8),
        flops=2 * 512 * 512 * 1024,
        position=at,
    )
    sums = exchange(shares, "row", Y_GROUPS)
    gw8 = call(
        grad_w_body,
        shaped((ZS, 512, 128), BF16),
        (*mixed4, cot16),
        flops=2 * 512 * 512 * 1024,
        position=at,
        after=(shares,),
    )
    keep, give = call(
        projected_body,
        [shaped((8, 128, 256), F32), shaped((8, 128, 256), BF16)],
        (*mixed4, w8),
        [pltpu.VMEM((COLS, 128, 256), F32)],
        flops=2 * 512 * 512 * 1024,
        position=at,
        after=(gw8,),
    )
    pieces = call(pair_body, shaped((8, 128, 256), BF16), (keep, other_core(give)), after=(sums,))
    grad_q, grad_conv = call(grad_conv_body, [tile, tile], (sums, q_proj, conv), after=(give,))
    later = shift_row(grad_conv, -1)
    grad_taps = call(
        grad_filters_body,
        shaped((32, 128), F32),
        (grad_conv, product, halo),
        [pltpu.VMEM((1024, 128), BF16), pltpu.VMEM((1024, 128), BF16)],
        flops=2 * 1024 * 128 * 128 * 8,
    )
    grad_k, grad_v = call(
        grad_kv_body,
        [tile, tile],
        (taps, grad_conv, later, k_proj, v_proj),
        [pltpu.VMEM((1024, 256), BF16), pltpu.VMEM((128, 512), F32)],
        flops=2 * 4096 * 256 * 128 * 4,
    )

    got = exchange(pieces, "col", CHIP_GROUPS)
    grad_taps = call(taps_body, shaped((YS * ZS, 32, 128), BF16), (grad_taps,), after=(got, grad_k))
    grad_taps = jnp.sum(lax.all_to_all(grad_taps, "row", 0, 0, tiled=True).astype(F32), 0)
    grad_filters = jnp.flip(grad_taps, 1).T

    projected = swap_pieces(jnp.sum(got.astype(F32), 0).astype(BF16))
    grad_w = lax.psum_scatter(gw8, "row", axis_index_groups=Z_GROUPS).astype(F32)
    return (projected, grad_q, grad_k, grad_v, grad_filters, grad_w)


def solution(mesh):
    placed = (
        P("row", "col"),
        P("row", "col"),
        P("row", "col"),
        P(None, "col"),
        P("col", "row"),
        P("row", "col"),
    )
    return jax.shard_map(
        local,
        mesh=mesh,
        in_specs=placed,
        out_specs=(
            P("row", "col"),
            P("row", "col"),
            P("row", "col"),
            P("row", "col"),
            P(None, "col"),
            P("col", "row"),
        ),
        check_vma=False,
    )
```

time: 388 us -> 144 us (0.37)
  the two profiles are of different devices: /device:TPU:4 before, /device:TPU:22 now
where the time goes in v1:
time: 144 us; the launch traced here: 143 us
  starting transfers between devices  55.6 us (39%)
  waiting for transfers between devices  33.7 us (23%)
  blocking collectives  17.4 us (12%)
  between operations  14.4 us (10%)
  Pallas kernels  13.7 us (10%)
  local copies, waits for them, and re-layouts  5.24 us (4%)
  other arithmetic  2.84 us (2%)
    all_to_all x1, blocking collectives, exchange(): lax.all_to_all(blocks, axis, 0, 0, axis_index_groups=groups, tiled=True)  17.4 us
    all_to_all x2, starting transfers between devices, exchange(): lax.all_to_all(blocks, axis, 0, 0, axis_index_groups=groups, tiled=True)  15 us
    pallas_call x10, Pallas kernels, call(): pl.pallas_call(run, out_shape=out_shape, in_specs=specs, scratch_shapes=l...  13.7 us
    ppermute x3, starting transfers between devices, shift_y(): return lax.ppermute(block, 'row', route)  13.2 us
    all_to_all x1, starting transfers between devices, local(): lax.all_to_all(grad_taps, 'row', 0, 0, tiled=True).astype(F32)  12.6 us
    all_to_all x1, waiting for transfers between devices, local(): lax.all_to_all(grad_taps, 'row', 0, 0, tiled=True).astype(F32)  11.5 us
    ppermute x2, waiting for transfers between devices, shift_row(): lax.ppermute(block, 'row', [(i, i + distance) for i in range(n) if 0 <= i...  10.3 us
    ppermute x2, starting transfers between devices, shift_row(): lax.ppermute(block, 'row', [(i, i + distance) for i in range(n) if 0 <= i...  9.45 us
  transfers between devices with their start and end apart: 14, of which 6 were waited for; matrix products, arithmetic and copies ran while one was open for 2% of the time, Pallas kernels for 8%

profile of v1, /device:TPU:22, one launch (start us, length us, event | category | flops | bytes accessed | tf_op | source)
XLA Modules:
  0.0 142.8 jit_solution(13598757890498118098)
XLA Ops:
  9.0 4.3 %collective-permute-start = (bf16[128,512]{1,0:T(8,128)(2,1)S(1)}, bf16[128,512]{1,0:T(8,128)(2,1)S(1)}, u32[]{:S(2)}, u32[]{:S(2)}) collective-permute-start(bf16[128,512]{1,0:T(8,128)(2,1)S(1)} %multiply_convert_fusion.refs_1_), channel_id=1, source_target_pairs={{0,16},{16,32},{32,48},{48,64},{64,80},{80,96},{96,112},{112,128},... | collective-permute-start | bytes 393224 | tf_op jit(solution)/shard_map/ppermute | solution.py:182
  14.2 9.1 %collective-permute-done.refs_2_ = bf16[128,512]{1,0:T(8,128)(2,1)S(1)} collective-permute-done((bf16[128,512]{1,0:T(8,128)(2,1)S(1)}, bf16[128,512]{1,0:T(8,128)(2,1)S(1)}, u32[]{:S(2)}, u32[]{:S(2)}) %collective-permute-start) | collective-permute-done | bytes 131104 | tf_op jit(solution)/shard_map/ppermute | solution.py:182
  23.3 1.6 %shard_map.109 = (f32[128,512]{1,0:T(8,128)S(1)}, bf16[128,512]{1,0:T(8,128)(2,1)S(1)}) custom-call(f32[32,128]{1,0:T(8,128)S(1)} %pad_maximum_fusion.refs_0_, bf16[128,512]{1,0:T(8,128)(2,1)S(1)} %multiply_convert_fusion.refs_1_, bf16[128,512]{1,0:T(8,128)(2,1)S(1)} %collective-permute-done.refs_2_, bf16[128,512]{1,0:T(8,128)(2,1)S(1)} %copy-done.14), custom_call_target="tpu_custom_call" | custom-call | flops 2147483648 | bytes 802816 | tf_op jit(solution)/shard_map/pallas_call | solution.py:38
  25.7 17.4 %all_to_all.20.refs_1_ = bf16[8,128,256]{2,1,0:T(8,128)(2,1)S(1)} all-to-all(bf16[8,128,256]{2,1,0:T(8,128)(2,1)S(1)} %shard_map.110), channel_id=1, replica_groups={{0,2,4,6,8,10,12,14},{1,3,5,7,9,11,13,15},{16,18,20,22,24,26,28,30},{17..., dimensions={0} | all-to-all | bytes 1048576 | tf_op jit(solution)/shard_map/all_to_all | solution.py:199
  43.2 1.9 %collective-permute-start.5 = (bf16[8,128,256]{2,1,0:T(8,128)(2,1)S(1)}, bf16[8,128,256]{2,1,0:T(8,128)(2,1)S(1)}, u32[]{:S(2)}, u32[]{:S(2)}) collective-permute-start(bf16[8,128,256]{2,1,0:T(8,128)(2,1)S(1)} %all_to_all.20.refs_1_), channel_id=1, source_target_pairs={{0,1},{1,0},{2,3},{3,2},{4,5},{5,4},{6,7},{7,6},{8,9},{9,8},{10,11... | collective-permute-start | bytes 1572872 | tf_op jit(solution)/shard_map/ppermute | solution.py:195
  45.1 1.9 %collective-permute-start.3 = (bf16[128,512]{1,0:T(8,128)(2,1)S(1)}, bf16[128,512]{1,0:T(8,128)(2,1)S(1)}, u32[]{:S(2)}, u32[]{:S(2)}) collective-permute-start(bf16[128,512]{1,0:T(8,128)(2,1)S(1)} %get-tuple-element.16.refs_1_), channel_id=1, source_target_pairs={{0,384},{16,400},{32,416},{48,432},{64,448},{80,464},{96,480},{112... | collective-permute-start | bytes 393224 | tf_op jit(solution)/shard_map/ppermute | solution.py:191
  47.0 6.7 %collective-permute-start.2 = (bf16[128,512]{1,0:T(8,128)(2,1)S(1)}, bf16[128,512]{1,0:T(8,128)(2,1)S(1)}, u32[]{:S(2)}, u32[]{:S(2)}) collective-permute-start(bf16[128,512]{1,0:T(8,128)(2,1)S(1)} %get-tuple-element.16.refs_1_), channel_id=1, source_target_pairs={{0,256},{16,272},{32,288},{48,304},{64,320},{80,336},{96,352},{112... | collective-permute-start | bytes 393224 | tf_op jit(solution)/shard_map/ppermute | solution.py:191
  53.7 4.7 %collective-permute-start.1 = (bf16[128,512]{1,0:T(8,128)(2,1)S(1)}, bf16[128,512]{1,0:T(8,128)(2,1)S(1)}, u32[]{:S(2)}, u32[]{:S(2)}) collective-permute-start(bf16[128,512]{1,0:T(8,128)(2,1)S(1)} %get-tuple-element.16.refs_1_), channel_id=1, source_target_pairs={{0,128},{16,144},{32,160},{48,176},{64,192},{80,208},{96,224},{112... | collective-permute-start | bytes 393224 | tf_op jit(solution)/shard_map/ppermute | solution.py:191
  58.5 1.2 copy-done
  59.7 2.8 %shard_map.111 = (bf16[16,128,256]{2,1,0:T(8,128)(2,1)S(1)}, bf16[4,128,512]{2,1,0:T(8,128)(2,1)}) custom-call(s32[2]{0:T(128)S(1)} %pad_add_fusion.refs_0_, bf16[8,128,256]{2,1,0:T(8,128)(2,1)S(1)} %all_to_all.20.refs_1_, bf16[8,128,256]{2,1,0:T(8,128)(2,1)S(1)} %collective-permute-done.5.refs_2_, bf16[8,512,128]{2,1,0:T(8,128)(2,1)S(1)} %bitcast.9), custom_call_target="tpu_custom_call" | custom-call | flops 536870912 | bytes 3670016 | tf_op jit(solution)/shard_map/pallas_call | solution.py:38
  62.5 2.2 %collective-permute-done.1.refs_2_ = bf16[128,512]{1,0:T(8,128)(2,1)S(1)} collective-permute-done((bf16[128,512]{1,0:T(8,128)(2,1)S(1)}, bf16[128,512]{1,0:T(8,128)(2,1)S(1)}, u32[]{:S(2)}, u32[]{:S(2)}) %collective-permute-start.1) | collective-permute-done | bytes 131104 | tf_op jit(solution)/shard_map/ppermute | solution.py:191
  64.7 2.3 %shard_map.112.refs_6_ = bf16[8,512,128]{2,1,0:T(8,128)(2,1)} custom-call(s32[2]{0:T(128)S(1)} %pad_add_fusion.refs_0_, bf16[128,512]{1,0:T(8,128)(2,1)S(1)} %get-tuple-element.16.refs_1_, bf16[128,512]{1,0:T(8,128)(2,1)S(1)} %collective-permute-done.1.refs_2_, bf16[128,512]{1,0:T(8,128)(2,1)S(1)} %collective-permute-done.2.refs_3_, ...), custom_call_target="tpu_custom_call" | custom-call | flops 536870912 | bytes 2621440 | tf_op jit(solution)/shard_map/pallas_call | solution.py:38
  67.0 7.3 %all-to-all-start.1 = ((bf16[4,128,512]{2,1,0:T(8,128)(2,1)}), bf16[4,128,512]{2,1,0:T(8,128)(2,1)S(1)}, u32[]{:S(2)}, u32[]{:S(2)}) async-start(bf16[4,128,512]{2,1,0:T(8,128)(2,1)} %get-tuple-element.18.refs_6_), calls=%async_computation.1 | async-start | bytes 1048576 | tf_op jit(solution)/shard_map/all_to_all | solution.py:199
  74.3 1.4 shard_map.113
  75.7 1.9 %collective-permute-start.6 = (bf16[8,128,256]{2,1,0:T(8,128)(2,1)S(1)}, bf16[8,128,256]{2,1,0:T(8,128)(2,1)S(1)}, u32[]{:S(2)}, u32[]{:S(2)}) collective-permute-start(bf16[8,128,256]{2,1,0:T(8,128)(2,1)S(1)} %get-tuple-element.20.refs_3_), channel_id=1, source_target_pairs={{0,1},{1,0},{2,3},{3,2},{4,5},{5,4},{6,7},{7,6},{8,9},{9,8},{10,11... | collective-permute-start | bytes 1572872 | tf_op jit(solution)/shard_map/ppermute | solution.py:195
  79.5 7.8 %all-to-all-done.1.refs_2_.refs_0_ = bf16[4,128,512]{2,1,0:T(8,128)(2,1)S(1)} async-done(((bf16[4,128,512]{2,1,0:T(8,128)(2,1)}), bf16[4,128,512]{2,1,0:T(8,128)(2,1)S(1)}, u32[]{:S(2)}, u32[]{:S(2)}) %all-to-all-start.1) | async-done | bytes 524320 | tf_op jit(solution)/shard_map/all_to_all | solution.py:199
  88.2 7.7 %all-to-all-start.2 = ((bf16[8,128,256]{2,1,0:T(8,128)(2,1)}), bf16[8,128,256]{2,1,0:T(8,128)(2,1)S(1)}, u32[]{:S(2)}, u32[]{:S(2)}) async-start(bf16[8,128,256]{2,1,0:T(8,128)(2,1)} %shard_map.114), calls=%async_computation.2 | async-start | bytes 1048576 | tf_op jit(solution)/shard_map/all_to_all | solution.py:199
  96.8 5.2 %collective-permute-start.8 = (bf16[128,512]{1,0:T(8,128)(2,1)S(1)}, bf16[128,512]{1,0:T(8,128)(2,1)S(1)}, u32[]{:S(2)}, u32[]{:S(2)}) collective-permute-start(bf16[128,512]{1,0:T(8,128)(2,1)S(1)} %get-tuple-element.23.refs_1_.refs_0_), channel_id=1, source_target_pairs={{16,0},{32,16},{48,32},{64,48},{80,64},{96,80},{112,96},{128,112},... | collective-permute-start | bytes 393224 | tf_op jit(solution)/shard_map/ppermute | solution.py:182
  102.0 1.6 %shard_map.117.refs_0_ = f32[32,128]{1,0:T(8,128)S(1)} custom-call(bf16[128,512]{1,0:T(8,128)(2,1)S(1)} %get-tuple-element.23.refs_1_.refs_0_, bf16[128,512]{1,0:T(8,128)(2,1)S(1)} %copy-done.12, bf16[128,512]{1,0:T(8,128)(2,1)S(1)} %copy-done.20), custom_call_target="tpu_custom_call" | custom-call | flops 268435456 | bytes 409600 | tf_op jit(solution)/shard_map/pallas_call | solution.py:38
  103.6 1.2 collective-permute-done.8.refs_2_
  104.8 1.7 %shard_map.116 = (bf16[128,512]{1,0:T(8,128)(2,1)}, bf16[128,512]{1,0:T(8,128)(2,1)}) custom-call(f32[32,128]{1,0:T(8,128)S(1)} %bitcast.13, bf16[128,512]{1,0:T(8,128)(2,1)S(1)} %get-tuple-element.23.refs_1_.refs_0_, bf16[128,512]{1,0:T(8,128)(2,1)S(1)} %collective-permute-done.8.refs_2_, bf16[128,512]{1,0:T(8,128)(2,1)S(1)} %copy-done.10, ...), custom_call_target="tpu_custom_call" | custom-call | flops 1073741824 | bytes 802816 | tf_op jit(solution)/shard_map/pallas_call | solution.py:38
  108.1 12.6 %all-to-all-start.3 = ((bf16[32,32,128]{2,1,0:T(8,128)(2,1)}), bf16[32,32,128]{2,1,0:T(8,128)(2,1)S(1)}, u32[]{:S(2)}, u32[]{:S(2)}) async-start(bf16[32,32,128]{2,1,0:T(8,128)(2,1)} %shard_map.118), calls=%async_computation.3 | async-start | bytes 524288 | tf_op jit(solution)/shard_map/all_to_all | solution.py:278
  121.5 1.6 %bitcast_convert_fusion = f32[512,128]{1,0:T(8,128)} fusion(bf16[1,512,128]{2,1,0:T(8,128)(2,1)} %reduce-scatter.2.cloned.1.call-done), kind=kLoop, calls=%fused_computation.2 | loop fusion | flops 65536 | bytes 393216 | tf_op jit(solution)/shard_map/convert_element_type | solution.py:282
  123.1 11.5 %all-to-all-done.3 = bf16[32,32,128]{2,1,0:T(8,128)(2,1)S(1)} async-done(((bf16[32,32,128]{2,1,0:T(8,128)(2,1)}), bf16[32,32,128]{2,1,0:T(8,128)(2,1)S(1)}, u32[]{:S(2)}, u32[]{:S(2)}) %all-to-all-start.3) | async-done | bytes 262176 | tf_op jit(solution)/shard_map/all_to_all | solution.py:278
  (71 shorter events, 10.8 us)
Async XLA Ops:
  7.2 51.3 %all-gather.3.cloned.1.call-start = ((), (), s32[]{:S(2)}) async-start(), calls=%async_computation.6 | async-start | bytes 1179648 | tf_op jit(solution)/shard_map/all_gather | solution.py:215
  7.9 15.4 %copy-start.14 = (bf16[128,512]{1,0:T(8,128)(2,1)S(1)}, bf16[128,512]{1,0:T(8,128)(2,1)}, u32[]{:S(2)}) copy-start(bf16[128,512]{1,0:T(8,128)(2,1)} %refs_1_.1) | copy-start | bytes 393220
  7.9 113.6 %reduce-scatter.2.cloned.1.call-start = ((), (), s32[]{:S(2)}) async-start(), calls=%async_computation.5 | async-start | bytes 1179648 | tf_op jit(solution)/shard_map/reduce_scatter | solution.py:282
  9.0 16.0 %copy-start.11 = (bf16[128,512]{1,0:T(8,128)(2,1)}, bf16[128,512]{1,0:T(8,128)(2,1)S(1)}, u32[]{:S(2)}) copy-start(bf16[128,512]{1,0:T(8,128)(2,1)S(1)} %multiply_convert_fusion.refs_1_) | copy-start | bytes 393220
  9.0 14.3 %collective-permute-start = (bf16[128,512]{1,0:T(8,128)(2,1)S(1)}, bf16[128,512]{1,0:T(8,128)(2,1)S(1)}, u32[]{:S(2)}, u32[]{:S(2)}) collective-permute-start(bf16[128,512]{1,0:T(8,128)(2,1)S(1)} %multiply_convert_fusion.refs_1_), channel_id=1, source_target_pairs={{0,16},{16,32},{32,48},{48,64},{64,80},{80,96},{96,112},{112,128},... | collective-permute-start | bytes 393224 | tf_op jit(solution)/shard_map/ppermute | solution.py:182
  13.3 12.4 %collective-permute-start.4 = (bf16[128,256]{1,0:T(8,128)(2,1)S(1)}, bf16[128,256]{1,0:T(8,128)(2,1)S(1)}, u32[]{:S(2)}, u32[]{:S(2)}) collective-permute-start(bf16[128,256]{1,0:T(8,128)(2,1)S(1)} %copy-done.21), channel_id=1, source_target_pairs={{0,0},{1,1},{2,2},{3,3},{4,128},{5,129},{6,130},{7,131},{8,256},{9... | collective-permute-start | bytes 196616 | tf_op jit(solution)/shard_map/ppermute | solution.py:209
  43.2 15.3 %collective-permute-start.5 = (bf16[8,128,256]{2,1,0:T(8,128)(2,1)S(1)}, bf16[8,128,256]{2,1,0:T(8,128)(2,1)S(1)}, u32[]{:S(2)}, u32[]{:S(2)}) collective-permute-start(bf16[8,128,256]{2,1,0:T(8,128)(2,1)S(1)} %all_to_all.20.refs_1_), channel_id=1, source_target_pairs={{0,1},{1,0},{2,3},{3,2},{4,5},{5,4},{6,7},{7,6},{8,9},{9,8},{10,11... | collective-permute-start | bytes 1572872 | tf_op jit(solution)/shard_map/ppermute | solution.py:195
  45.1 17.4 %collective-permute-start.3 = (bf16[128,512]{1,0:T(8,128)(2,1)S(1)}, bf16[128,512]{1,0:T(8,128)(2,1)S(1)}, u32[]{:S(2)}, u32[]{:S(2)}) collective-permute-start(bf16[128,512]{1,0:T(8,128)(2,1)S(1)} %get-tuple-element.16.refs_1_), channel_id=1, source_target_pairs={{0,384},{16,400},{32,416},{48,432},{64,448},{80,464},{96,480},{112... | collective-permute-start | bytes 393224 | tf_op jit(solution)/shard_map/ppermute | solution.py:191
  47.0 15.5 %collective-permute-start.2 = (bf16[128,512]{1,0:T(8,128)(2,1)S(1)}, bf16[128,512]{1,0:T(8,128)(2,1)S(1)}, u32[]{:S(2)}, u32[]{:S(2)}) collective-permute-start(bf16[128,512]{1,0:T(8,128)(2,1)S(1)} %get-tuple-element.16.refs_1_), channel_id=1, source_target_pairs={{0,256},{16,272},{32,288},{48,304},{64,320},{80,336},{96,352},{112... | collective-permute-start | bytes 393224 | tf_op jit(solution)/shard_map/ppermute | solution.py:191
  53.7 11.0 %collective-permute-start.1 = (bf16[128,512]{1,0:T(8,128)(2,1)S(1)}, bf16[128,512]{1,0:T(8,128)(2,1)S(1)}, u32[]{:S(2)}, u32[]{:S(2)}) collective-permute-start(bf16[128,512]{1,0:T(8,128)(2,1)S(1)} %get-tuple-element.16.refs_1_), channel_id=1, source_target_pairs={{0,128},{16,144},{32,160},{48,176},{64,192},{80,208},{96,224},{112... | collective-permute-start | bytes 393224 | tf_op jit(solution)/shard_map/ppermute | solution.py:191
  67.0 7.3 %copy-start.1 = (bf16[4096,128]{1,0:T(8,128)(2,1)S(1)}, bf16[4096,128]{1,0:T(8,128)(2,1)}, u32[]{:S(2)}) copy-start(bf16[4096,128]{1,0:T(8,128)(2,1)} %all-gather.3.cloned.1.call-done) | copy-start | bytes 3145732
  67.0 7.3 %copy-start.5 = (bf16[128,512]{1,0:T(8,128)(2,1)S(1)}, bf16[128,512]{1,0:T(8,128)(2,1)}, u32[]{:S(2)}) copy-start(bf16[128,512]{1,0:T(8,128)(2,1)} %copy-done.4) | copy-start | bytes 393220
  67.0 7.3 %copy-start.18 = (s32[2]{0:T(128)S(1)}, s32[2]{0:T(128)}, u32[]{:S(2)}) copy-start(s32[2]{0:T(128)} %copy-done.17) | copy-start | bytes 28
  67.0 20.3 %all-to-all-start.1 = ((bf16[4,128,512]{2,1,0:T(8,128)(2,1)}), bf16[4,128,512]{2,1,0:T(8,128)(2,1)S(1)}, u32[]{:S(2)}, u32[]{:S(2)}) async-start(bf16[4,128,512]{2,1,0:T(8,128)(2,1)} %get-tuple-element.18.refs_6_), calls=%async_computation.1 | async-start | bytes 1048576 | tf_op jit(solution)/shard_map/all_to_all | solution.py:199
  75.7 3.8 %collective-permute-start.6 = (bf16[8,128,256]{2,1,0:T(8,128)(2,1)S(1)}, bf16[8,128,256]{2,1,0:T(8,128)(2,1)S(1)}, u32[]{:S(2)}, u32[]{:S(2)}) collective-permute-start(bf16[8,128,256]{2,1,0:T(8,128)(2,1)S(1)} %get-tuple-element.20.refs_3_), channel_id=1, source_target_pairs={{0,1},{1,0},{2,3},{3,2},{4,5},{5,4},{6,7},{7,6},{8,9},{9,8},{10,11... | collective-permute-start | bytes 1572872 | tf_op jit(solution)/shard_map/ppermute | solution.py:195
  88.2 7.8 %copy-start.3 = (bf16[8,128,256]{2,1,0:T(8,128)(2,1)S(1)}, bf16[8,128,256]{2,1,0:T(8,128)(2,1)}, u32[]{:S(2)}) copy-start(bf16[8,128,256]{2,1,0:T(8,128)(2,1)} %copy-done.2) | copy-start | bytes 1572868
  88.2 7.8 %copy-start.7 = (f32[128,512]{1,0:T(8,128)S(1)}, f32[128,512]{1,0:T(8,128)}, u32[]{:S(2)}) copy-start(f32[128,512]{1,0:T(8,128)} %copy-done.6) | copy-start | bytes 786436
  88.2 7.8 %copy-start.15 = (bf16[128,512]{1,0:T(8,128)(2,1)S(1)}, bf16[128,512]{1,0:T(8,128)(2,1)}, u32[]{:S(2)}) copy-start(bf16[128,512]{1,0:T(8,128)(2,1)} %refs_1_.1) | copy-start | bytes 393220
  88.2 18.2 %all-to-all-start.2 = ((bf16[8,128,256]{2,1,0:T(8,128)(2,1)}), bf16[8,128,256]{2,1,0:T(8,128)(2,1)S(1)}, u32[]{:S(2)}, u32[]{:S(2)}) async-start(bf16[8,128,256]{2,1,0:T(8,128)(2,1)} %shard_map.114), calls=%async_computation.2 | async-start | bytes 1048576 | tf_op jit(solution)/shard_map/all_to_all | solution.py:199
  96.8 8.1 %copy-start.9 = (bf16[128,512]{1,0:T(8,128)(2,1)S(1)}, bf16[128,512]{1,0:T(8,128)(2,1)}, u32[]{:S(2)}) copy-start(bf16[128,512]{1,0:T(8,128)(2,1)} %refs_4_.1) | copy-start | bytes 393220
  96.8 8.1 %copy-start.10 = (bf16[128,512]{1,0:T(8,128)(2,1)S(1)}, bf16[128,512]{1,0:T(8,128)(2,1)}, u32[]{:S(2)}) copy-start(bf16[128,512]{1,0:T(8,128)(2,1)} %refs_3_.3) | copy-start | bytes 393220
  96.8 8.0 %collective-permute-start.8 = (bf16[128,512]{1,0:T(8,128)(2,1)S(1)}, bf16[128,512]{1,0:T(8,128)(2,1)S(1)}, u32[]{:S(2)}, u32[]{:S(2)}) collective-permute-start(bf16[128,512]{1,0:T(8,128)(2,1)S(1)} %get-tuple-element.23.refs_1_.refs_0_), channel_id=1, source_target_pairs={{16,0},{32,16},{48,32},{64,48},{80,64},{96,80},{112,96},{128,112},... | collective-permute-start | bytes 393224 | tf_op jit(solution)/shard_map/ppermute | solution.py:182
  108.1 26.5 %all-to-all-start.3 = ((bf16[32,32,128]{2,1,0:T(8,128)(2,1)}), bf16[32,32,128]{2,1,0:T(8,128)(2,1)S(1)}, u32[]{:S(2)}, u32[]{:S(2)}) async-start(bf16[32,32,128]{2,1,0:T(8,128)(2,1)} %shard_map.118), calls=%async_computation.3 | async-start | bytes 524288 | tf_op jit(solution)/shard_map/all_to_all | solution.py:278
  120.8 0.7 collective-permute-start.7
  (12 other events, 38.1 us)
Sparse Core Ops, SparseCore 0:
  10.1 46.7 all-gather.2
  67.1 40.0 reduce-scatter.1

commit v2 on v1

--- a/solution.py
+++ b/solution.py
@@ -13,7 +13,6 @@
 TN = (((0,), (0,)), ((), ()))
 NN = (((1,), (0,)), ((), ()))
 Z_GROUPS = [[y * ZS + z for z in range(ZS)] for y in range(YS)]
-Y_GROUPS = [[y * ZS + z for y in range(YS)] for z in range(ZS)]
 CHIP_GROUPS = [[2 * i + core for i in range(8)] for core in range(2)]
 
 
@@ -94,15 +93,16 @@
         out_ref[i] = piece_ref[...]
 
 
-def grad_mixed_body(at_ref, own_ref, pair_ref, w_ref, cot_ref, out_ref):
-    core = at_ref[1]
+def grad_mixed_body(at_ref, own_ref, pair_ref, w_ref, cot_ref, *out_refs):
+    y, core = at_ref[0], at_ref[1]
     for i in range(8):
         cot_ref[2 * i + core] = own_ref[i]
         cot_ref[2 * i + 1 - core] = pair_ref[i]
     w = jnp.concatenate([w_ref[z] for z in range(ZS)], 1)
-    for y in range(YS):
-        lhs = jnp.concatenate([cot_ref[4 * y + k] for k in range(4)], 1)
-        out_ref[y] = lax.dot_general(lhs, w, NT, preferred_element_type=F32).astype(BF16)
+    for d in range(YS):
+        at = lax.rem(y + d, YS) * 4
+        lhs = jnp.concatenate([cot_ref[at + k] for k in range(4)], 1)
+        out_refs[d][...] = lax.dot_general(lhs, w, NT, preferred_element_type=F32).astype(BF16)
 
 
 def projected_body(at_ref, m0_ref, m1_ref, m2_ref, m3_ref, w_ref, keep_ref, give_ref, total):
@@ -138,10 +138,8 @@
         out_ref[2 * k + 1] = r[:, 128:]
 
 
-def grad_conv_body(shares_ref, q_ref, conv_ref, grad_q_ref, grad_conv_ref):
-    g = shares_ref[0].astype(F32)
-    for y in range(1, YS):
-        g = g + shares_ref[y].astype(F32)
+def grad_conv_body(a_ref, b_ref, c_ref, d_ref, q_ref, conv_ref, grad_q_ref, grad_conv_ref):
+    g = a_ref[...].astype(F32) + b_ref[...].astype(F32) + c_ref[...].astype(F32) + d_ref[...].astype(F32)
     grad_q_ref[...] = (g * conv_ref[...]).astype(BF16)
     grad_conv_ref[...] = (g * q_ref[...].astype(F32)).astype(BF16)
 
@@ -225,26 +223,26 @@
         [pltpu.VMEM((1024, 512), BF16)],
         flops=2 * 4096 * 512 * 128 * 4,
     )
-    own8 = call(spread_body, shaped((8, 128, 256), BF16), (piece,), after=(mixed,))
+    mixed4 = [mixed] + [shift_y(mixed, d) for d in (1, 2, 3)]
+    own8 = call(spread_body, shaped((8, 128, 256), BF16), (piece,), after=mixed4[1:2])
     own8 = exchange(own8, "col", CHIP_GROUPS)
     pair8 = other_core(own8)
-    mixed4 = [mixed] + [shift_y(mixed, d) for d in (1, 2, 3)]
-
-    cot16, shares = call(
+
+    cot16, *shares = call(
         grad_mixed_body,
-        [shaped((COLS, 128, 256), BF16), shaped((YS, 128, 512), BF16)],
+        [shaped((COLS, 128, 256), BF16)] + [tile] * YS,
         (own8, pair8, w8),
         flops=2 * 512 * 512 * 1024,
         position=at,
     )
-    sums = exchange(shares, "row", Y_GROUPS)
+    sums = [shares[0]] + [shift_y(shares[d], d) for d in (1, 2, 3)]
     gw8 = call(
         grad_w_body,
         shaped((ZS, 512, 128), BF16),
         (*mixed4, cot16),
         flops=2 * 512 * 512 * 1024,
         position=at,
-        after=(shares,),
+        after=(shares[1],),
     )
     keep, give = call(
         projected_body,
@@ -253,10 +251,10 @@
         [pltpu.VMEM((COLS, 128, 256), F32)],
         flops=2 * 512 * 512 * 1024,
         position=at,
-        after=(gw8,),
-    )
-    pieces = call(pair_body, shaped((8, 128, 256), BF16), (keep, other_core(give)), after=(sums,))
-    grad_q, grad_conv = call(grad_conv_body, [tile, tile], (sums, q_proj, conv), after=(give,))
+        after=[gw8] + sums[1:],
+    )
+    pieces = call(pair_body, shaped((8, 128, 256), BF16), (keep, other_core(give)))
+    grad_q, grad_conv = call(grad_conv_body, [tile, tile], (*sums, q_proj, conv), after=(give,))
     later = shift_row(grad_conv, -1)
     grad_taps = call(
         grad_filters_body,

time: 144 us -> 149 us (1.035)
  the two profiles are of different devices: /device:TPU:22 before, /device:TPU:8 now
where the time goes in v2:
time: 149 us; the launch traced here: 148 us
  starting transfers between devices  71 us (48%)
  waiting for transfers between devices  27.9 us (19%)
  blocking collectives  15.3 us (10%)
  between operations  14.3 us (10%)
  Pallas kernels  13 us (9%)
  local copies, waits for them, and re-layouts  3.6 us (2%)
  other arithmetic  2.91 us (2%)
    ppermute x6, starting transfers between devices, shift_y(): return lax.ppermute(block, 'row', route)  35.3 us
    all_to_all x1, blocking collectives, exchange(): lax.all_to_all(blocks, axis, 0, 0, axis_index_groups=groups, tiled=True)  15.3 us
    pallas_call x10, Pallas kernels, call(): pl.pallas_call(run, out_shape=out_shape, in_specs=specs, scratch_shapes=l...  13 us
    ppermute x2, waiting for transfers between devices, swap_pieces(): return lax.ppermute(piece, ('row', 'col'), route)  10.7 us
    ppermute x2, starting transfers between devices, swap_pieces(): return lax.ppermute(piece, ('row', 'col'), route)  9.26 us
    all_to_all x1, starting transfers between devices, local(): lax.all_to_all(grad_taps, 'row', 0, 0, tiled=True).astype(F32)  9.11 us
    ppermute x2, waiting for transfers between devices, shift_row(): lax.ppermute(block, 'row', [(i, i + distance) for i in range(n) if 0 <= i...  8.42 us
    all_to_all x1, starting transfers between devices, exchange(): lax.all_to_all(blocks, axis, 0, 0, axis_index_groups=groups, tiled=True)  7.58 us
  transfers between devices with their start and end apart: 16, of which 8 were waited for; matrix products, arithmetic and copies ran while one was open for 1% of the time, Pallas kernels for 9%

profile of v2, /device:TPU:8, one launch (start us, length us, event | category | flops | bytes accessed | tf_op | source)
XLA Modules:
  0.0 148.0 jit_solution(9659505518011490814)
XLA Ops:
  8.2 4.4 %collective-permute-start = (bf16[128,512]{1,0:T(8,128)(2,1)S(1)}, bf16[128,512]{1,0:T(8,128)(2,1)S(1)}, u32[]{:S(2)}, u32[]{:S(2)}) collective-permute-start(bf16[128,512]{1,0:T(8,128)(2,1)S(1)} %multiply_convert_fusion.refs_1_), channel_id=1, source_target_pairs={{0,16},{16,32},{32,48},{48,64},{64,80},{80,96},{96,112},{112,128},... | collective-permute-start | bytes 393224 | tf_op jit(solution)/shard_map/ppermute | solution.py:180
  13.0 2.4 %collective-permute-done.refs_2_ = bf16[128,512]{1,0:T(8,128)(2,1)S(1)} collective-permute-done((bf16[128,512]{1,0:T(8,128)(2,1)S(1)}, bf16[128,512]{1,0:T(8,128)(2,1)S(1)}, u32[]{:S(2)}, u32[]{:S(2)}) %collective-permute-start) | collective-permute-done | bytes 131104 | tf_op jit(solution)/shard_map/ppermute | solution.py:180
  17.0 14.5 %collective-permute-start.1 = (bf16[128,512]{1,0:T(8,128)(2,1)S(1)}, bf16[128,512]{1,0:T(8,128)(2,1)S(1)}, u32[]{:S(2)}, u32[]{:S(2)}) collective-permute-start(bf16[128,512]{1,0:T(8,128)(2,1)S(1)} %get-tuple-element.19.refs_1_), channel_id=1, source_target_pairs={{0,128},{16,144},{32,160},{48,176},{64,192},{80,208},{96,224},{112... | collective-permute-start | bytes 393224 | tf_op jit(solution)/shard_map/ppermute | solution.py:189
  31.5 6.7 %collective-permute-start.4 = (bf16[128,256]{1,0:T(8,128)(2,1)S(1)}, bf16[128,256]{1,0:T(8,128)(2,1)S(1)}, u32[]{:S(2)}, u32[]{:S(2)}) collective-permute-start(bf16[128,256]{1,0:T(8,128)(2,1)S(1)} %copy-done.7), channel_id=1, source_target_pairs={{0,0},{1,1},{2,2},{3,3},{4,128},{5,129},{6,130},{7,131},{8,256},{9... | collective-permute-start | bytes 196616 | tf_op jit(solution)/shard_map/ppermute | solution.py:207
  38.3 2.4 %collective-permute-done.4.refs_0_ = bf16[128,256]{1,0:T(8,128)(2,1)S(1)} collective-permute-done((bf16[128,256]{1,0:T(8,128)(2,1)S(1)}, bf16[128,256]{1,0:T(8,128)(2,1)S(1)}, u32[]{:S(2)}, u32[]{:S(2)}) %collective-permute-start.4) | collective-permute-done | bytes 65568 | tf_op jit(solution)/shard_map/ppermute | solution.py:207
  40.7 15.3 %all_to_all.15.refs_1_ = bf16[8,128,256]{2,1,0:T(8,128)(2,1)S(1)} all-to-all(bf16[8,128,256]{2,1,0:T(8,128)(2,1)S(1)} %shard_map.110), channel_id=1, replica_groups={{0,2,4,6,8,10,12,14},{1,3,5,7,9,11,13,15},{16,18,20,22,24,26,28,30},{17..., dimensions={0} | all-to-all | bytes 1048576 | tf_op jit(solution)/shard_map/all_to_all | solution.py:197
  56.0 1.9 %collective-permute-start.5 = (bf16[8,128,256]{2,1,0:T(8,128)(2,1)S(1)}, bf16[8,128,256]{2,1,0:T(8,128)(2,1)S(1)}, u32[]{:S(2)}, u32[]{:S(2)}) collective-permute-start(bf16[8,128,256]{2,1,0:T(8,128)(2,1)S(1)} %all_to_all.15.refs_1_), channel_id=1, source_target_pairs={{0,1},{1,0},{2,3},{3,2},{4,5},{5,4},{6,7},{7,6},{8,9},{9,8},{10,11... | collective-permute-start | bytes 1572872 | tf_op jit(solution)/shard_map/ppermute | solution.py:193
  58.1 5.2 %collective-permute-start.2 = (bf16[128,512]{1,0:T(8,128)(2,1)S(1)}, bf16[128,512]{1,0:T(8,128)(2,1)S(1)}, u32[]{:S(2)}, u32[]{:S(2)}) collective-permute-start(bf16[128,512]{1,0:T(8,128)(2,1)S(1)} %get-tuple-element.19.refs_1_), channel_id=1, source_target_pairs={{0,256},{16,272},{32,288},{48,304},{64,320},{80,336},{96,352},{112... | collective-permute-start | bytes 393224 | tf_op jit(solution)/shard_map/ppermute | solution.py:189
  63.3 3.5 %collective-permute-start.3 = (bf16[128,512]{1,0:T(8,128)(2,1)S(1)}, bf16[128,512]{1,0:T(8,128)(2,1)S(1)}, u32[]{:S(2)}, u32[]{:S(2)}) collective-permute-start(bf16[128,512]{1,0:T(8,128)(2,1)S(1)} %get-tuple-element.19.refs_1_), channel_id=1, source_target_pairs={{0,384},{16,400},{32,416},{48,432},{64,448},{80,464},{96,480},{112... | collective-permute-start | bytes 393224 | tf_op jit(solution)/shard_map/ppermute | solution.py:189
  68.1 2.0 %shard_map.111 = (bf16[16,128,256]{2,1,0:T(8,128)(2,1)S(1)}, bf16[128,512]{1,0:T(8,128)(2,1)S(1)}, bf16[128,512]{1,0:T(8,128)(2,1)S(1)}, bf16[128,512]{1,0:T(8,128)(2,1)S(1)}, bf16[128,512]{1,0:T(8,128)(2,1)S(1)}) custom-call(s32[2]{0:T(128)S(1)} %pad_add_fusion.refs_0_, bf16[8,128,256]{2,1,0:T(8,128)(2,1)S(1)} %all_to_all.15.refs_1_, ...), custom_call_target="tpu_custom_call" | custom-call | flops 536870912 | bytes 3670016 | tf_op jit(solution)/shard_map/pallas_call | solution.py:37
  70.1 3.2 %collective-permute-start.6 = (bf16[128,512]{1,0:T(8,128)(2,1)S(1)}, bf16[128,512]{1,0:T(8,128)(2,1)S(1)}, u32[]{:S(2)}, u32[]{:S(2)}) collective-permute-start(bf16[128,512]{1,0:T(8,128)(2,1)S(1)} %get-tuple-element.21.refs_6_), channel_id=1, source_target_pairs={{0,128},{16,144},{32,160},{48,176},{64,192},{80,208},{96,224},{112... | collective-permute-start | bytes 393224 | tf_op jit(solution)/shard_map/ppermute | solution.py:189
  73.3 4.5 %collective-permute-start.7 = (bf16[128,512]{1,0:T(8,128)(2,1)S(1)}, bf16[128,512]{1,0:T(8,128)(2,1)S(1)}, u32[]{:S(2)}, u32[]{:S(2)}) collective-permute-start(bf16[128,512]{1,0:T(8,128)(2,1)S(1)} %get-tuple-element.22), channel_id=1, source_target_pairs={{0,256},{16,272},{32,288},{48,304},{64,320},{80,336},{96,352},{112... | collective-permute-start | bytes 393224 | tf_op jit(solution)/shard_map/ppermute | solution.py:189
  77.8 4.4 %collective-permute-start.8 = (bf16[128,512]{1,0:T(8,128)(2,1)S(1)}, bf16[128,512]{1,0:T(8,128)(2,1)S(1)}, u32[]{:S(2)}, u32[]{:S(2)}) collective-permute-start(bf16[128,512]{1,0:T(8,128)(2,1)S(1)} %get-tuple-element.23), channel_id=1, source_target_pairs={{0,384},{16,400},{32,416},{48,432},{64,448},{80,464},{96,480},{112... | collective-permute-start | bytes 393224 | tf_op jit(solution)/shard_map/ppermute | solution.py:189
  82.3 2.3 %shard_map.112.refs_6_ = bf16[8,512,128]{2,1,0:T(8,128)(2,1)} custom-call(s32[2]{0:T(128)S(1)} %pad_add_fusion.refs_0_, bf16[128,512]{1,0:T(8,128)(2,1)S(1)} %get-tuple-element.19.refs_1_, bf16[128,512]{1,0:T(8,128)(2,1)S(1)} %collective-permute-done.1.refs_1_.refs_2_, bf16[128,512]{1,0:T(8,128)(2,1)S(1)} %collective-permute-done.2.refs_3_, ...), custom_call_target="tpu_custom_call" | custom-call | flops 536870912 | bytes 2621440 | tf_op jit(solution)/shard_map/pallas_call | solution.py:37
  84.6 3.3 %collective-permute-done.6.refs_7_.refs_1_ = bf16[128,512]{1,0:T(8,128)(2,1)S(1)} collective-permute-done((bf16[128,512]{1,0:T(8,128)(2,1)S(1)}, bf16[128,512]{1,0:T(8,128)(2,1)S(1)}, u32[]{:S(2)}, u32[]{:S(2)}) %collective-permute-start.6) | collective-permute-done | bytes 131104 | tf_op jit(solution)/shard_map/ppermute | solution.py:189
  90.6 1.9 %collective-permute-start.9 = (bf16[8,128,256]{2,1,0:T(8,128)(2,1)S(1)}, bf16[8,128,256]{2,1,0:T(8,128)(2,1)S(1)}, u32[]{:S(2)}, u32[]{:S(2)}) collective-permute-start(bf16[8,128,256]{2,1,0:T(8,128)(2,1)S(1)} %get-tuple-element.25.refs_6_), channel_id=1, source_target_pairs={{0,1},{1,0},{2,3},{3,2},{4,5},{5,4},{6,7},{7,6},{8,9},{9,8},{10,11... | collective-permute-start | bytes 1572872 | tf_op jit(solution)/shard_map/ppermute | solution.py:193
  92.5 1.9 %collective-permute-done.9.refs_1_ = bf16[8,128,256]{2,1,0:T(8,128)(2,1)S(1)} collective-permute-done((bf16[8,128,256]{2,1,0:T(8,128)(2,1)S(1)}, bf16[8,128,256]{2,1,0:T(8,128)(2,1)S(1)}, u32[]{:S(2)}, u32[]{:S(2)}) %collective-permute-start.9) | collective-permute-done | bytes 524320 | tf_op jit(solution)/shard_map/ppermute | solution.py:193
  95.3 7.6 %all-to-all-start.1 = ((bf16[8,128,256]{2,1,0:T(8,128)(2,1)}), bf16[8,128,256]{2,1,0:T(8,128)(2,1)S(1)}, u32[]{:S(2)}, u32[]{:S(2)}) async-start(bf16[8,128,256]{2,1,0:T(8,128)(2,1)} %shard_map.114), calls=%async_computation.1 | async-start | bytes 1048576 | tf_op jit(solution)/shard_map/all_to_all | solution.py:197
  106.6 6.0 %collective-permute-done.11.refs_2_ = bf16[128,512]{1,0:T(8,128)(2,1)S(1)} collective-permute-done((bf16[128,512]{1,0:T(8,128)(2,1)S(1)}, bf16[128,512]{1,0:T(8,128)(2,1)S(1)}, u32[]{:S(2)}, u32[]{:S(2)}) %collective-permute-start.11) | collective-permute-done | bytes 131104 | tf_op jit(solution)/shard_map/ppermute | solution.py:180
  112.7 1.7 %shard_map.116 = (bf16[128,512]{1,0:T(8,128)(2,1)}, bf16[128,512]{1,0:T(8,128)(2,1)}) custom-call(f32[32,128]{1,0:T(8,128)S(1)} %bitcast.13, bf16[128,512]{1,0:T(8,128)(2,1)S(1)} %get-tuple-element.29.refs_1_.refs_0_, bf16[128,512]{1,0:T(8,128)(2,1)S(1)} %collective-permute-done.11.refs_2_, bf16[128,512]{1,0:T(8,128)(2,1)S(1)} %copy-done.3, ...), custom_call_target="tpu_custom_call" | custom-call | flops 1073741824 | bytes 802816 | tf_op jit(solution)/shard_map/pallas_call | solution.py:37
  115.9 9.1 %all-to-all-start.2 = ((bf16[32,32,128]{2,1,0:T(8,128)(2,1)}), bf16[32,32,128]{2,1,0:T(8,128)(2,1)S(1)}, u32[]{:S(2)}, u32[]{:S(2)}) async-start(bf16[32,32,128]{2,1,0:T(8,128)(2,1)} %shard_map.118), calls=%async_computation.2 | async-start | bytes 524288 | tf_op jit(solution)/shard_map/all_to_all | solution.py:276
  125.1 2.5 %collective-permute-start.10 = (bf16[128,256]{1,0:T(8,128)(2,1)S(1)}, bf16[128,256]{1,0:T(8,128)(2,1)S(1)}, u32[]{:S(2)}, u32[]{:S(2)}) collective-permute-start(bf16[128,256]{1,0:T(8,128)(2,1)S(1)} %reduce_sum.21), channel_id=1, source_target_pairs={{0,0},{1,1},{2,2},{3,3},{4,128},{5,129},{6,130},{7,131},{8,256},{9... | collective-permute-start | bytes 196616 | tf_op jit(solution)/shard_map/ppermute | solution.py:207
  127.7 8.3 %collective-permute-done.10 = bf16[128,256]{1,0:T(8,128)(2,1)S(1)} collective-permute-done((bf16[128,256]{1,0:T(8,128)(2,1)S(1)}, bf16[128,256]{1,0:T(8,128)(2,1)S(1)}, u32[]{:S(2)}, u32[]{:S(2)}) %collective-permute-start.10) | collective-permute-done | bytes 65568 | tf_op jit(solution)/shard_map/ppermute | solution.py:207
  136.0 2.2 %all-to-all-done.2 = bf16[32,32,128]{2,1,0:T(8,128)(2,1)S(1)} async-done(((bf16[32,32,128]{2,1,0:T(8,128)(2,1)}), bf16[32,32,128]{2,1,0:T(8,128)(2,1)S(1)}, u32[]{:S(2)}, u32[]{:S(2)}) %all-to-all-start.2) | async-done | bytes 262176 | tf_op jit(solution)/shard_map/all_to_all | solution.py:276
  (47 shorter events, 16.4 us)
Async XLA Ops:
  7.2 59.7 %all-gather.3.cloned.1.call-start = ((), (), s32[]{:S(2)}) async-start(), calls=%async_computation.5 | async-start | bytes 1179648 | tf_op jit(solution)/shard_map/all_gather | solution.py:213
  7.2 5.5 %copy-start.6 = (f32[128,32]{0,1:T(8,128)S(1)}, f32[128,32]{0,1:T(8,128)}, u32[]{:S(2)}) copy-start(f32[128,32]{0,1:T(8,128)} %param.9) | copy-start | bytes 49156
  8.2 7.2 %copy-start.5 = (bf16[128,512]{1,0:T(8,128)(2,1)S(1)}, bf16[128,512]{1,0:T(8,128)(2,1)}, u32[]{:S(2)}) copy-start(bf16[128,512]{1,0:T(8,128)(2,1)} %refs_4_.2) | copy-start | bytes 393220
  8.2 7.2 %collective-permute-start = (bf16[128,512]{1,0:T(8,128)(2,1)S(1)}, bf16[128,512]{1,0:T(8,128)(2,1)S(1)}, u32[]{:S(2)}, u32[]{:S(2)}) collective-permute-start(bf16[128,512]{1,0:T(8,128)(2,1)S(1)} %multiply_convert_fusion.refs_1_), channel_id=1, source_target_pairs={{0,16},{16,32},{32,48},{48,64},{64,80},{80,96},{96,112},{112,128},... | collective-permute-start | bytes 393224 | tf_op jit(solution)/shard_map/ppermute | solution.py:180
  12.7 126.2 %reduce-scatter.2.cloned.1.call-start = ((), (), s32[]{:S(2)}) async-start(), calls=%async_computation.4 | async-start | bytes 1179648 | tf_op jit(solution)/shard_map/reduce_scatter | solution.py:280
  13.0 18.6 %copy-start.7 = (bf16[128,256]{1,0:T(8,128)(2,1)S(1)}, bf16[128,256]{1,0:T(8,128)(2,1)}, u32[]{:S(2)}) copy-start(bf16[128,256]{1,0:T(8,128)(2,1)} %param.11) | copy-start | bytes 196612
  17.0 23.7 %collective-permute-start.1 = (bf16[128,512]{1,0:T(8,128)(2,1)S(1)}, bf16[128,512]{1,0:T(8,128)(2,1)S(1)}, u32[]{:S(2)}, u32[]{:S(2)}) collective-permute-start(bf16[128,512]{1,0:T(8,128)(2,1)S(1)} %get-tuple-element.19.refs_1_), channel_id=1, source_target_pairs={{0,128},{16,144},{32,160},{48,176},{64,192},{80,208},{96,224},{112... | collective-permute-start | bytes 393224 | tf_op jit(solution)/shard_map/ppermute | solution.py:189
  31.5 9.2 %collective-permute-start.4 = (bf16[128,256]{1,0:T(8,128)(2,1)S(1)}, bf16[128,256]{1,0:T(8,128)(2,1)S(1)}, u32[]{:S(2)}, u32[]{:S(2)}) collective-permute-start(bf16[128,256]{1,0:T(8,128)(2,1)S(1)} %copy-done.7), channel_id=1, source_target_pairs={{0,0},{1,1},{2,2},{3,3},{4,128},{5,129},{6,130},{7,131},{8,256},{9... | collective-permute-start | bytes 196616 | tf_op jit(solution)/shard_map/ppermute | solution.py:207
  56.0 10.8 %collective-permute-start.5 = (bf16[8,128,256]{2,1,0:T(8,128)(2,1)S(1)}, bf16[8,128,256]{2,1,0:T(8,128)(2,1)S(1)}, u32[]{:S(2)}, u32[]{:S(2)}) collective-permute-start(bf16[8,128,256]{2,1,0:T(8,128)(2,1)S(1)} %all_to_all.15.refs_1_), channel_id=1, source_target_pairs={{0,1},{1,0},{2,3},{3,2},{4,5},{5,4},{6,7},{7,6},{8,9},{9,8},{10,11... | collective-permute-start | bytes 1572872 | tf_op jit(solution)/shard_map/ppermute | solution.py:193
  58.1 24.2 %collective-permute-start.2 = (bf16[128,512]{1,0:T(8,128)(2,1)S(1)}, bf16[128,512]{1,0:T(8,128)(2,1)S(1)}, u32[]{:S(2)}, u32[]{:S(2)}) collective-permute-start(bf16[128,512]{1,0:T(8,128)(2,1)S(1)} %get-tuple-element.19.refs_1_), channel_id=1, source_target_pairs={{0,256},{16,272},{32,288},{48,304},{64,320},{80,336},{96,352},{112... | collective-permute-start | bytes 393224 | tf_op jit(solution)/shard_map/ppermute | solution.py:189
  63.3 18.9 %collective-permute-start.3 = (bf16[128,512]{1,0:T(8,128)(2,1)S(1)}, bf16[128,512]{1,0:T(8,128)(2,1)S(1)}, u32[]{:S(2)}, u32[]{:S(2)}) collective-permute-start(bf16[128,512]{1,0:T(8,128)(2,1)S(1)} %get-tuple-element.19.refs_1_), channel_id=1, source_target_pairs={{0,384},{16,400},{32,416},{48,432},{64,448},{80,464},{96,480},{112... | collective-permute-start | bytes 393224 | tf_op jit(solution)/shard_map/ppermute | solution.py:189
  66.9 1.2 copy-start
  70.1 17.8 %collective-permute-start.6 = (bf16[128,512]{1,0:T(8,128)(2,1)S(1)}, bf16[128,512]{1,0:T(8,128)(2,1)S(1)}, u32[]{:S(2)}, u32[]{:S(2)}) collective-permute-start(bf16[128,512]{1,0:T(8,128)(2,1)S(1)} %get-tuple-element.21.refs_6_), channel_id=1, source_target_pairs={{0,128},{16,144},{32,160},{48,176},{64,192},{80,208},{96,224},{112... | collective-permute-start | bytes 393224 | tf_op jit(solution)/shard_map/ppermute | solution.py:189
  73.3 14.5 %collective-permute-start.7 = (bf16[128,512]{1,0:T(8,128)(2,1)S(1)}, bf16[128,512]{1,0:T(8,128)(2,1)S(1)}, u32[]{:S(2)}, u32[]{:S(2)}) collective-permute-start(bf16[128,512]{1,0:T(8,128)(2,1)S(1)} %get-tuple-element.22), channel_id=1, source_target_pairs={{0,256},{16,272},{32,288},{48,304},{64,320},{80,336},{96,352},{112... | collective-permute-start | bytes 393224 | tf_op jit(solution)/shard_map/ppermute | solution.py:189
  77.8 11.3 %collective-permute-start.8 = (bf16[128,512]{1,0:T(8,128)(2,1)S(1)}, bf16[128,512]{1,0:T(8,128)(2,1)S(1)}, u32[]{:S(2)}, u32[]{:S(2)}) collective-permute-start(bf16[128,512]{1,0:T(8,128)(2,1)S(1)} %get-tuple-element.23), channel_id=1, source_target_pairs={{0,384},{16,400},{32,416},{48,432},{64,448},{80,464},{96,480},{112... | collective-permute-start | bytes 393224 | tf_op jit(solution)/shard_map/ppermute | solution.py:189
  84.6 4.6 %copy-start.1 = (bf16[4096,128]{1,0:T(8,128)(2,1)S(1)}, bf16[4096,128]{1,0:T(8,128)(2,1)}, u32[]{:S(2)}) copy-start(bf16[4096,128]{1,0:T(8,128)(2,1)} %all-gather.3.cloned.1.call-done) | copy-start | bytes 3145732
  90.6 3.8 %collective-permute-start.9 = (bf16[8,128,256]{2,1,0:T(8,128)(2,1)S(1)}, bf16[8,128,256]{2,1,0:T(8,128)(2,1)S(1)}, u32[]{:S(2)}, u32[]{:S(2)}) collective-permute-start(bf16[8,128,256]{2,1,0:T(8,128)(2,1)S(1)} %get-tuple-element.25.refs_6_), channel_id=1, source_target_pairs={{0,1},{1,0},{2,3},{3,2},{4,5},{5,4},{6,7},{7,6},{8,9},{9,8},{10,11... | collective-permute-start | bytes 1572872 | tf_op jit(solution)/shard_map/ppermute | solution.py:193
  95.3 19.0 %all-to-all-start.1 = ((bf16[8,128,256]{2,1,0:T(8,128)(2,1)}), bf16[8,128,256]{2,1,0:T(8,128)(2,1)S(1)}, u32[]{:S(2)}, u32[]{:S(2)}) async-start(bf16[8,128,256]{2,1,0:T(8,128)(2,1)} %shard_map.114), calls=%async_computation.1 | async-start | bytes 1048576 | tf_op jit(solution)/shard_map/all_to_all | solution.py:197
  103.6 9.0 %copy-start.2 = (bf16[128,512]{1,0:T(8,128)(2,1)S(1)}, bf16[128,512]{1,0:T(8,128)(2,1)}, u32[]{:S(2)}) copy-start(bf16[128,512]{1,0:T(8,128)(2,1)} %refs_4_.3) | copy-start | bytes 393220
  103.6 9.0 %copy-start.3 = (bf16[128,512]{1,0:T(8,128)(2,1)S(1)}, bf16[128,512]{1,0:T(8,128)(2,1)}, u32[]{:S(2)}) copy-start(bf16[128,512]{1,0:T(8,128)(2,1)} %refs_3_.3) | copy-start | bytes 393220
  103.6 9.0 %collective-permute-start.11 = (bf16[128,512]{1,0:T(8,128)(2,1)S(1)}, bf16[128,512]{1,0:T(8,128)(2,1)S(1)}, u32[]{:S(2)}, u32[]{:S(2)}) collective-permute-start(bf16[128,512]{1,0:T(8,128)(2,1)S(1)} %get-tuple-element.29.refs_1_.refs_0_), channel_id=1, source_target_pairs={{16,0},{32,16},{48,32},{64,48},{80,64},{96,80},{112,96},{128,112},... | collective-permute-start | bytes 393224 | tf_op jit(solution)/shard_map/ppermute | solution.py:180
  114.3 0.9 copy-start.4
  115.9 22.3 %all-to-all-start.2 = ((bf16[32,32,128]{2,1,0:T(8,128)(2,1)}), bf16[32,32,128]{2,1,0:T(8,128)(2,1)S(1)}, u32[]{:S(2)}, u32[]{:S(2)}) async-start(bf16[32,32,128]{2,1,0:T(8,128)(2,1)} %shard_map.118), calls=%async_computation.2 | async-start | bytes 524288 | tf_op jit(solution)/shard_map/all_to_all | solution.py:276
  125.1 10.8 %collective-permute-start.10 = (bf16[128,256]{1,0:T(8,128)(2,1)S(1)}, bf16[128,256]{1,0:T(8,128)(2,1)S(1)}, u32[]{:S(2)}, u32[]{:S(2)}) collective-permute-start(bf16[128,256]{1,0:T(8,128)(2,1)S(1)} %reduce_sum.21), channel_id=1, source_target_pairs={{0,0},{1,1},{2,2},{3,3},{4,128},{5,129},{6,130},{7,131},{8,256},{9... | collective-permute-start | bytes 196616 | tf_op jit(solution)/shard_map/ppermute | solution.py:207
Sparse Core Ops, SparseCore 0:
  12.8 45.8 all-gather.2
  84.7 35.3 reduce-scatter.1

commit v3 on v2

--- a/solution.py
+++ b/solution.py
@@ -222,18 +222,28 @@
         (forward_rows, product, halo, q_proj),
         [pltpu.VMEM((1024, 512), BF16)],
         flops=2 * 4096 * 512 * 128 * 4,
+        after=(piece,),
     )
     mixed4 = [mixed] + [shift_y(mixed, d) for d in (1, 2, 3)]
-    own8 = call(spread_body, shaped((8, 128, 256), BF16), (piece,), after=mixed4[1:2])
+    own8 = call(spread_body, shaped((8, 128, 256), BF16), (piece,), after=mixed4[1:])
     own8 = exchange(own8, "col", CHIP_GROUPS)
     pair8 = other_core(own8)
 
+    keep, give = call(
+        projected_body,
+        [shaped((8, 128, 256), F32), shaped((8, 128, 256), BF16)],
+        (*mixed4, w8),
+        [pltpu.VMEM((COLS, 128, 256), F32)],
+        flops=2 * 512 * 512 * 1024,
+        position=at,
+    )
     cot16, *shares = call(
         grad_mixed_body,
         [shaped((COLS, 128, 256), BF16)] + [tile] * YS,
         (own8, pair8, w8),
         flops=2 * 512 * 512 * 1024,
         position=at,
+        after=(give,),
     )
     sums = [shares[0]] + [shift_y(shares[d], d) for d in (1, 2, 3)]
     gw8 = call(
@@ -244,17 +254,8 @@
         position=at,
         after=(shares[1],),
     )
-    keep, give = call(
-        projected_body,
-        [shaped((8, 128, 256), F32), shaped((8, 128, 256), BF16)],
-        (*mixed4, w8),
-        [pltpu.VMEM((COLS, 128, 256), F32)],
-        flops=2 * 512 * 512 * 1024,
-        position=at,
-        after=[gw8] + sums[1:],
-    )
-    pieces = call(pair_body, shaped((8, 128, 256), BF16), (keep, other_core(give)))
-    grad_q, grad_conv = call(grad_conv_body, [tile, tile], (*sums, q_proj, conv), after=(give,))
+    pieces = call(pair_body, shaped((8, 128, 256), BF16), (keep, other_core(give)), after=sums[1:])
+    grad_q, grad_conv = call(grad_conv_body, [tile, tile], (*sums, q_proj, conv))
     later = shift_row(grad_conv, -1)
     grad_taps = call(
         grad_filters_body,

time: 149 us -> 155 us (1.040)
  the two profiles are of different devices: /device:TPU:8 before, /device:TPU:4 now
where the time goes in v3:
time: 155 us
  starting transfers between devices  71.2 us (46%)
  waiting for transfers between devices  32.6 us (21%)
  between operations  14.4 us (9%)
  Pallas kernels  12.9 us (8%)
  blocking collectives  11.7 us (8%)
  local copies, waits for them, and re-layouts  8.46 us (5%)
  other arithmetic  3.44 us (2%)
    ppermute x6, starting transfers between devices, shift_y(): return lax.ppermute(block, 'row', route)  31.6 us
    all_to_all x1, starting transfers between devices, local(): lax.all_to_all(grad_taps, 'row', 0, 0, tiled=True).astype(F32)  14.5 us
    ppermute x6, waiting for transfers between devices, shift_y(): return lax.ppermute(block, 'row', route)  13.4 us
    pallas_call x10, Pallas kernels, call(): pl.pallas_call(run, out_shape=out_shape, in_specs=specs, scratch_shapes=l...  12.9 us
    all_to_all x1, blocking collectives, exchange(): lax.all_to_all(blocks, axis, 0, 0, axis_index_groups=groups, tiled=True)  11.7 us
    ppermute x2, waiting for transfers between devices, swap_pieces(): return lax.ppermute(piece, ('row', 'col'), route)  10.8 us
    ppermute x2, starting transfers between devices, swap_pieces(): return lax.ppermute(piece, ('row', 'col'), route)  8.77 us
    unnamed x45, local copies, waits for them, and re-layouts  7.63 us
  transfers between devices with their start and end apart: 16, of which 8 were waited for; matrix products, arithmetic and copies ran while one was open for 1% of the time, Pallas kernels for 6%

profile of v3, /device:TPU:4, one launch (start us, length us, event | category | flops | bytes accessed | tf_op | source)
XLA Modules:
  0.0 154.6 jit_solution(15219490682680682009)
XLA Ops:
  8.3 4.4 %collective-permute-start = (bf16[128,512]{1,0:T(8,128)(2,1)S(1)}, bf16[128,512]{1,0:T(8,128)(2,1)S(1)}, u32[]{:S(2)}, u32[]{:S(2)}) collective-permute-start(bf16[128,512]{1,0:T(8,128)(2,1)S(1)} %multiply_convert_fusion.refs_1_), channel_id=1, source_target_pairs={{0,16},{16,32},{32,48},{48,64},{64,80},{80,96},{96,112},{112,128},... | collective-permute-start | bytes 393224 | tf_op jit(solution)/shard_map/ppermute | solution.py:180
  12.8 4.4 %collective-permute-start.1 = (bf16[128,256]{1,0:T(8,128)(2,1)S(1)}, bf16[128,256]{1,0:T(8,128)(2,1)S(1)}, u32[]{:S(2)}, u32[]{:S(2)}) collective-permute-start(bf16[128,256]{1,0:T(8,128)(2,1)S(1)} %copy-done.21), channel_id=1, source_target_pairs={{0,0},{1,1},{2,2},{3,3},{4,128},{5,129},{6,130},{7,131},{8,256},{9... | collective-permute-start | bytes 196616 | tf_op jit(solution)/shard_map/ppermute | solution.py:207
  17.5 4.8 %collective-permute-done.1.refs_4_.refs_0_ = bf16[128,256]{1,0:T(8,128)(2,1)S(1)} collective-permute-done((bf16[128,256]{1,0:T(8,128)(2,1)S(1)}, bf16[128,256]{1,0:T(8,128)(2,1)S(1)}, u32[]{:S(2)}, u32[]{:S(2)}) %collective-permute-start.1) | collective-permute-done | bytes 65568 | tf_op jit(solution)/shard_map/ppermute | solution.py:207
  23.9 12.6 %collective-permute-start.4 = (bf16[128,512]{1,0:T(8,128)(2,1)S(1)}, bf16[128,512]{1,0:T(8,128)(2,1)S(1)}, u32[]{:S(2)}, u32[]{:S(2)}) collective-permute-start(bf16[128,512]{1,0:T(8,128)(2,1)S(1)} %get-tuple-element.19.refs_1_), channel_id=1, source_target_pairs={{0,384},{16,400},{32,416},{48,432},{64,448},{80,464},{96,480},{112... | collective-permute-start | bytes 393224 | tf_op jit(solution)/shard_map/ppermute | solution.py:189
  36.5 1.9 %collective-permute-start.3 = (bf16[128,512]{1,0:T(8,128)(2,1)S(1)}, bf16[128,512]{1,0:T(8,128)(2,1)S(1)}, u32[]{:S(2)}, u32[]{:S(2)}) collective-permute-start(bf16[128,512]{1,0:T(8,128)(2,1)S(1)} %get-tuple-element.19.refs_1_), channel_id=1, source_target_pairs={{0,256},{16,272},{32,288},{48,304},{64,320},{80,336},{96,352},{112... | collective-permute-start | bytes 393224 | tf_op jit(solution)/shard_map/ppermute | solution.py:189
  38.5 4.3 %collective-permute-start.2 = (bf16[128,512]{1,0:T(8,128)(2,1)S(1)}, bf16[128,512]{1,0:T(8,128)(2,1)S(1)}, u32[]{:S(2)}, u32[]{:S(2)}) collective-permute-start(bf16[128,512]{1,0:T(8,128)(2,1)S(1)} %get-tuple-element.19.refs_1_), channel_id=1, source_target_pairs={{0,128},{16,144},{32,160},{48,176},{64,192},{80,208},{96,224},{112... | collective-permute-start | bytes 393224 | tf_op jit(solution)/shard_map/ppermute | solution.py:189
  43.4 4.9 %collective-permute-done.3.refs_3_.refs_2_ = bf16[128,512]{1,0:T(8,128)(2,1)S(1)} collective-permute-done((bf16[128,512]{1,0:T(8,128)(2,1)S(1)}, bf16[128,512]{1,0:T(8,128)(2,1)S(1)}, u32[]{:S(2)}, u32[]{:S(2)}) %collective-permute-start.3) | collective-permute-done | bytes 131104 | tf_op jit(solution)/shard_map/ppermute | solution.py:189
  48.3 1.9 %collective-permute-done.2.refs_2_.refs_1_ = bf16[128,512]{1,0:T(8,128)(2,1)S(1)} collective-permute-done((bf16[128,512]{1,0:T(8,128)(2,1)S(1)}, bf16[128,512]{1,0:T(8,128)(2,1)S(1)}, u32[]{:S(2)}, u32[]{:S(2)}) %collective-permute-start.2) | collective-permute-done | bytes 131104 | tf_op jit(solution)/shard_map/ppermute | solution.py:189
  50.2 11.7 %all_to_all.15.refs_1_ = bf16[8,128,256]{2,1,0:T(8,128)(2,1)S(1)} all-to-all(bf16[8,128,256]{2,1,0:T(8,128)(2,1)S(1)} %shard_map.111), channel_id=1, replica_groups={{0,2,4,6,8,10,12,14},{1,3,5,7,9,11,13,15},{16,18,20,22,24,26,28,30},{17..., dimensions={0} | all-to-all | bytes 1048576 | tf_op jit(solution)/shard_map/all_to_all | solution.py:197
  61.9 1.9 %collective-permute-start.6 = (bf16[8,128,256]{2,1,0:T(8,128)(2,1)S(1)}, bf16[8,128,256]{2,1,0:T(8,128)(2,1)S(1)}, u32[]{:S(2)}, u32[]{:S(2)}) collective-permute-start(bf16[8,128,256]{2,1,0:T(8,128)(2,1)S(1)} %all_to_all.15.refs_1_), channel_id=1, source_target_pairs={{0,1},{1,0},{2,3},{3,2},{4,5},{5,4},{6,7},{7,6},{8,9},{9,8},{10,11... | collective-permute-start | bytes 1572872 | tf_op jit(solution)/shard_map/ppermute | solution.py:193
  68.6 2.0 %shard_map.112 = (bf16[16,128,256]{2,1,0:T(8,128)(2,1)S(1)}, bf16[128,512]{1,0:T(8,128)(2,1)S(1)}, bf16[128,512]{1,0:T(8,128)(2,1)S(1)}, bf16[128,512]{1,0:T(8,128)(2,1)S(1)}, bf16[128,512]{1,0:T(8,128)(2,1)S(1)}) custom-call(s32[2]{0:T(128)S(1)} %copy-done.14, bf16[8,128,256]{2,1,0:T(8,128)(2,1)S(1)} %all_to_all.15.refs_1_, ...), custom_call_target="tpu_custom_call" | custom-call | flops 536870912 | bytes 3670016 | tf_op jit(solution)/shard_map/pallas_call | solution.py:37
  72.6 2.3 %shard_map.118 = bf16[8,512,128]{2,1,0:T(8,128)(2,1)} custom-call(s32[2]{0:T(128)S(1)} %copy-done.14, bf16[128,512]{1,0:T(8,128)(2,1)S(1)} %copy-done.7, bf16[128,512]{1,0:T(8,128)(2,1)S(1)} %collective-permute-done.2.refs_2_.refs_1_, bf16[128,512]{1,0:T(8,128)(2,1)S(1)} %collective-permute-done.3.refs_3_.refs_2_, ...), custom_call_target="tpu_custom_call" | custom-call | flops 536870912 | bytes 2621440 | tf_op jit(solution)/shard_map/pallas_call | solution.py:37
  75.5 2.5 %collective-permute-start.5 = (bf16[8,128,256]{2,1,0:T(8,128)(2,1)S(1)}, bf16[8,128,256]{2,1,0:T(8,128)(2,1)S(1)}, u32[]{:S(2)}, u32[]{:S(2)}) collective-permute-start(bf16[8,128,256]{2,1,0:T(8,128)(2,1)S(1)} %get-tuple-element.21.refs_4_), channel_id=1, source_target_pairs={{0,1},{1,0},{2,3},{3,2},{4,5},{5,4},{6,7},{7,6},{8,9},{9,8},{10,11... | collective-permute-start | bytes 1572872 | tf_op jit(solution)/shard_map/ppermute | solution.py:193
  78.1 6.0 %collective-permute-start.8 = (bf16[128,512]{1,0:T(8,128)(2,1)S(1)}, bf16[128,512]{1,0:T(8,128)(2,1)S(1)}, u32[]{:S(2)}, u32[]{:S(2)}) collective-permute-start(bf16[128,512]{1,0:T(8,128)(2,1)S(1)} %copy-done.20), channel_id=1, source_target_pairs={{0,256},{16,272},{32,288},{48,304},{64,320},{80,336},{96,352},{112... | collective-permute-start | bytes 393224 | tf_op jit(solution)/shard_map/ppermute | solution.py:189
  84.1 1.9 %collective-permute-start.9 = (bf16[128,512]{1,0:T(8,128)(2,1)S(1)}, bf16[128,512]{1,0:T(8,128)(2,1)S(1)}, u32[]{:S(2)}, u32[]{:S(2)}) collective-permute-start(bf16[128,512]{1,0:T(8,128)(2,1)S(1)} %copy-done.18), channel_id=1, source_target_pairs={{0,384},{16,400},{32,416},{48,432},{64,448},{80,464},{96,480},{112... | collective-permute-start | bytes 393224 | tf_op jit(solution)/shard_map/ppermute | solution.py:189
  86.0 4.8 %collective-permute-start.7 = (bf16[128,512]{1,0:T(8,128)(2,1)S(1)}, bf16[128,512]{1,0:T(8,128)(2,1)S(1)}, u32[]{:S(2)}, u32[]{:S(2)}) collective-permute-start(bf16[128,512]{1,0:T(8,128)(2,1)S(1)} %copy-done.12), channel_id=1, source_target_pairs={{0,128},{16,144},{32,160},{48,176},{64,192},{80,208},{96,224},{112... | collective-permute-start | bytes 393224 | tf_op jit(solution)/shard_map/ppermute | solution.py:189
  92.2 5.3 %collective-permute-done.9.refs_4_.refs_3_ = bf16[128,512]{1,0:T(8,128)(2,1)S(1)} collective-permute-done((bf16[128,512]{1,0:T(8,128)(2,1)S(1)}, bf16[128,512]{1,0:T(8,128)(2,1)S(1)}, u32[]{:S(2)}, u32[]{:S(2)}) %collective-permute-start.9) | collective-permute-done | bytes 131104 | tf_op jit(solution)/shard_map/ppermute | solution.py:189
  98.4 6.1 %all-to-all-start.1 = ((bf16[8,128,256]{2,1,0:T(8,128)(2,1)}), bf16[8,128,256]{2,1,0:T(8,128)(2,1)S(1)}, u32[]{:S(2)}, u32[]{:S(2)}) async-start(bf16[8,128,256]{2,1,0:T(8,128)(2,1)} %shard_map.113), calls=%async_computation.1 | async-start | bytes 1048576 | tf_op jit(solution)/shard_map/all_to_all | solution.py:197
  108.2 5.4 %collective-permute-done.11.refs_2_ = bf16[128,512]{1,0:T(8,128)(2,1)S(1)} collective-permute-done((bf16[128,512]{1,0:T(8,128)(2,1)S(1)}, bf16[128,512]{1,0:T(8,128)(2,1)S(1)}, u32[]{:S(2)}, u32[]{:S(2)}) %collective-permute-start.11) | collective-permute-done | bytes 131104 | tf_op jit(solution)/shard_map/ppermute | solution.py:180
  113.7 1.7 %shard_map.115 = (bf16[128,512]{1,0:T(8,128)(2,1)}, bf16[128,512]{1,0:T(8,128)(2,1)}) custom-call(f32[32,128]{1,0:T(8,128)S(1)} %bitcast.13, bf16[128,512]{1,0:T(8,128)(2,1)S(1)} %get-tuple-element.28.refs_1_.refs_0_, bf16[128,512]{1,0:T(8,128)(2,1)S(1)} %collective-permute-done.11.refs_2_, bf16[128,512]{1,0:T(8,128)(2,1)S(1)} %copy-done.4, ...), custom_call_target="tpu_custom_call" | custom-call | flops 1073741824 | bytes 802816 | tf_op jit(solution)/shard_map/pallas_call | solution.py:37
  116.9 14.5 %all-to-all-start.2 = ((bf16[32,32,128]{2,1,0:T(8,128)(2,1)}), bf16[32,32,128]{2,1,0:T(8,128)(2,1)S(1)}, u32[]{:S(2)}, u32[]{:S(2)}) async-start(bf16[32,32,128]{2,1,0:T(8,128)(2,1)} %shard_map.117), calls=%async_computation.2 | async-start | bytes 524288 | tf_op jit(solution)/shard_map/all_to_all | solution.py:277
  131.5 4.3 %collective-permute-start.10 = (bf16[128,256]{1,0:T(8,128)(2,1)S(1)}, bf16[128,256]{1,0:T(8,128)(2,1)S(1)}, u32[]{:S(2)}, u32[]{:S(2)}) collective-permute-start(bf16[128,256]{1,0:T(8,128)(2,1)S(1)} %reduce_sum.21), channel_id=1, source_target_pairs={{0,0},{1,1},{2,2},{3,3},{4,128},{5,129},{6,130},{7,131},{8,256},{9... | collective-permute-start | bytes 196616 | tf_op jit(solution)/shard_map/ppermute | solution.py:207
  135.8 6.0 %collective-permute-done.10 = bf16[128,256]{1,0:T(8,128)(2,1)S(1)} collective-permute-done((bf16[128,256]{1,0:T(8,128)(2,1)S(1)}, bf16[128,256]{1,0:T(8,128)(2,1)S(1)}, u32[]{:S(2)}, u32[]{:S(2)}) %collective-permute-start.10) | collective-permute-done | bytes 65568 | tf_op jit(solution)/shard_map/ppermute | solution.py:207
  141.8 3.0 %all-to-all-done.2 = bf16[32,32,128]{2,1,0:T(8,128)(2,1)S(1)} async-done(((bf16[32,32,128]{2,1,0:T(8,128)(2,1)}), bf16[32,32,128]{2,1,0:T(8,128)(2,1)S(1)}, u32[]{:S(2)}, u32[]{:S(2)}) %all-to-all-start.2) | async-done | bytes 262176 | tf_op jit(solution)/shard_map/all_to_all | solution.py:277
  (75 shorter events, 21.7 us)
Async XLA Ops:
  7.2 57.2 %all-gather.3.cloned.1.call-start = ((), (), s32[]{:S(2)}) async-start(), calls=%async_computation.5 | async-start | bytes 1179648 | tf_op jit(solution)/shard_map/all_gather | solution.py:213
  7.2 5.6 %copy-start.21 = (bf16[128,256]{1,0:T(8,128)(2,1)S(1)}, bf16[128,256]{1,0:T(8,128)(2,1)}, u32[]{:S(2)}) copy-start(bf16[128,256]{1,0:T(8,128)(2,1)} %param.11) | copy-start | bytes 196612
  7.2 10.0 %copy-start.13 = (f32[128,32]{0,1:T(8,128)S(1)}, f32[128,32]{0,1:T(8,128)}, u32[]{:S(2)}) copy-start(f32[128,32]{0,1:T(8,128)} %param.9) | copy-start | bytes 49156
  8.3 14.0 %copy-start.2 = (bf16[128,512]{1,0:T(8,128)(2,1)S(1)}, bf16[128,512]{1,0:T(8,128)(2,1)}, u32[]{:S(2)}) copy-start(bf16[128,512]{1,0:T(8,128)(2,1)} %refs_4_.2) | copy-start | bytes 393220
  8.3 14.0 %collective-permute-start = (bf16[128,512]{1,0:T(8,128)(2,1)S(1)}, bf16[128,512]{1,0:T(8,128)(2,1)S(1)}, u32[]{:S(2)}, u32[]{:S(2)}) collective-permute-start(bf16[128,512]{1,0:T(8,128)(2,1)S(1)} %multiply_convert_fusion.refs_1_), channel_id=1, source_target_pairs={{0,16},{16,32},{32,48},{48,64},{64,80},{80,96},{96,112},{112,128},... | collective-permute-start | bytes 393224 | tf_op jit(solution)/shard_map/ppermute | solution.py:180
  12.7 132.8 %reduce-scatter.2.cloned.1.call-start = ((), (), s32[]{:S(2)}) async-start(), calls=%async_computation.4 | async-start | bytes 1179648 | tf_op jit(solution)/shard_map/reduce_scatter | solution.py:281
  12.8 9.5 %collective-permute-start.1 = (bf16[128,256]{1,0:T(8,128)(2,1)S(1)}, bf16[128,256]{1,0:T(8,128)(2,1)S(1)}, u32[]{:S(2)}, u32[]{:S(2)}) collective-permute-start(bf16[128,256]{1,0:T(8,128)(2,1)S(1)} %copy-done.21), channel_id=1, source_target_pairs={{0,0},{1,1},{2,2},{3,3},{4,128},{5,129},{6,130},{7,131},{8,256},{9... | collective-permute-start | bytes 196616 | tf_op jit(solution)/shard_map/ppermute | solution.py:207
  23.9 19.5 %collective-permute-start.4 = (bf16[128,512]{1,0:T(8,128)(2,1)S(1)}, bf16[128,512]{1,0:T(8,128)(2,1)S(1)}, u32[]{:S(2)}, u32[]{:S(2)}) collective-permute-start(bf16[128,512]{1,0:T(8,128)(2,1)S(1)} %get-tuple-element.19.refs_1_), channel_id=1, source_target_pairs={{0,384},{16,400},{32,416},{48,432},{64,448},{80,464},{96,480},{112... | collective-permute-start | bytes 393224 | tf_op jit(solution)/shard_map/ppermute | solution.py:189
  36.5 11.7 %collective-permute-start.3 = (bf16[128,512]{1,0:T(8,128)(2,1)S(1)}, bf16[128,512]{1,0:T(8,128)(2,1)S(1)}, u32[]{:S(2)}, u32[]{:S(2)}) collective-permute-start(bf16[128,512]{1,0:T(8,128)(2,1)S(1)} %get-tuple-element.19.refs_1_), channel_id=1, source_target_pairs={{0,256},{16,272},{32,288},{48,304},{64,320},{80,336},{96,352},{112... | collective-permute-start | bytes 393224 | tf_op jit(solution)/shard_map/ppermute | solution.py:189
  38.5 11.6 %collective-permute-start.2 = (bf16[128,512]{1,0:T(8,128)(2,1)S(1)}, bf16[128,512]{1,0:T(8,128)(2,1)S(1)}, u32[]{:S(2)}, u32[]{:S(2)}) collective-permute-start(bf16[128,512]{1,0:T(8,128)(2,1)S(1)} %get-tuple-element.19.refs_1_), channel_id=1, source_target_pairs={{0,128},{16,144},{32,160},{48,176},{64,192},{80,208},{96,224},{112... | collective-permute-start | bytes 393224 | tf_op jit(solution)/shard_map/ppermute | solution.py:189
  61.9 6.7 %collective-permute-start.6 = (bf16[8,128,256]{2,1,0:T(8,128)(2,1)S(1)}, bf16[8,128,256]{2,1,0:T(8,128)(2,1)S(1)}, u32[]{:S(2)}, u32[]{:S(2)}) collective-permute-start(bf16[8,128,256]{2,1,0:T(8,128)(2,1)S(1)} %all_to_all.15.refs_1_), channel_id=1, source_target_pairs={{0,1},{1,0},{2,3},{3,2},{4,5},{5,4},{6,7},{7,6},{8,9},{9,8},{10,11... | collective-permute-start | bytes 1572872 | tf_op jit(solution)/shard_map/ppermute | solution.py:193
  75.5 8.6 %copy-start.18 = (bf16[128,512]{1,0:T(8,128)(2,1)S(1)}, bf16[128,512]{1,0:T(8,128)(2,1)}, u32[]{:S(2)}) copy-start(bf16[128,512]{1,0:T(8,128)(2,1)} %copy-done.17) | copy-start | bytes 393220
  75.5 10.5 %copy-start.12 = (bf16[128,512]{1,0:T(8,128)(2,1)S(1)}, bf16[128,512]{1,0:T(8,128)(2,1)}, u32[]{:S(2)}) copy-start(bf16[128,512]{1,0:T(8,128)(2,1)} %copy-done.11) | copy-start | bytes 393220
  75.5 22.0 %collective-permute-start.5 = (bf16[8,128,256]{2,1,0:T(8,128)(2,1)S(1)}, bf16[8,128,256]{2,1,0:T(8,128)(2,1)S(1)}, u32[]{:S(2)}, u32[]{:S(2)}) collective-permute-start(bf16[8,128,256]{2,1,0:T(8,128)(2,1)S(1)} %get-tuple-element.21.refs_4_), channel_id=1, source_target_pairs={{0,1},{1,0},{2,3},{3,2},{4,5},{5,4},{6,7},{7,6},{8,9},{9,8},{10,11... | collective-permute-start | bytes 1572872 | tf_op jit(solution)/shard_map/ppermute | solution.py:193
  78.1 14.1 %collective-permute-start.8 = (bf16[128,512]{1,0:T(8,128)(2,1)S(1)}, bf16[128,512]{1,0:T(8,128)(2,1)S(1)}, u32[]{:S(2)}, u32[]{:S(2)}) collective-permute-start(bf16[128,512]{1,0:T(8,128)(2,1)S(1)} %copy-done.20), channel_id=1, source_target_pairs={{0,256},{16,272},{32,288},{48,304},{64,320},{80,336},{96,352},{112... | collective-permute-start | bytes 393224 | tf_op jit(solution)/shard_map/ppermute | solution.py:189
  84.1 13.4 %collective-permute-start.9 = (bf16[128,512]{1,0:T(8,128)(2,1)S(1)}, bf16[128,512]{1,0:T(8,128)(2,1)S(1)}, u32[]{:S(2)}, u32[]{:S(2)}) collective-permute-start(bf16[128,512]{1,0:T(8,128)(2,1)S(1)} %copy-done.18), channel_id=1, source_target_pairs={{0,384},{16,400},{32,416},{48,432},{64,448},{80,464},{96,480},{112... | collective-permute-start | bytes 393224 | tf_op jit(solution)/shard_map/ppermute | solution.py:189
  86.0 11.5 %collective-permute-start.7 = (bf16[128,512]{1,0:T(8,128)(2,1)S(1)}, bf16[128,512]{1,0:T(8,128)(2,1)S(1)}, u32[]{:S(2)}, u32[]{:S(2)}) collective-permute-start(bf16[128,512]{1,0:T(8,128)(2,1)S(1)} %copy-done.12), channel_id=1, source_target_pairs={{0,128},{16,144},{32,160},{48,176},{64,192},{80,208},{96,224},{112... | collective-permute-start | bytes 393224 | tf_op jit(solution)/shard_map/ppermute | solution.py:189
  98.4 6.1 %copy-start.9 = (bf16[128,512]{1,0:T(8,128)(2,1)S(1)}, bf16[128,512]{1,0:T(8,128)(2,1)}, u32[]{:S(2)}) copy-start(bf16[128,512]{1,0:T(8,128)(2,1)} %copy-done.8) | copy-start | bytes 393220
  98.4 16.9 %all-to-all-start.1 = ((bf16[8,128,256]{2,1,0:T(8,128)(2,1)}), bf16[8,128,256]{2,1,0:T(8,128)(2,1)S(1)}, u32[]{:S(2)}, u32[]{:S(2)}) async-start(bf16[8,128,256]{2,1,0:T(8,128)(2,1)} %shard_map.113), calls=%async_computation.1 | async-start | bytes 1048576 | tf_op jit(solution)/shard_map/all_to_all | solution.py:197
  105.2 8.4 %copy-start.3 = (bf16[128,512]{1,0:T(8,128)(2,1)S(1)}, bf16[128,512]{1,0:T(8,128)(2,1)}, u32[]{:S(2)}) copy-start(bf16[128,512]{1,0:T(8,128)(2,1)} %refs_4_.3) | copy-start | bytes 393220
  105.2 8.4 %copy-start.4 = (bf16[128,512]{1,0:T(8,128)(2,1)S(1)}, bf16[128,512]{1,0:T(8,128)(2,1)}, u32[]{:S(2)}) copy-start(bf16[128,512]{1,0:T(8,128)(2,1)} %refs_3_.3) | copy-start | bytes 393220
  105.2 8.4 %collective-permute-start.11 = (bf16[128,512]{1,0:T(8,128)(2,1)S(1)}, bf16[128,512]{1,0:T(8,128)(2,1)S(1)}, u32[]{:S(2)}, u32[]{:S(2)}) collective-permute-start(bf16[128,512]{1,0:T(8,128)(2,1)S(1)} %get-tuple-element.28.refs_1_.refs_0_), channel_id=1, source_target_pairs={{16,0},{32,16},{48,32},{64,48},{80,64},{96,80},{112,96},{128,112},... | collective-permute-start | bytes 393224 | tf_op jit(solution)/shard_map/ppermute | solution.py:180
  116.9 27.9 %all-to-all-start.2 = ((bf16[32,32,128]{2,1,0:T(8,128)(2,1)}), bf16[32,32,128]{2,1,0:T(8,128)(2,1)S(1)}, u32[]{:S(2)}, u32[]{:S(2)}) async-start(bf16[32,32,128]{2,1,0:T(8,128)(2,1)} %shard_map.117), calls=%async_computation.2 | async-start | bytes 524288 | tf_op jit(solution)/shard_map/all_to_all | solution.py:277
  131.5 10.3 %collective-permute-start.10 = (bf16[128,256]{1,0:T(8,128)(2,1)S(1)}, bf16[128,256]{1,0:T(8,128)(2,1)S(1)}, u32[]{:S(2)}, u32[]{:S(2)}) collective-permute-start(bf16[128,256]{1,0:T(8,128)(2,1)S(1)} %reduce_sum.21), channel_id=1, source_target_pairs={{0,0},{1,1},{2,2},{3,3},{4,128},{5,129},{6,130},{7,131},{8,256},{9... | collective-permute-start | bytes 196616 | tf_op jit(solution)/shard_map/ppermute | solution.py:207
  (14 other events, 18.7 us)
Sparse Core Ops, SparseCore 0:
  12.8 45.8 all-gather.2
  75.6 42.0 reduce-scatter.1

commit v4 on v1

--- a/solution.py
+++ b/solution.py
@@ -1,5 +1,3 @@
-import functools
-
 import jax
 import jax.numpy as jnp
 from jax import lax
@@ -89,13 +87,13 @@
     mixed_ref[...] = (q_ref[...].astype(F32) * conv_ref[...]).astype(BF16)
 
 
-def spread_body(piece_ref, out_ref):
-    for i in range(8):
-        out_ref[i] = piece_ref[...]
+def spread_body(block_ref, out_ref):
+    for i in range(out_ref.shape[0]):
+        out_ref[i] = block_ref[...]
 
 
 def grad_mixed_body(at_ref, own_ref, pair_ref, w_ref, cot_ref, out_ref):
-    core = at_ref[1]
+    core = at_ref[0]
     for i in range(8):
         cot_ref[2 * i + core] = own_ref[i]
         cot_ref[2 * i + 1 - core] = pair_ref[i]
@@ -105,14 +103,14 @@
         out_ref[y] = lax.dot_general(lhs, w, NT, preferred_element_type=F32).astype(BF16)
 
 
-def projected_body(at_ref, m0_ref, m1_ref, m2_ref, m3_ref, w_ref, keep_ref, give_ref, total):
-    y, core = at_ref[0], at_ref[1]
-    mixed = jnp.concatenate([m[...] for m in (m0_ref, m1_ref, m2_ref, m3_ref)], 0)
+def projected_body(at_ref, mixed_ref, w_ref, keep_ref, give_ref, total):
+    core = at_ref[0]
+    mixed = jnp.concatenate([mixed_ref[y] for y in range(YS)], 0)
     for k in range(4):
         w = jnp.concatenate([w_ref[2 * k], w_ref[2 * k + 1]], 1)
         r = lax.dot_general(mixed, w, NN, preferred_element_type=F32)
-        for d in range(YS):
-            total[4 * lax.rem(y + YS - d, YS) + k] = r[d * 128 : d * 128 + 128]
+        for y in range(YS):
+            total[4 * y + k] = r[y * 128 : y * 128 + 128]
     for i in range(8):
         keep_ref[i] = total[2 * i + core]
         give_ref[i] = total[2 * i + 1 - core].astype(BF16)
@@ -129,10 +127,10 @@
         out_ref[i] = taps
 
 
-def grad_w_body(at_ref, m0_ref, m1_ref, m2_ref, m3_ref, cot_ref, out_ref):
-    mixed = jnp.concatenate([m[...] for m in (m0_ref, m1_ref, m2_ref, m3_ref)], 0)
+def grad_w_body(mixed_ref, cot_ref, out_ref):
+    mixed = jnp.concatenate([mixed_ref[y] for y in range(YS)], 0)
     for k in range(4):
-        cot = jnp.concatenate([cot_ref[4 * lax.rem(at_ref[0] + YS - d, YS) + k] for d in range(YS)], 0)
+        cot = jnp.concatenate([cot_ref[4 * y + k] for y in range(YS)], 0)
         r = lax.dot_general(mixed, cot, TN, preferred_element_type=F32).astype(BF16)
         out_ref[2 * k] = r[:, :128]
         out_ref[2 * k + 1] = r[:, 128:]
@@ -184,13 +182,6 @@
     )
 
 
-def shift_y(block, distance):
-    route = [
-        (y * ZS + z, (y + distance) % YS * ZS + z) for y in range(YS) for z in range(ZS)
-    ]
-    return lax.ppermute(block, "row", route)
-
-
 def other_core(block):
     return lax.ppermute(block, "col", [(i, i ^ 1) for i in range(COLS)])
 
@@ -210,7 +201,7 @@
 
 
 def local(q_proj, k_proj, v_proj, filters, w_out, cotangent):
-    at = jnp.stack([lax.axis_index("row") // ZS, lax.axis_index("col") % 2]).astype(jnp.int32)
+    at = (lax.axis_index("col") % 2).astype(jnp.int32).reshape(1)
     tile = shaped((128, 512), BF16)
     w8 = lax.all_gather(w_out, "row", axis_index_groups=Z_GROUPS)
     product = (k_proj.astype(F32) * v_proj.astype(F32)).astype(BF16)
@@ -228,7 +219,8 @@
     own8 = call(spread_body, shaped((8, 128, 256), BF16), (piece,), after=(mixed,))
     own8 = exchange(own8, "col", CHIP_GROUPS)
     pair8 = other_core(own8)
-    mixed4 = [mixed] + [shift_y(mixed, d) for d in (1, 2, 3)]
+    mixed4 = call(spread_body, shaped((YS, 128, 512), BF16), (mixed,), after=(own8,))
+    mixed4 = exchange(mixed4, "row", Y_GROUPS)
 
     cot16, shares = call(
         grad_mixed_body,
@@ -241,15 +233,14 @@
     gw8 = call(
         grad_w_body,
         shaped((ZS, 512, 128), BF16),
-        (*mixed4, cot16),
+        (mixed4, cot16),
         flops=2 * 512 * 512 * 1024,
-        position=at,
         after=(shares,),
     )
     keep, give = call(
         projected_body,
         [shaped((8, 128, 256), F32), shaped((8, 128, 256), BF16)],
-        (*mixed4, w8),
+        (mixed4, w8),
         [pltpu.VMEM((COLS, 128, 256), F32)],
         flops=2 * 512 * 512 * 1024,
         position=at,
@@ -274,7 +265,7 @@
     )
 
     got = exchange(pieces, "col", CHIP_GROUPS)
-    grad_taps = call(taps_body, shaped((YS * ZS, 32, 128), BF16), (grad_taps,), after=(got, grad_k))
+    grad_taps = call(taps_body, shaped((YS * ZS, 32, 128), BF16), (grad_taps,), after=(got,))
     grad_taps = jnp.sum(lax.all_to_all(grad_taps, "row", 0, 0, tiled=True).astype(F32), 0)
     grad_filters = jnp.flip(grad_taps, 1).T
 

time: 144 us -> 132 us (0.917)
  the two profiles are of different devices: /device:TPU:22 before, /device:TPU:48 now
where the time goes in v4:
time: 132 us; the launch traced here: 131 us
  starting transfers between devices  46.5 us (35%)
  waiting for transfers between devices  36.5 us (28%)
  between operations  14.3 us (11%)
  blocking collectives  14.2 us (11%)
  Pallas kernels  13 us (10%)
  local copies, waits for them, and re-layouts  3.67 us (3%)
  other arithmetic  2.86 us (2%)
    all_to_all x3, starting transfers between devices, exchange(): lax.all_to_all(blocks, axis, 0, 0, axis_index_groups=groups, tiled=True)  17.5 us
    all_to_all x1, blocking collectives, exchange(): lax.all_to_all(blocks, axis, 0, 0, axis_index_groups=groups, tiled=True)  14.2 us
    pallas_call x11, Pallas kernels, call(): pl.pallas_call(run, out_shape=out_shape, in_specs=specs, scratch_shapes=l...  13 us
    all_to_all x3, waiting for transfers between devices, exchange(): lax.all_to_all(blocks, axis, 0, 0, axis_index_groups=groups, tiled=True)  12.4 us
    ppermute x2, starting transfers between devices, shift_row(): lax.ppermute(block, 'row', [(i, i + distance) for i in range(n) if 0 <= i...  10.9 us
    ppermute x2, waiting for transfers between devices, shift_row(): lax.ppermute(block, 'row', [(i, i + distance) for i in range(n) if 0 <= i...  10.8 us
    ppermute x2, starting transfers between devices, swap_pieces(): return lax.ppermute(piece, ('row', 'col'), route)  7.19 us
    all_to_all x1, starting transfers between devices, local(): lax.all_to_all(grad_taps, 'row', 0, 0, tiled=True).astype(F32)  7.05 us
  transfers between devices with their start and end apart: 12, of which 9 were waited for; matrix products, arithmetic and copies ran while one was open for 1% of the time, Pallas kernels for 9%

profile of v4, /device:TPU:48, one launch (start us, length us, event | category | flops | bytes accessed | tf_op | source)
XLA Modules:
  0.0 131.0 jit_solution(9544942402887606950)
XLA Ops:
  8.3 4.4 %collective-permute-start = (bf16[128,512]{1,0:T(8,128)(2,1)S(1)}, bf16[128,512]{1,0:T(8,128)(2,1)S(1)}, u32[]{:S(2)}, u32[]{:S(2)}) collective-permute-start(bf16[128,512]{1,0:T(8,128)(2,1)S(1)} %multiply_convert_fusion.refs_1_), channel_id=1, source_target_pairs={{0,16},{16,32},{32,48},{48,64},{64,80},{80,96},{96,112},{112,128},... | collective-permute-start | bytes 393224 | tf_op jit(solution)/shard_map/ppermute | solution.py:180
  12.7 5.3 %collective-permute-start.1 = (bf16[128,256]{1,0:T(8,128)(2,1)S(1)}, bf16[128,256]{1,0:T(8,128)(2,1)S(1)}, u32[]{:S(2)}, u32[]{:S(2)}) collective-permute-start(bf16[128,256]{1,0:T(8,128)(2,1)S(1)} %copy-done.11), channel_id=1, source_target_pairs={{0,0},{1,1},{2,2},{3,3},{4,128},{5,129},{6,130},{7,131},{8,256},{9... | collective-permute-start | bytes 196616 | tf_op jit(solution)/shard_map/ppermute | solution.py:200
  18.2 9.0 %collective-permute-done.refs_2_ = bf16[128,512]{1,0:T(8,128)(2,1)S(1)} collective-permute-done((bf16[128,512]{1,0:T(8,128)(2,1)S(1)}, bf16[128,512]{1,0:T(8,128)(2,1)S(1)}, u32[]{:S(2)}, u32[]{:S(2)}) %collective-permute-start) | collective-permute-done | bytes 131104 | tf_op jit(solution)/shard_map/ppermute | solution.py:180
  27.2 1.6 %shard_map.109 = (f32[128,512]{1,0:T(8,128)S(1)}, bf16[128,512]{1,0:T(8,128)(2,1)S(1)}) custom-call(f32[32,128]{1,0:T(8,128)S(1)} %pad_maximum_fusion.refs_0_, bf16[128,512]{1,0:T(8,128)(2,1)S(1)} %multiply_convert_fusion.refs_1_, bf16[128,512]{1,0:T(8,128)(2,1)S(1)} %collective-permute-done.refs_2_, bf16[128,512]{1,0:T(8,128)(2,1)S(1)} %copy-done.6), custom_call_target="tpu_custom_call" | custom-call | flops 2147483648 | bytes 802816 | tf_op jit(solution)/shard_map/pallas_call | solution.py:36
  28.9 14.2 %all_to_all.25.refs_1_ = bf16[8,128,256]{2,1,0:T(8,128)(2,1)S(1)} all-to-all(bf16[8,128,256]{2,1,0:T(8,128)(2,1)S(1)} %shard_map.110), channel_id=1, replica_groups={{0,2,4,6,8,10,12,14},{1,3,5,7,9,11,13,15},{16,18,20,22,24,26,28,30},{17..., dimensions={0} | all-to-all | bytes 1048576 | tf_op jit(solution)/shard_map/all_to_all | solution.py:190
  44.0 6.2 %all-to-all-start.1 = ((bf16[4,128,512]{2,1,0:T(8,128)(2,1)}), bf16[4,128,512]{2,1,0:T(8,128)(2,1)S(1)}, u32[]{:S(2)}, u32[]{:S(2)}) async-start(bf16[4,128,512]{2,1,0:T(8,128)(2,1)} %shard_map.111), calls=%async_computation.1 | async-start | bytes 1048576 | tf_op jit(solution)/shard_map/all_to_all | solution.py:190
  50.2 1.9 %collective-permute-start.2 = (bf16[8,128,256]{2,1,0:T(8,128)(2,1)S(1)}, bf16[8,128,256]{2,1,0:T(8,128)(2,1)S(1)}, u32[]{:S(2)}, u32[]{:S(2)}) collective-permute-start(bf16[8,128,256]{2,1,0:T(8,128)(2,1)S(1)} %all_to_all.25.refs_1_), channel_id=1, source_target_pairs={{0,1},{1,0},{2,3},{3,2},{4,5},{5,4},{6,7},{7,6},{8,9},{9,8},{10,11... | collective-permute-start | bytes 1572872 | tf_op jit(solution)/shard_map/ppermute | solution.py:186
  52.2 1.9 %collective-permute-done.2.refs_2_ = bf16[8,128,256]{2,1,0:T(8,128)(2,1)S(1)} collective-permute-done((bf16[8,128,256]{2,1,0:T(8,128)(2,1)S(1)}, bf16[8,128,256]{2,1,0:T(8,128)(2,1)S(1)}, u32[]{:S(2)}, u32[]{:S(2)}) %collective-permute-start.2) | collective-permute-done | bytes 524320 | tf_op jit(solution)/shard_map/ppermute | solution.py:186
  54.0 4.2 %all-gather.3.cloned.1.call-done = bf16[4096,128]{1,0:T(8,128)(2,1)} async-done(((bf16[512,128]{1,0:T(8,128)(2,1)}), bf16[4096,128]{1,0:T(8,128)(2,1)}) %all-gather.3.cloned.1.call-update) | async-done | bytes 1048592 | tf_op jit(solution)/shard_map/all_gather | solution.py:206
  59.5 2.3 %shard_map.112 = (bf16[16,128,256]{2,1,0:T(8,128)(2,1)S(1)}, bf16[4,128,512]{2,1,0:T(8,128)(2,1)}) custom-call(s32[1]{0:T(128)} %bitcast.refs_0_, bf16[8,128,256]{2,1,0:T(8,128)(2,1)S(1)} %all_to_all.25.refs_1_, bf16[8,128,256]{2,1,0:T(8,128)(2,1)S(1)} %collective-permute-done.2.refs_2_, bf16[8,512,128]{2,1,0:T(8,128)(2,1)S(1)} %bitcast.8), custom_call_target="tpu_custom_call" | custom-call | flops 536870912 | bytes 3670016 | tf_op jit(solution)/shard_map/pallas_call | solution.py:36
  62.2 1.8 %shard_map.113.refs_3_ = bf16[8,512,128]{2,1,0:T(8,128)(2,1)} custom-call(bf16[4,128,512]{2,1,0:T(8,128)(2,1)S(1)} %all-to-all-done.1.refs_0_.refs_1_, bf16[16,128,256]{2,1,0:T(8,128)(2,1)S(1)} %get-tuple-element.17.refs_1_, bf16[4,128,512]{2,1,0:T(8,128)(2,1)} %get-tuple-element.18.refs_2_), custom_call_target="tpu_custom_call" | custom-call | flops 536870912 | bytes 2621440 | tf_op jit(solution)/shard_map/pallas_call | solution.py:36
  63.9 6.7 %all-to-all-start.2 = ((bf16[4,128,512]{2,1,0:T(8,128)(2,1)}), bf16[4,128,512]{2,1,0:T(8,128)(2,1)S(1)}, u32[]{:S(2)}, u32[]{:S(2)}) async-start(bf16[4,128,512]{2,1,0:T(8,128)(2,1)} %get-tuple-element.18.refs_2_), calls=%async_computation.2 | async-start | bytes 1048576 | tf_op jit(solution)/shard_map/all_to_all | solution.py:190
  71.5 1.9 %collective-permute-start.3 = (bf16[8,128,256]{2,1,0:T(8,128)(2,1)S(1)}, bf16[8,128,256]{2,1,0:T(8,128)(2,1)S(1)}, u32[]{:S(2)}, u32[]{:S(2)}) collective-permute-start(bf16[8,128,256]{2,1,0:T(8,128)(2,1)S(1)} %get-tuple-element.20.refs_3_), channel_id=1, source_target_pairs={{0,1},{1,0},{2,3},{3,2},{4,5},{5,4},{6,7},{7,6},{8,9},{9,8},{10,11... | collective-permute-start | bytes 1572872 | tf_op jit(solution)/shard_map/ppermute | solution.py:186
  75.3 6.2 %all-to-all-done.2.refs_2_.refs_0_ = bf16[4,128,512]{2,1,0:T(8,128)(2,1)S(1)} async-done(((bf16[4,128,512]{2,1,0:T(8,128)(2,1)}), bf16[4,128,512]{2,1,0:T(8,128)(2,1)S(1)}, u32[]{:S(2)}, u32[]{:S(2)}) %all-to-all-start.2) | async-done | bytes 524320 | tf_op jit(solution)/shard_map/all_to_all | solution.py:190
  82.4 4.5 %all-to-all-start.3 = ((bf16[8,128,256]{2,1,0:T(8,128)(2,1)}), bf16[8,128,256]{2,1,0:T(8,128)(2,1)S(1)}, u32[]{:S(2)}, u32[]{:S(2)}) async-start(bf16[8,128,256]{2,1,0:T(8,128)(2,1)} %shard_map.115), calls=%async_computation.3 | async-start | bytes 1048576 | tf_op jit(solution)/shard_map/all_to_all | solution.py:190
  87.9 1.6 %shard_map.118.refs_0_ = f32[32,128]{1,0:T(8,128)S(1)} custom-call(bf16[128,512]{1,0:T(8,128)(2,1)S(1)} %get-tuple-element.23.refs_1_.refs_0_, bf16[128,512]{1,0:T(8,128)(2,1)S(1)} %multiply_convert_fusion.refs_1_, bf16[128,512]{1,0:T(8,128)(2,1)S(1)} %copy-done.10), custom_call_target="tpu_custom_call" | custom-call | flops 268435456 | bytes 409600 | tf_op jit(solution)/shard_map/pallas_call | solution.py:36
  89.5 5.8 %all-to-all-done.3.refs_1_ = bf16[8,128,256]{2,1,0:T(8,128)(2,1)S(1)} async-done(((bf16[8,128,256]{2,1,0:T(8,128)(2,1)}), bf16[8,128,256]{2,1,0:T(8,128)(2,1)S(1)}, u32[]{:S(2)}, u32[]{:S(2)}) %all-to-all-start.3) | async-done | bytes 524320 | tf_op jit(solution)/shard_map/all_to_all | solution.py:190
  96.0 7.0 %all-to-all-start.4 = ((bf16[32,32,128]{2,1,0:T(8,128)(2,1)}), bf16[32,32,128]{2,1,0:T(8,128)(2,1)S(1)}, u32[]{:S(2)}, u32[]{:S(2)}) async-start(bf16[32,32,128]{2,1,0:T(8,128)(2,1)} %shard_map.119), calls=%async_computation.4 | async-start | bytes 524288 | tf_op jit(solution)/shard_map/all_to_all | solution.py:269
  103.0 6.5 %collective-permute-start.5 = (bf16[128,512]{1,0:T(8,128)(2,1)S(1)}, bf16[128,512]{1,0:T(8,128)(2,1)S(1)}, u32[]{:S(2)}, u32[]{:S(2)}) collective-permute-start(bf16[128,512]{1,0:T(8,128)(2,1)S(1)} %get-tuple-element.23.refs_1_.refs_0_), channel_id=1, source_target_pairs={{16,0},{32,16},{48,32},{64,48},{80,64},{96,80},{112,96},{128,112},... | collective-permute-start | bytes 393224 | tf_op jit(solution)/shard_map/ppermute | solution.py:180
  109.6 1.9 %collective-permute-start.4 = (bf16[128,256]{1,0:T(8,128)(2,1)S(1)}, bf16[128,256]{1,0:T(8,128)(2,1)S(1)}, u32[]{:S(2)}, u32[]{:S(2)}) collective-permute-start(bf16[128,256]{1,0:T(8,128)(2,1)S(1)} %reduce_sum.21), channel_id=1, source_target_pairs={{0,0},{1,1},{2,2},{3,3},{4,128},{5,129},{6,130},{7,131},{8,256},{9... | collective-permute-start | bytes 196616 | tf_op jit(solution)/shard_map/ppermute | solution.py:200
  111.6 1.9 %collective-permute-done.5.refs_2_ = bf16[128,512]{1,0:T(8,128)(2,1)S(1)} collective-permute-done((bf16[128,512]{1,0:T(8,128)(2,1)S(1)}, bf16[128,512]{1,0:T(8,128)(2,1)S(1)}, u32[]{:S(2)}, u32[]{:S(2)}) %collective-permute-start.5) | collective-permute-done | bytes 131104 | tf_op jit(solution)/shard_map/ppermute | solution.py:180
  113.4 1.7 %shard_map.117 = (bf16[128,512]{1,0:T(8,128)(2,1)}, bf16[128,512]{1,0:T(8,128)(2,1)}) custom-call(f32[32,128]{1,0:T(8,128)S(1)} %bitcast.12, bf16[128,512]{1,0:T(8,128)(2,1)S(1)} %get-tuple-element.23.refs_1_.refs_0_, bf16[128,512]{1,0:T(8,128)(2,1)S(1)} %collective-permute-done.5.refs_2_, bf16[128,512]{1,0:T(8,128)(2,1)S(1)} %copy-done.5, ...), custom_call_target="tpu_custom_call" | custom-call | flops 1073741824 | bytes 802816 | tf_op jit(solution)/shard_map/pallas_call | solution.py:36
  115.1 6.1 %collective-permute-done.4 = bf16[128,256]{1,0:T(8,128)(2,1)S(1)} collective-permute-done((bf16[128,256]{1,0:T(8,128)(2,1)S(1)}, bf16[128,256]{1,0:T(8,128)(2,1)S(1)}, u32[]{:S(2)}, u32[]{:S(2)}) %collective-permute-start.4) | collective-permute-done | bytes 65568 | tf_op jit(solution)/shard_map/ppermute | solution.py:200
  121.2 1.6 %bitcast_convert_fusion = f32[512,128]{1,0:T(8,128)} fusion(bf16[1,512,128]{2,1,0:T(8,128)(2,1)} %reduce-scatter.2.cloned.1.call-done), kind=kLoop, calls=%fused_computation.2 | loop fusion | flops 65536 | bytes 393216 | tf_op jit(solution)/shard_map/convert_element_type | solution.py:273
  (47 shorter events, 10.5 us)
Async XLA Ops:
  7.2 51.1 %all-gather.3.cloned.1.call-start = ((), (), s32[]{:S(2)}) async-start(), calls=%async_computation.7 | async-start | bytes 1179648 | tf_op jit(solution)/shard_map/all_gather | solution.py:206
  7.2 5.5 %copy-start.11 = (bf16[128,256]{1,0:T(8,128)(2,1)S(1)}, bf16[128,256]{1,0:T(8,128)(2,1)}, u32[]{:S(2)}) copy-start(bf16[128,256]{1,0:T(8,128)(2,1)} %param.11) | copy-start | bytes 196612
  7.2 10.8 %copy-start.8 = (f32[128,32]{0,1:T(8,128)S(1)}, f32[128,32]{0,1:T(8,128)}, u32[]{:S(2)}) copy-start(f32[128,32]{0,1:T(8,128)} %param.9) | copy-start | bytes 49156
  8.3 19.0 %copy-start.6 = (bf16[128,512]{1,0:T(8,128)(2,1)S(1)}, bf16[128,512]{1,0:T(8,128)(2,1)}, u32[]{:S(2)}) copy-start(bf16[128,512]{1,0:T(8,128)(2,1)} %refs_1_.1) | copy-start | bytes 393220
  8.3 18.9 %collective-permute-start = (bf16[128,512]{1,0:T(8,128)(2,1)S(1)}, bf16[128,512]{1,0:T(8,128)(2,1)S(1)}, u32[]{:S(2)}, u32[]{:S(2)}) collective-permute-start(bf16[128,512]{1,0:T(8,128)(2,1)S(1)} %multiply_convert_fusion.refs_1_), channel_id=1, source_target_pairs={{0,16},{16,32},{32,48},{48,64},{64,80},{80,96},{96,112},{112,128},... | collective-permute-start | bytes 393224 | tf_op jit(solution)/shard_map/ppermute | solution.py:180
  12.7 16.1 %collective-permute-start.1 = (bf16[128,256]{1,0:T(8,128)(2,1)S(1)}, bf16[128,256]{1,0:T(8,128)(2,1)S(1)}, u32[]{:S(2)}, u32[]{:S(2)}) collective-permute-start(bf16[128,256]{1,0:T(8,128)(2,1)S(1)} %copy-done.11), channel_id=1, source_target_pairs={{0,0},{1,1},{2,2},{3,3},{4,128},{5,129},{6,130},{7,131},{8,256},{9... | collective-permute-start | bytes 196616 | tf_op jit(solution)/shard_map/ppermute | solution.py:200
  27.2 1.6 %copy-start.9 = (bf16[128,512]{1,0:T(8,128)(2,1)}, bf16[128,512]{1,0:T(8,128)(2,1)S(1)}, u32[]{:S(2)}) copy-start(bf16[128,512]{1,0:T(8,128)(2,1)S(1)} %collective-permute-done.refs_2_) | copy-start | bytes 393220
  44.0 18.2 %all-to-all-start.1 = ((bf16[4,128,512]{2,1,0:T(8,128)(2,1)}), bf16[4,128,512]{2,1,0:T(8,128)(2,1)S(1)}, u32[]{:S(2)}, u32[]{:S(2)}) async-start(bf16[4,128,512]{2,1,0:T(8,128)(2,1)} %shard_map.111), calls=%async_computation.1 | async-start | bytes 1048576 | tf_op jit(solution)/shard_map/all_to_all | solution.py:190
  50.2 71.0 %reduce-scatter.2.cloned.1.call-start = ((), (), s32[]{:S(2)}) async-start(), calls=%async_computation.6 | async-start | bytes 1179648 | tf_op jit(solution)/shard_map/reduce_scatter | solution.py:273
  50.2 3.8 %collective-permute-start.2 = (bf16[8,128,256]{2,1,0:T(8,128)(2,1)S(1)}, bf16[8,128,256]{2,1,0:T(8,128)(2,1)S(1)}, u32[]{:S(2)}, u32[]{:S(2)}) collective-permute-start(bf16[8,128,256]{2,1,0:T(8,128)(2,1)S(1)} %all_to_all.25.refs_1_), channel_id=1, source_target_pairs={{0,1},{1,0},{2,3},{3,2},{4,5},{5,4},{6,7},{7,6},{8,9},{9,8},{10,11... | collective-permute-start | bytes 1572872 | tf_op jit(solution)/shard_map/ppermute | solution.py:186
  58.2 1.2 copy-start
  63.9 6.7 %copy-start.1 = (bf16[4096,128]{1,0:T(8,128)(2,1)S(1)}, bf16[4096,128]{1,0:T(8,128)(2,1)}, u32[]{:S(2)}) copy-start(bf16[4096,128]{1,0:T(8,128)(2,1)} %all-gather.3.cloned.1.call-done) | copy-start | bytes 3145732
  63.9 17.6 %all-to-all-start.2 = ((bf16[4,128,512]{2,1,0:T(8,128)(2,1)}), bf16[4,128,512]{2,1,0:T(8,128)(2,1)S(1)}, u32[]{:S(2)}, u32[]{:S(2)}) async-start(bf16[4,128,512]{2,1,0:T(8,128)(2,1)} %get-tuple-element.18.refs_2_), calls=%async_computation.2 | async-start | bytes 1048576 | tf_op jit(solution)/shard_map/all_to_all | solution.py:190
  71.5 3.8 %collective-permute-start.3 = (bf16[8,128,256]{2,1,0:T(8,128)(2,1)S(1)}, bf16[8,128,256]{2,1,0:T(8,128)(2,1)S(1)}, u32[]{:S(2)}, u32[]{:S(2)}) collective-permute-start(bf16[8,128,256]{2,1,0:T(8,128)(2,1)S(1)} %get-tuple-element.20.refs_3_), channel_id=1, source_target_pairs={{0,1},{1,0},{2,3},{3,2},{4,5},{5,4},{6,7},{7,6},{8,9},{9,8},{10,11... | collective-permute-start | bytes 1572872 | tf_op jit(solution)/shard_map/ppermute | solution.py:186
  73.4 0.8 copy-start.2
  82.4 4.6 %copy-start.3 = (bf16[8,128,256]{2,1,0:T(8,128)(2,1)S(1)}, bf16[8,128,256]{2,1,0:T(8,128)(2,1)}, u32[]{:S(2)}) copy-start(bf16[8,128,256]{2,1,0:T(8,128)(2,1)} %copy-done.2) | copy-start | bytes 1572868
  82.4 4.6 %copy-start.7 = (bf16[128,512]{1,0:T(8,128)(2,1)S(1)}, bf16[128,512]{1,0:T(8,128)(2,1)}, u32[]{:S(2)}) copy-start(bf16[128,512]{1,0:T(8,128)(2,1)} %refs_1_.1) | copy-start | bytes 393220
  82.4 12.8 %all-to-all-start.3 = ((bf16[8,128,256]{2,1,0:T(8,128)(2,1)}), bf16[8,128,256]{2,1,0:T(8,128)(2,1)S(1)}, u32[]{:S(2)}, u32[]{:S(2)}) async-start(bf16[8,128,256]{2,1,0:T(8,128)(2,1)} %shard_map.115), calls=%async_computation.3 | async-start | bytes 1048576 | tf_op jit(solution)/shard_map/all_to_all | solution.py:190
  87.0 0.9 copy-start.10
  96.0 26.9 %all-to-all-start.4 = ((bf16[32,32,128]{2,1,0:T(8,128)(2,1)}), bf16[32,32,128]{2,1,0:T(8,128)(2,1)S(1)}, u32[]{:S(2)}, u32[]{:S(2)}) async-start(bf16[32,32,128]{2,1,0:T(8,128)(2,1)} %shard_map.119), calls=%async_computation.4 | async-start | bytes 524288 | tf_op jit(solution)/shard_map/all_to_all | solution.py:269
  103.0 10.4 %copy-start.4 = (bf16[128,512]{1,0:T(8,128)(2,1)S(1)}, bf16[128,512]{1,0:T(8,128)(2,1)}, u32[]{:S(2)}) copy-start(bf16[128,512]{1,0:T(8,128)(2,1)} %refs_4_.1) | copy-start | bytes 393220
  103.0 10.4 %copy-start.5 = (bf16[128,512]{1,0:T(8,128)(2,1)S(1)}, bf16[128,512]{1,0:T(8,128)(2,1)}, u32[]{:S(2)}) copy-start(bf16[128,512]{1,0:T(8,128)(2,1)} %refs_3_.3) | copy-start | bytes 393220
  103.0 10.4 %collective-permute-start.5 = (bf16[128,512]{1,0:T(8,128)(2,1)S(1)}, bf16[128,512]{1,0:T(8,128)(2,1)S(1)}, u32[]{:S(2)}, u32[]{:S(2)}) collective-permute-start(bf16[128,512]{1,0:T(8,128)(2,1)S(1)} %get-tuple-element.23.refs_1_.refs_0_), channel_id=1, source_target_pairs={{16,0},{32,16},{48,32},{64,48},{80,64},{96,80},{112,96},{128,112},... | collective-permute-start | bytes 393224 | tf_op jit(solution)/shard_map/ppermute | solution.py:180
  109.6 11.6 %collective-permute-start.4 = (bf16[128,256]{1,0:T(8,128)(2,1)S(1)}, bf16[128,256]{1,0:T(8,128)(2,1)S(1)}, u32[]{:S(2)}, u32[]{:S(2)}) collective-permute-start(bf16[128,256]{1,0:T(8,128)(2,1)S(1)} %reduce_sum.21), channel_id=1, source_target_pairs={{0,0},{1,1},{2,2},{3,3},{4,128},{5,129},{6,130},{7,131},{8,256},{9... | collective-permute-start | bytes 196616 | tf_op jit(solution)/shard_map/ppermute | solution.py:200
Sparse Core Ops, SparseCore 0:
  12.8 45.3 all-gather.2
  64.1 40.0 reduce-scatter.1

commit v5 on v4

--- a/solution.py
+++ b/solution.py
@@ -84,7 +84,9 @@
 def conv_body(rows_ref, product_ref, halo_ref, q_ref, conv_ref, mixed_ref, stack):
     row, lane = iotas(128, 128)
     apply_filters(rows_ref, lane <= row, product_ref, halo_ref, stack, conv_ref, True)
-    mixed_ref[...] = (q_ref[...].astype(F32) * conv_ref[...]).astype(BF16)
+    mixed = (q_ref[...].astype(F32) * conv_ref[...]).astype(BF16)
+    for y in range(YS):
+        mixed_ref[y] = mixed
 
 
 def spread_body(block_ref, out_ref):
@@ -209,18 +211,17 @@
     piece = swap_pieces(cotangent)
     taps = filters.T
     forward_rows = jnp.roll(jnp.flip(taps, 1), 1, axis=1)
-    conv, mixed = call(
+    conv, mixed4 = call(
         conv_body,
-        [shaped((128, 512), F32), tile],
+        [shaped((128, 512), F32), shaped((YS, 128, 512), BF16)],
         (forward_rows, product, halo, q_proj),
         [pltpu.VMEM((1024, 512), BF16)],
         flops=2 * 4096 * 512 * 128 * 4,
     )
-    own8 = call(spread_body, shaped((8, 128, 256), BF16), (piece,), after=(mixed,))
+    mixed4 = exchange(mixed4, "row", Y_GROUPS)
+    own8 = call(spread_body, shaped((8, 128, 256), BF16), (piece,), after=(mixed4,))
     own8 = exchange(own8, "col", CHIP_GROUPS)
     pair8 = other_core(own8)
-    mixed4 = call(spread_body, shaped((YS, 128, 512), BF16), (mixed,), after=(own8,))
-    mixed4 = exchange(mixed4, "row", Y_GROUPS)
 
     cot16, shares = call(
         grad_mixed_body,
@@ -265,7 +266,7 @@
     )
 
     got = exchange(pieces, "col", CHIP_GROUPS)
-    grad_taps = call(taps_body, shaped((YS * ZS, 32, 128), BF16), (grad_taps,), after=(got,))
+    grad_taps = call(taps_body, shaped((YS * ZS, 32, 128), BF16), (grad_taps,), after=(got, later))
     grad_taps = jnp.sum(lax.all_to_all(grad_taps, "row", 0, 0, tiled=True).astype(F32), 0)
     grad_filters = jnp.flip(grad_taps, 1).T
 

time: 132 us -> 147 us (1.11)
  the two profiles are of different devices: /device:TPU:48 before, /device:TPU:4 now
where the time goes in v5:
time: 147 us; the launch traced here: 146 us
  starting transfers between devices  55.5 us (38%)
  waiting for transfers between devices  45.4 us (31%)
  between operations  14.2 us (10%)
  Pallas kernels  12.9 us (9%)
  blocking collectives  11.4 us (8%)
  local copies, waits for them, and re-layouts  3.58 us (2%)
  other arithmetic  2.86 us (2%)
    all_to_all x3, starting transfers between devices, exchange(): lax.all_to_all(blocks, axis, 0, 0, axis_index_groups=groups, tiled=True)  28.9 us
    ppermute x2, waiting for transfers between devices, swap_pieces(): return lax.ppermute(piece, ('row', 'col'), route)  16.2 us
    pallas_call x10, Pallas kernels, call(): pl.pallas_call(run, out_shape=out_shape, in_specs=specs, scratch_shapes=l...  12.9 us
    all_gather x1, waiting for transfers between devices, local(): w8 = lax.all_gather(w_out, 'row', axis_index_groups=Z_GROUPS)  11.8 us
    all_to_all x1, blocking collectives, exchange(): lax.all_to_all(blocks, axis, 0, 0, axis_index_groups=groups, tiled=True)  11.4 us
    all_to_all x1, starting transfers between devices, local(): lax.all_to_all(grad_taps, 'row', 0, 0, tiled=True).astype(F32)  9.45 us
    all_to_all x3, waiting for transfers between devices, exchange(): lax.all_to_all(blocks, axis, 0, 0, axis_index_groups=groups, tiled=True)  7.74 us
    ppermute x2, starting transfers between devices, swap_pieces(): return lax.ppermute(piece, ('row', 'col'), route)  7.71 us
  transfers between devices with their start and end apart: 12, of which 8 were waited for; matrix products, arithmetic and copies ran while one was open for 1% of the time, Pallas kernels for 4%

profile of v5, /device:TPU:4, one launch (start us, length us, event | category | flops | bytes accessed | tf_op | source)
XLA Modules:
  0.0 145.9 jit_solution(12518005393452254276)
XLA Ops:
  8.2 4.3 %collective-permute-start = (bf16[128,512]{1,0:T(8,128)(2,1)S(1)}, bf16[128,512]{1,0:T(8,128)(2,1)S(1)}, u32[]{:S(2)}, u32[]{:S(2)}) collective-permute-start(bf16[128,512]{1,0:T(8,128)(2,1)S(1)} %multiply_convert_fusion.refs_1_), channel_id=1, source_target_pairs={{0,16},{16,32},{32,48},{48,64},{64,80},{80,96},{96,112},{112,128},... | collective-permute-start | bytes 393224 | tf_op jit(solution)/shard_map/ppermute | solution.py:182
  12.8 2.5 %collective-permute-done.refs_2_ = bf16[128,512]{1,0:T(8,128)(2,1)S(1)} collective-permute-done((bf16[128,512]{1,0:T(8,128)(2,1)S(1)}, bf16[128,512]{1,0:T(8,128)(2,1)S(1)}, u32[]{:S(2)}, u32[]{:S(2)}) %collective-permute-start) | collective-permute-done | bytes 131104 | tf_op jit(solution)/shard_map/ppermute | solution.py:182
  15.3 2.5 %shard_map.109 = (f32[128,512]{1,0:T(8,128)S(1)}, bf16[4,128,512]{2,1,0:T(8,128)(2,1)}) custom-call(f32[32,128]{1,0:T(8,128)S(1)} %pad_maximum_fusion.refs_0_, bf16[128,512]{1,0:T(8,128)(2,1)S(1)} %multiply_convert_fusion.refs_1_, bf16[128,512]{1,0:T(8,128)(2,1)S(1)} %collective-permute-done.refs_2_, bf16[128,512]{1,0:T(8,128)(2,1)S(1)} %copy-done.6), custom_call_target="tpu_custom_call" | custom-call | flops 2147483648 | bytes 1196032 | tf_op jit(solution)/shard_map/pallas_call | solution.py:36
  17.7 17.3 %all-to-all-start = ((bf16[4,128,512]{2,1,0:T(8,128)(2,1)}), bf16[4,128,512]{2,1,0:T(8,128)(2,1)S(1)}, u32[]{:S(2)}, u32[]{:S(2)}) async-start(bf16[4,128,512]{2,1,0:T(8,128)(2,1)} %get-tuple-element.16), calls=%async_computation | async-start | bytes 1048576 | tf_op jit(solution)/shard_map/all_to_all | solution.py:192
  35.9 4.8 %collective-permute-start.1 = (bf16[128,256]{1,0:T(8,128)(2,1)S(1)}, bf16[128,256]{1,0:T(8,128)(2,1)S(1)}, u32[]{:S(2)}, u32[]{:S(2)}) collective-permute-start(bf16[128,256]{1,0:T(8,128)(2,1)S(1)} %copy-done.11), channel_id=1, source_target_pairs={{0,0},{1,1},{2,2},{3,3},{4,128},{5,129},{6,130},{7,131},{8,256},{9... | collective-permute-start | bytes 196616 | tf_op jit(solution)/shard_map/ppermute | solution.py:202
  40.6 10.8 %collective-permute-done.1.refs_0_ = bf16[128,256]{1,0:T(8,128)(2,1)S(1)} collective-permute-done((bf16[128,256]{1,0:T(8,128)(2,1)S(1)}, bf16[128,256]{1,0:T(8,128)(2,1)S(1)}, u32[]{:S(2)}, u32[]{:S(2)}) %collective-permute-start.1) | collective-permute-done | bytes 65568 | tf_op jit(solution)/shard_map/ppermute | solution.py:202
  51.4 11.4 %all_to_all.25.refs_1_ = bf16[8,128,256]{2,1,0:T(8,128)(2,1)S(1)} all-to-all(bf16[8,128,256]{2,1,0:T(8,128)(2,1)S(1)} %shard_map.110), channel_id=1, replica_groups={{0,2,4,6,8,10,12,14},{1,3,5,7,9,11,13,15},{16,18,20,22,24,26,28,30},{17..., dimensions={0} | all-to-all | bytes 1048576 | tf_op jit(solution)/shard_map/all_to_all | solution.py:192
  62.8 1.9 %collective-permute-start.2 = (bf16[8,128,256]{2,1,0:T(8,128)(2,1)S(1)}, bf16[8,128,256]{2,1,0:T(8,128)(2,1)S(1)}, u32[]{:S(2)}, u32[]{:S(2)}) collective-permute-start(bf16[8,128,256]{2,1,0:T(8,128)(2,1)S(1)} %all_to_all.25.refs_1_), channel_id=1, source_target_pairs={{0,1},{1,0},{2,3},{3,2},{4,5},{5,4},{6,7},{7,6},{8,9},{9,8},{10,11... | collective-permute-start | bytes 1572872 | tf_op jit(solution)/shard_map/ppermute | solution.py:188
  64.8 11.8 %all-gather.3.cloned.1.call-done = bf16[4096,128]{1,0:T(8,128)(2,1)} async-done(((bf16[512,128]{1,0:T(8,128)(2,1)}), bf16[4096,128]{1,0:T(8,128)(2,1)}) %all-gather.3.cloned.1.call-update) | async-done | bytes 1048592 | tf_op jit(solution)/shard_map/all_gather | solution.py:208
  76.5 1.2 copy-done
  77.8 2.3 %shard_map.111 = (bf16[16,128,256]{2,1,0:T(8,128)(2,1)S(1)}, bf16[4,128,512]{2,1,0:T(8,128)(2,1)}) custom-call(s32[1]{0:T(128)} %bitcast.refs_0_, bf16[8,128,256]{2,1,0:T(8,128)(2,1)S(1)} %all_to_all.25.refs_1_, bf16[8,128,256]{2,1,0:T(8,128)(2,1)S(1)} %collective-permute-done.2.refs_2_, bf16[8,512,128]{2,1,0:T(8,128)(2,1)S(1)} %bitcast.8), custom_call_target="tpu_custom_call" | custom-call | flops 536870912 | bytes 3670016 | tf_op jit(solution)/shard_map/pallas_call | solution.py:36
  80.0 1.7 %shard_map.112.refs_3_ = bf16[8,512,128]{2,1,0:T(8,128)(2,1)} custom-call(bf16[4,128,512]{2,1,0:T(8,128)(2,1)S(1)} %all-to-all-done.refs_1_.refs_0_, bf16[16,128,256]{2,1,0:T(8,128)(2,1)S(1)} %get-tuple-element.17.refs_1_, bf16[4,128,512]{2,1,0:T(8,128)(2,1)} %get-tuple-element.18.refs_2_), custom_call_target="tpu_custom_call" | custom-call | flops 536870912 | bytes 2621440 | tf_op jit(solution)/shard_map/pallas_call | solution.py:36
  81.8 6.7 %all-to-all-start.2 = ((bf16[4,128,512]{2,1,0:T(8,128)(2,1)}), bf16[4,128,512]{2,1,0:T(8,128)(2,1)S(1)}, u32[]{:S(2)}, u32[]{:S(2)}) async-start(bf16[4,128,512]{2,1,0:T(8,128)(2,1)} %get-tuple-element.18.refs_2_), calls=%async_computation.2 | async-start | bytes 1048576 | tf_op jit(solution)/shard_map/all_to_all | solution.py:192
  89.4 1.9 %collective-permute-start.3 = (bf16[8,128,256]{2,1,0:T(8,128)(2,1)S(1)}, bf16[8,128,256]{2,1,0:T(8,128)(2,1)S(1)}, u32[]{:S(2)}, u32[]{:S(2)}) collective-permute-start(bf16[8,128,256]{2,1,0:T(8,128)(2,1)S(1)} %get-tuple-element.20.refs_3_), channel_id=1, source_target_pairs={{0,1},{1,0},{2,3},{3,2},{4,5},{5,4},{6,7},{7,6},{8,9},{9,8},{10,11... | collective-permute-start | bytes 1572872 | tf_op jit(solution)/shard_map/ppermute | solution.py:188
  93.2 7.7 %all-to-all-done.2.refs_2_.refs_0_ = bf16[4,128,512]{2,1,0:T(8,128)(2,1)S(1)} async-done(((bf16[4,128,512]{2,1,0:T(8,128)(2,1)}), bf16[4,128,512]{2,1,0:T(8,128)(2,1)S(1)}, u32[]{:S(2)}, u32[]{:S(2)}) %all-to-all-start.2) | async-done | bytes 524320 | tf_op jit(solution)/shard_map/all_to_all | solution.py:192
  101.8 4.9 %all-to-all-start.3 = ((bf16[8,128,256]{2,1,0:T(8,128)(2,1)}), bf16[8,128,256]{2,1,0:T(8,128)(2,1)S(1)}, u32[]{:S(2)}, u32[]{:S(2)}) async-start(bf16[8,128,256]{2,1,0:T(8,128)(2,1)} %shard_map.114), calls=%async_computation.3 | async-start | bytes 1048576 | tf_op jit(solution)/shard_map/all_to_all | solution.py:192
  107.5 1.3 collective-permute-start.5
  108.8 1.6 %shard_map.117.refs_0_ = f32[32,128]{1,0:T(8,128)S(1)} custom-call(bf16[128,512]{1,0:T(8,128)(2,1)S(1)} %get-tuple-element.23.refs_1_.refs_0_, bf16[128,512]{1,0:T(8,128)(2,1)S(1)} %multiply_convert_fusion.refs_1_, bf16[128,512]{1,0:T(8,128)(2,1)S(1)} %copy-done.10), custom_call_target="tpu_custom_call" | custom-call | flops 268435456 | bytes 409600 | tf_op jit(solution)/shard_map/pallas_call | solution.py:36
  110.4 4.1 %collective-permute-done.5.refs_2_ = bf16[128,512]{1,0:T(8,128)(2,1)S(1)} collective-permute-done((bf16[128,512]{1,0:T(8,128)(2,1)S(1)}, bf16[128,512]{1,0:T(8,128)(2,1)S(1)}, u32[]{:S(2)}, u32[]{:S(2)}) %collective-permute-start.5) | collective-permute-done | bytes 131104 | tf_op jit(solution)/shard_map/ppermute | solution.py:182
  115.2 9.4 %all-to-all-start.4 = ((bf16[32,32,128]{2,1,0:T(8,128)(2,1)}), bf16[32,32,128]{2,1,0:T(8,128)(2,1)S(1)}, u32[]{:S(2)}, u32[]{:S(2)}) async-start(bf16[32,32,128]{2,1,0:T(8,128)(2,1)} %shard_map.118), calls=%async_computation.4 | async-start | bytes 524288 | tf_op jit(solution)/shard_map/all_to_all | solution.py:270
  124.8 2.9 %collective-permute-start.4 = (bf16[128,256]{1,0:T(8,128)(2,1)S(1)}, bf16[128,256]{1,0:T(8,128)(2,1)S(1)}, u32[]{:S(2)}, u32[]{:S(2)}) collective-permute-start(bf16[128,256]{1,0:T(8,128)(2,1)S(1)} %reduce_sum.21), channel_id=1, source_target_pairs={{0,0},{1,1},{2,2},{3,3},{4,128},{5,129},{6,130},{7,131},{8,256},{9... | collective-permute-start | bytes 196616 | tf_op jit(solution)/shard_map/ppermute | solution.py:202
  127.8 1.7 %shard_map.116 = (bf16[128,512]{1,0:T(8,128)(2,1)}, bf16[128,512]{1,0:T(8,128)(2,1)}) custom-call(f32[32,128]{1,0:T(8,128)S(1)} %bitcast.12, bf16[128,512]{1,0:T(8,128)(2,1)S(1)} %get-tuple-element.23.refs_1_.refs_0_, bf16[128,512]{1,0:T(8,128)(2,1)S(1)} %collective-permute-done.5.refs_2_, bf16[128,512]{1,0:T(8,128)(2,1)S(1)} %copy-done.5, ...), custom_call_target="tpu_custom_call" | custom-call | flops 1073741824 | bytes 802816 | tf_op jit(solution)/shard_map/pallas_call | solution.py:36
  129.4 5.5 %collective-permute-done.4 = bf16[128,256]{1,0:T(8,128)(2,1)S(1)} collective-permute-done((bf16[128,256]{1,0:T(8,128)(2,1)S(1)}, bf16[128,256]{1,0:T(8,128)(2,1)S(1)}, u32[]{:S(2)}, u32[]{:S(2)}) %collective-permute-start.4) | collective-permute-done | bytes 65568 | tf_op jit(solution)/shard_map/ppermute | solution.py:202
  134.9 1.6 %bitcast_convert_fusion = f32[512,128]{1,0:T(8,128)} fusion(bf16[1,512,128]{2,1,0:T(8,128)(2,1)} %reduce-scatter.2.cloned.1.call-done), kind=kLoop, calls=%fused_computation.2 | loop fusion | flops 65536 | bytes 393216 | tf_op jit(solution)/shard_map/convert_element_type | solution.py:274
  (46 shorter events, 9.9 us)
Async XLA Ops:
  7.2 5.4 %copy-start.8 = (f32[128,32]{0,1:T(8,128)S(1)}, f32[128,32]{0,1:T(8,128)}, u32[]{:S(2)}) copy-start(f32[128,32]{0,1:T(8,128)} %param.9) | copy-start | bytes 49156
  7.2 8.1 %copy-start.6 = (bf16[128,512]{1,0:T(8,128)(2,1)S(1)}, bf16[128,512]{1,0:T(8,128)(2,1)}, u32[]{:S(2)}) copy-start(bf16[128,512]{1,0:T(8,128)(2,1)} %refs_1_.1) | copy-start | bytes 393220
  8.2 7.0 %collective-permute-start = (bf16[128,512]{1,0:T(8,128)(2,1)S(1)}, bf16[128,512]{1,0:T(8,128)(2,1)S(1)}, u32[]{:S(2)}, u32[]{:S(2)}) collective-permute-start(bf16[128,512]{1,0:T(8,128)(2,1)S(1)} %multiply_convert_fusion.refs_1_), channel_id=1, source_target_pairs={{0,16},{16,32},{32,48},{48,64},{64,80},{80,96},{96,112},{112,128},... | collective-permute-start | bytes 393224 | tf_op jit(solution)/shard_map/ppermute | solution.py:182
  15.3 2.5 %copy-start.9 = (bf16[128,512]{1,0:T(8,128)(2,1)}, bf16[128,512]{1,0:T(8,128)(2,1)S(1)}, u32[]{:S(2)}) copy-start(bf16[128,512]{1,0:T(8,128)(2,1)S(1)} %collective-permute-done.refs_2_) | copy-start | bytes 393220
  17.7 33.7 %all-to-all-start = ((bf16[4,128,512]{2,1,0:T(8,128)(2,1)}), bf16[4,128,512]{2,1,0:T(8,128)(2,1)S(1)}, u32[]{:S(2)}, u32[]{:S(2)}) async-start(bf16[4,128,512]{2,1,0:T(8,128)(2,1)} %get-tuple-element.16), calls=%async_computation | async-start | bytes 1048576 | tf_op jit(solution)/shard_map/all_to_all | solution.py:192
  35.0 0.8 copy-start.11
  35.0 41.5 %all-gather.3.cloned.1.call-start = ((), (), s32[]{:S(2)}) async-start(), calls=%async_computation.7 | async-start | bytes 1179648 | tf_op jit(solution)/shard_map/all_gather | solution.py:208
  35.8 99.1 %reduce-scatter.2.cloned.1.call-start = ((), (), s32[]{:S(2)}) async-start(), calls=%async_computation.6 | async-start | bytes 1179648 | tf_op jit(solution)/shard_map/reduce_scatter | solution.py:274
  35.9 15.5 %collective-permute-start.1 = (bf16[128,256]{1,0:T(8,128)(2,1)S(1)}, bf16[128,256]{1,0:T(8,128)(2,1)S(1)}, u32[]{:S(2)}, u32[]{:S(2)}) collective-permute-start(bf16[128,256]{1,0:T(8,128)(2,1)S(1)} %copy-done.11), channel_id=1, source_target_pairs={{0,0},{1,1},{2,2},{3,3},{4,128},{5,129},{6,130},{7,131},{8,256},{9... | collective-permute-start | bytes 196616 | tf_op jit(solution)/shard_map/ppermute | solution.py:202
  62.8 13.7 %collective-permute-start.2 = (bf16[8,128,256]{2,1,0:T(8,128)(2,1)S(1)}, bf16[8,128,256]{2,1,0:T(8,128)(2,1)S(1)}, u32[]{:S(2)}, u32[]{:S(2)}) collective-permute-start(bf16[8,128,256]{2,1,0:T(8,128)(2,1)S(1)} %all_to_all.25.refs_1_), channel_id=1, source_target_pairs={{0,1},{1,0},{2,3},{3,2},{4,5},{5,4},{6,7},{7,6},{8,9},{9,8},{10,11... | collective-permute-start | bytes 1572872 | tf_op jit(solution)/shard_map/ppermute | solution.py:188
  76.5 1.2 copy-start
  81.8 6.7 %copy-start.1 = (bf16[4096,128]{1,0:T(8,128)(2,1)S(1)}, bf16[4096,128]{1,0:T(8,128)(2,1)}, u32[]{:S(2)}) copy-start(bf16[4096,128]{1,0:T(8,128)(2,1)} %all-gather.3.cloned.1.call-done) | copy-start | bytes 3145732
  81.8 19.1 %all-to-all-start.2 = ((bf16[4,128,512]{2,1,0:T(8,128)(2,1)}), bf16[4,128,512]{2,1,0:T(8,128)(2,1)S(1)}, u32[]{:S(2)}, u32[]{:S(2)}) async-start(bf16[4,128,512]{2,1,0:T(8,128)(2,1)} %get-tuple-element.18.refs_2_), calls=%async_computation.2 | async-start | bytes 1048576 | tf_op jit(solution)/shard_map/all_to_all | solution.py:192
  89.4 3.8 %collective-permute-start.3 = (bf16[8,128,256]{2,1,0:T(8,128)(2,1)S(1)}, bf16[8,128,256]{2,1,0:T(8,128)(2,1)S(1)}, u32[]{:S(2)}, u32[]{:S(2)}) collective-permute-start(bf16[8,128,256]{2,1,0:T(8,128)(2,1)S(1)} %get-tuple-element.20.refs_3_), channel_id=1, source_target_pairs={{0,1},{1,0},{2,3},{3,2},{4,5},{5,4},{6,7},{7,6},{8,9},{9,8},{10,11... | collective-permute-start | bytes 1572872 | tf_op jit(solution)/shard_map/ppermute | solution.py:188
  91.3 0.8 copy-start.2
  101.8 4.9 %copy-start.3 = (bf16[8,128,256]{2,1,0:T(8,128)(2,1)S(1)}, bf16[8,128,256]{2,1,0:T(8,128)(2,1)}, u32[]{:S(2)}) copy-start(bf16[8,128,256]{2,1,0:T(8,128)(2,1)} %copy-done.2) | copy-start | bytes 1572868
  101.8 4.9 %copy-start.7 = (bf16[128,512]{1,0:T(8,128)(2,1)S(1)}, bf16[128,512]{1,0:T(8,128)(2,1)}, u32[]{:S(2)}) copy-start(bf16[128,512]{1,0:T(8,128)(2,1)} %refs_1_.1) | copy-start | bytes 393220
  101.8 12.7 %all-to-all-start.3 = ((bf16[8,128,256]{2,1,0:T(8,128)(2,1)}), bf16[8,128,256]{2,1,0:T(8,128)(2,1)S(1)}, u32[]{:S(2)}, u32[]{:S(2)}) async-start(bf16[8,128,256]{2,1,0:T(8,128)(2,1)} %shard_map.114), calls=%async_computation.3 | async-start | bytes 1048576 | tf_op jit(solution)/shard_map/all_to_all | solution.py:192
  106.7 2.0 %copy-start.10 = (bf16[128,512]{1,0:T(8,128)(2,1)S(1)}, bf16[128,512]{1,0:T(8,128)(2,1)}, u32[]{:S(2)}) copy-start(bf16[128,512]{1,0:T(8,128)(2,1)} %copy-done.9) | copy-start | bytes 393220
  107.5 7.0 %collective-permute-start.5 = (bf16[128,512]{1,0:T(8,128)(2,1)S(1)}, bf16[128,512]{1,0:T(8,128)(2,1)S(1)}, u32[]{:S(2)}, u32[]{:S(2)}) collective-permute-start(bf16[128,512]{1,0:T(8,128)(2,1)S(1)} %get-tuple-element.23.refs_1_.refs_0_), channel_id=1, source_target_pairs={{16,0},{32,16},{48,32},{64,48},{80,64},{96,80},{112,96},{128,112},... | collective-permute-start | bytes 393224 | tf_op jit(solution)/shard_map/ppermute | solution.py:182
  115.2 22.5 %all-to-all-start.4 = ((bf16[32,32,128]{2,1,0:T(8,128)(2,1)}), bf16[32,32,128]{2,1,0:T(8,128)(2,1)S(1)}, u32[]{:S(2)}, u32[]{:S(2)}) async-start(bf16[32,32,128]{2,1,0:T(8,128)(2,1)} %shard_map.118), calls=%async_computation.4 | async-start | bytes 524288 | tf_op jit(solution)/shard_map/all_to_all | solution.py:270
  124.7 3.1 %copy-start.4 = (bf16[128,512]{1,0:T(8,128)(2,1)S(1)}, bf16[128,512]{1,0:T(8,128)(2,1)}, u32[]{:S(2)}) copy-start(bf16[128,512]{1,0:T(8,128)(2,1)} %refs_4_.1) | copy-start | bytes 393220
  124.7 3.1 %copy-start.5 = (bf16[128,512]{1,0:T(8,128)(2,1)S(1)}, bf16[128,512]{1,0:T(8,128)(2,1)}, u32[]{:S(2)}) copy-start(bf16[128,512]{1,0:T(8,128)(2,1)} %refs_3_.3) | copy-start | bytes 393220
  124.8 10.1 %collective-permute-start.4 = (bf16[128,256]{1,0:T(8,128)(2,1)S(1)}, bf16[128,256]{1,0:T(8,128)(2,1)S(1)}, u32[]{:S(2)}, u32[]{:S(2)}) collective-permute-start(bf16[128,256]{1,0:T(8,128)(2,1)S(1)} %reduce_sum.21), channel_id=1, source_target_pairs={{0,0},{1,1},{2,2},{3,3},{4,128},{5,129},{6,130},{7,131},{8,256},{9... | collective-permute-start | bytes 196616 | tf_op jit(solution)/shard_map/ppermute | solution.py:202
Sparse Core Ops, SparseCore 0:
  37.9 38.5 all-gather.2
  81.9 40.5 reduce-scatter.1

commit v6 on v4

--- a/solution.py
+++ b/solution.py
@@ -265,7 +265,7 @@
     )
 
     got = exchange(pieces, "col", CHIP_GROUPS)
-    grad_taps = call(taps_body, shaped((YS * ZS, 32, 128), BF16), (grad_taps,), after=(got,))
+    grad_taps = call(taps_body, shaped((YS * ZS, 32, 128), BF16), (grad_taps,), after=(got, later))
     grad_taps = jnp.sum(lax.all_to_all(grad_taps, "row", 0, 0, tiled=True).astype(F32), 0)
     grad_filters = jnp.flip(grad_taps, 1).T
 

time: 132 us -> 131 us (level)
  the two profiles are of different devices: /device:TPU:48 before, /device:TPU:2 now
where the time goes in v6:
time: 131 us
  starting transfers between devices  43 us (33%)
  waiting for transfers between devices  33.1 us (25%)
  blocking collectives  19.7 us (15%)
  between operations  14.3 us (11%)
  Pallas kernels  13 us (10%)
  local copies, waits for them, and re-layouts  4.95 us (4%)
  other arithmetic  2.86 us (2%)
    all_to_all x3, starting transfers between devices, exchange(): lax.all_to_all(blocks, axis, 0, 0, axis_index_groups=groups, tiled=True)  23.1 us
    all_to_all x1, blocking collectives, exchange(): lax.all_to_all(blocks, axis, 0, 0, axis_index_groups=groups, tiled=True)  19.7 us
    pallas_call x11, Pallas kernels, call(): pl.pallas_call(run, out_shape=out_shape, in_specs=specs, scratch_shapes=l...  13 us
    all_to_all x1, waiting for transfers between devices, local(): lax.all_to_all(grad_taps, 'row', 0, 0, tiled=True).astype(F32)  8.93 us
    all_to_all x1, starting transfers between devices, local(): lax.all_to_all(grad_taps, 'row', 0, 0, tiled=True).astype(F32)  8.9 us
    all_to_all x3, waiting for transfers between devices, exchange(): lax.all_to_all(blocks, axis, 0, 0, axis_index_groups=groups, tiled=True)  8.08 us
    ppermute x2, waiting for transfers between devices, shift_row(): lax.ppermute(block, 'row', [(i, i + distance) for i in range(n) if 0 <= i...  6.43 us
    all_gather x1, waiting for transfers between devices, local(): w8 = lax.all_gather(w_out, 'row', axis_index_groups=Z_GROUPS)  5.91 us
  transfers between devices with their start and end apart: 12, of which 8 were waited for; matrix products, arithmetic and copies ran while one was open for 1% of the time, Pallas kernels for 9%

profile of v6, /device:TPU:2, one launch (start us, length us, event | category | flops | bytes accessed | tf_op | source)
XLA Modules:
  0.0 130.8 jit_solution(17404661150275908101)
XLA Ops:
  8.3 4.4 %collective-permute-start = (bf16[128,512]{1,0:T(8,128)(2,1)S(1)}, bf16[128,512]{1,0:T(8,128)(2,1)S(1)}, u32[]{:S(2)}, u32[]{:S(2)}) collective-permute-start(bf16[128,512]{1,0:T(8,128)(2,1)S(1)} %multiply_convert_fusion.refs_1_), channel_id=1, source_target_pairs={{0,16},{16,32},{32,48},{48,64},{64,80},{80,96},{96,112},{112,128},... | collective-permute-start | bytes 393224 | tf_op jit(solution)/shard_map/ppermute | solution.py:180
  13.6 1.8 %collective-permute-done.refs_2_ = bf16[128,512]{1,0:T(8,128)(2,1)S(1)} collective-permute-done((bf16[128,512]{1,0:T(8,128)(2,1)S(1)}, bf16[128,512]{1,0:T(8,128)(2,1)S(1)}, u32[]{:S(2)}, u32[]{:S(2)}) %collective-permute-start) | collective-permute-done | bytes 131104 | tf_op jit(solution)/shard_map/ppermute | solution.py:180
  15.4 1.6 %shard_map.109 = (f32[128,512]{1,0:T(8,128)S(1)}, bf16[128,512]{1,0:T(8,128)(2,1)S(1)}) custom-call(f32[32,128]{1,0:T(8,128)S(1)} %pad_maximum_fusion.refs_0_, bf16[128,512]{1,0:T(8,128)(2,1)S(1)} %multiply_convert_fusion.refs_1_, bf16[128,512]{1,0:T(8,128)(2,1)S(1)} %collective-permute-done.refs_2_, bf16[128,512]{1,0:T(8,128)(2,1)S(1)} %copy-done.6), custom_call_target="tpu_custom_call" | custom-call | flops 2147483648 | bytes 802816 | tf_op jit(solution)/shard_map/pallas_call | solution.py:36
  17.1 19.7 %all_to_all.25.refs_1_ = bf16[8,128,256]{2,1,0:T(8,128)(2,1)S(1)} all-to-all(bf16[8,128,256]{2,1,0:T(8,128)(2,1)S(1)} %shard_map.110), channel_id=1, replica_groups={{0,2,4,6,8,10,12,14},{1,3,5,7,9,11,13,15},{16,18,20,22,24,26,28,30},{17..., dimensions={0} | all-to-all | bytes 1048576 | tf_op jit(solution)/shard_map/all_to_all | solution.py:190
  37.7 11.4 %all-to-all-start.1 = ((bf16[4,128,512]{2,1,0:T(8,128)(2,1)}), bf16[4,128,512]{2,1,0:T(8,128)(2,1)S(1)}, u32[]{:S(2)}, u32[]{:S(2)}) async-start(bf16[4,128,512]{2,1,0:T(8,128)(2,1)} %shard_map.111), calls=%async_computation.1 | async-start | bytes 1048576 | tf_op jit(solution)/shard_map/all_to_all | solution.py:190
  49.1 1.9 %collective-permute-start.2 = (bf16[8,128,256]{2,1,0:T(8,128)(2,1)S(1)}, bf16[8,128,256]{2,1,0:T(8,128)(2,1)S(1)}, u32[]{:S(2)}, u32[]{:S(2)}) collective-permute-start(bf16[8,128,256]{2,1,0:T(8,128)(2,1)S(1)} %all_to_all.25.refs_1_), channel_id=1, source_target_pairs={{0,1},{1,0},{2,3},{3,2},{4,5},{5,4},{6,7},{7,6},{8,9},{9,8},{10,11... | collective-permute-start | bytes 1572872 | tf_op jit(solution)/shard_map/ppermute | solution.py:186
  51.0 1.9 %collective-permute-done.2.refs_2_ = bf16[8,128,256]{2,1,0:T(8,128)(2,1)S(1)} collective-permute-done((bf16[8,128,256]{2,1,0:T(8,128)(2,1)S(1)}, bf16[8,128,256]{2,1,0:T(8,128)(2,1)S(1)}, u32[]{:S(2)}, u32[]{:S(2)}) %collective-permute-start.2) | collective-permute-done | bytes 524320 | tf_op jit(solution)/shard_map/ppermute | solution.py:186
  52.9 5.9 %all-gather.3.cloned.1.call-done = bf16[4096,128]{1,0:T(8,128)(2,1)} async-done(((bf16[512,128]{1,0:T(8,128)(2,1)}), bf16[4096,128]{1,0:T(8,128)(2,1)}) %all-gather.3.cloned.1.call-update) | async-done | bytes 1048592 | tf_op jit(solution)/shard_map/all_gather | solution.py:206
  58.8 1.2 copy-done
  60.0 2.3 %shard_map.112 = (bf16[16,128,256]{2,1,0:T(8,128)(2,1)S(1)}, bf16[4,128,512]{2,1,0:T(8,128)(2,1)}) custom-call(s32[1]{0:T(128)} %bitcast.refs_0_, bf16[8,128,256]{2,1,0:T(8,128)(2,1)S(1)} %all_to_all.25.refs_1_, bf16[8,128,256]{2,1,0:T(8,128)(2,1)S(1)} %collective-permute-done.2.refs_2_, bf16[8,512,128]{2,1,0:T(8,128)(2,1)S(1)} %bitcast.8), custom_call_target="tpu_custom_call" | custom-call | flops 536870912 | bytes 3670016 | tf_op jit(solution)/shard_map/pallas_call | solution.py:36
  63.1 1.8 %shard_map.113.refs_3_ = bf16[8,512,128]{2,1,0:T(8,128)(2,1)} custom-call(bf16[4,128,512]{2,1,0:T(8,128)(2,1)S(1)} %all-to-all-done.1.refs_0_.refs_1_, bf16[16,128,256]{2,1,0:T(8,128)(2,1)S(1)} %get-tuple-element.17.refs_1_, bf16[4,128,512]{2,1,0:T(8,128)(2,1)} %get-tuple-element.18.refs_2_), custom_call_target="tpu_custom_call" | custom-call | flops 536870912 | bytes 2621440 | tf_op jit(solution)/shard_map/pallas_call | solution.py:36
  64.9 6.0 %all-to-all-start.2 = ((bf16[4,128,512]{2,1,0:T(8,128)(2,1)}), bf16[4,128,512]{2,1,0:T(8,128)(2,1)S(1)}, u32[]{:S(2)}, u32[]{:S(2)}) async-start(bf16[4,128,512]{2,1,0:T(8,128)(2,1)} %get-tuple-element.18.refs_2_), calls=%async_computation.2 | async-start | bytes 1048576 | tf_op jit(solution)/shard_map/all_to_all | solution.py:190
  72.7 1.9 %collective-permute-start.3 = (bf16[8,128,256]{2,1,0:T(8,128)(2,1)S(1)}, bf16[8,128,256]{2,1,0:T(8,128)(2,1)S(1)}, u32[]{:S(2)}, u32[]{:S(2)}) collective-permute-start(bf16[8,128,256]{2,1,0:T(8,128)(2,1)S(1)} %get-tuple-element.20.refs_3_), channel_id=1, source_target_pairs={{0,1},{1,0},{2,3},{3,2},{4,5},{5,4},{6,7},{7,6},{8,9},{9,8},{10,11... | collective-permute-start | bytes 1572872 | tf_op jit(solution)/shard_map/ppermute | solution.py:186
  74.6 1.9 %collective-permute-done.3.refs_1_ = bf16[8,128,256]{2,1,0:T(8,128)(2,1)S(1)} collective-permute-done((bf16[8,128,256]{2,1,0:T(8,128)(2,1)S(1)}, bf16[8,128,256]{2,1,0:T(8,128)(2,1)S(1)}, u32[]{:S(2)}, u32[]{:S(2)}) %collective-permute-start.3) | collective-permute-done | bytes 524320 | tf_op jit(solution)/shard_map/ppermute | solution.py:186
  76.5 7.2 %all-to-all-done.2.refs_2_.refs_0_ = bf16[4,128,512]{2,1,0:T(8,128)(2,1)S(1)} async-done(((bf16[4,128,512]{2,1,0:T(8,128)(2,1)}), bf16[4,128,512]{2,1,0:T(8,128)(2,1)S(1)}, u32[]{:S(2)}, u32[]{:S(2)}) %all-to-all-start.2) | async-done | bytes 524320 | tf_op jit(solution)/shard_map/all_to_all | solution.py:190
  83.8 1.2 copy-done.3
  85.9 5.6 %all-to-all-start.3 = ((bf16[8,128,256]{2,1,0:T(8,128)(2,1)}), bf16[8,128,256]{2,1,0:T(8,128)(2,1)S(1)}, u32[]{:S(2)}, u32[]{:S(2)}) async-start(bf16[8,128,256]{2,1,0:T(8,128)(2,1)} %shard_map.115), calls=%async_computation.3 | async-start | bytes 1048576 | tf_op jit(solution)/shard_map/all_to_all | solution.py:190
  92.2 1.3 collective-permute-start.5
  93.5 1.6 %shard_map.118.refs_0_ = f32[32,128]{1,0:T(8,128)S(1)} custom-call(bf16[128,512]{1,0:T(8,128)(2,1)S(1)} %get-tuple-element.23.refs_1_.refs_0_, bf16[128,512]{1,0:T(8,128)(2,1)S(1)} %multiply_convert_fusion.refs_1_, bf16[128,512]{1,0:T(8,128)(2,1)S(1)} %copy-done.10), custom_call_target="tpu_custom_call" | custom-call | flops 268435456 | bytes 409600 | tf_op jit(solution)/shard_map/pallas_call | solution.py:36
  95.1 4.6 %collective-permute-done.5.refs_2_ = bf16[128,512]{1,0:T(8,128)(2,1)S(1)} collective-permute-done((bf16[128,512]{1,0:T(8,128)(2,1)S(1)}, bf16[128,512]{1,0:T(8,128)(2,1)S(1)}, u32[]{:S(2)}, u32[]{:S(2)}) %collective-permute-start.5) | collective-permute-done | bytes 131104 | tf_op jit(solution)/shard_map/ppermute | solution.py:180
  100.5 8.9 %all-to-all-start.4 = ((bf16[32,32,128]{2,1,0:T(8,128)(2,1)}), bf16[32,32,128]{2,1,0:T(8,128)(2,1)S(1)}, u32[]{:S(2)}, u32[]{:S(2)}) async-start(bf16[32,32,128]{2,1,0:T(8,128)(2,1)} %shard_map.119), calls=%async_computation.4 | async-start | bytes 524288 | tf_op jit(solution)/shard_map/all_to_all | solution.py:269
  110.4 1.7 %shard_map.117 = (bf16[128,512]{1,0:T(8,128)(2,1)}, bf16[128,512]{1,0:T(8,128)(2,1)}) custom-call(f32[32,128]{1,0:T(8,128)S(1)} %bitcast.12, bf16[128,512]{1,0:T(8,128)(2,1)S(1)} %get-tuple-element.23.refs_1_.refs_0_, bf16[128,512]{1,0:T(8,128)(2,1)S(1)} %collective-permute-done.5.refs_2_, bf16[128,512]{1,0:T(8,128)(2,1)S(1)} %copy-done.5, ...), custom_call_target="tpu_custom_call" | custom-call | flops 1073741824 | bytes 802816 | tf_op jit(solution)/shard_map/pallas_call | solution.py:36
  112.1 1.6 %bitcast_convert_fusion = f32[512,128]{1,0:T(8,128)} fusion(bf16[1,512,128]{2,1,0:T(8,128)(2,1)} %reduce-scatter.2.cloned.1.call-done), kind=kLoop, calls=%fused_computation.2 | loop fusion | flops 65536 | bytes 393216 | tf_op jit(solution)/shard_map/convert_element_type | solution.py:273
  113.7 8.9 %all-to-all-done.4 = bf16[32,32,128]{2,1,0:T(8,128)(2,1)S(1)} async-done(((bf16[32,32,128]{2,1,0:T(8,128)(2,1)}), bf16[32,32,128]{2,1,0:T(8,128)(2,1)S(1)}, u32[]{:S(2)}, u32[]{:S(2)}) %all-to-all-start.4) | async-done | bytes 262176 | tf_op jit(solution)/shard_map/all_to_all | solution.py:269
  (47 shorter events, 10.2 us)
Async XLA Ops:
  7.2 51.6 %all-gather.3.cloned.1.call-start = ((), (), s32[]{:S(2)}) async-start(), calls=%async_computation.7 | async-start | bytes 1179648 | tf_op jit(solution)/shard_map/all_gather | solution.py:206
  7.2 5.5 %copy-start.11 = (bf16[128,256]{1,0:T(8,128)(2,1)S(1)}, bf16[128,256]{1,0:T(8,128)(2,1)}, u32[]{:S(2)}) copy-start(bf16[128,256]{1,0:T(8,128)(2,1)} %param.11) | copy-start | bytes 196612
  7.2 6.2 %copy-start.8 = (f32[128,32]{0,1:T(8,128)S(1)}, f32[128,32]{0,1:T(8,128)}, u32[]{:S(2)}) copy-start(f32[128,32]{0,1:T(8,128)} %param.9) | copy-start | bytes 49156
  8.3 7.2 %copy-start.6 = (bf16[128,512]{1,0:T(8,128)(2,1)S(1)}, bf16[128,512]{1,0:T(8,128)(2,1)}, u32[]{:S(2)}) copy-start(bf16[128,512]{1,0:T(8,128)(2,1)} %refs_1_.1) | copy-start | bytes 393220
  8.3 7.2 %collective-permute-start = (bf16[128,512]{1,0:T(8,128)(2,1)S(1)}, bf16[128,512]{1,0:T(8,128)(2,1)S(1)}, u32[]{:S(2)}, u32[]{:S(2)}) collective-permute-start(bf16[128,512]{1,0:T(8,128)(2,1)S(1)} %multiply_convert_fusion.refs_1_), channel_id=1, source_target_pairs={{0,16},{16,32},{32,48},{48,64},{64,80},{80,96},{96,112},{112,128},... | collective-permute-start | bytes 393224 | tf_op jit(solution)/shard_map/ppermute | solution.py:180
  12.7 4.4 %collective-permute-start.1 = (bf16[128,256]{1,0:T(8,128)(2,1)S(1)}, bf16[128,256]{1,0:T(8,128)(2,1)S(1)}, u32[]{:S(2)}, u32[]{:S(2)}) collective-permute-start(bf16[128,256]{1,0:T(8,128)(2,1)S(1)} %copy-done.11), channel_id=1, source_target_pairs={{0,0},{1,1},{2,2},{3,3},{4,128},{5,129},{6,130},{7,131},{8,256},{9... | collective-permute-start | bytes 196616 | tf_op jit(solution)/shard_map/ppermute | solution.py:200
  15.4 1.6 %copy-start.9 = (bf16[128,512]{1,0:T(8,128)(2,1)}, bf16[128,512]{1,0:T(8,128)(2,1)S(1)}, u32[]{:S(2)}) copy-start(bf16[128,512]{1,0:T(8,128)(2,1)S(1)} %collective-permute-done.refs_2_) | copy-start | bytes 393220
  37.7 25.5 %all-to-all-start.1 = ((bf16[4,128,512]{2,1,0:T(8,128)(2,1)}), bf16[4,128,512]{2,1,0:T(8,128)(2,1)S(1)}, u32[]{:S(2)}, u32[]{:S(2)}) async-start(bf16[4,128,512]{2,1,0:T(8,128)(2,1)} %shard_map.111), calls=%async_computation.1 | async-start | bytes 1048576 | tf_op jit(solution)/shard_map/all_to_all | solution.py:190
  49.1 63.0 %reduce-scatter.2.cloned.1.call-start = ((), (), s32[]{:S(2)}) async-start(), calls=%async_computation.6 | async-start | bytes 1179648 | tf_op jit(solution)/shard_map/reduce_scatter | solution.py:273
  49.1 3.8 %collective-permute-start.2 = (bf16[8,128,256]{2,1,0:T(8,128)(2,1)S(1)}, bf16[8,128,256]{2,1,0:T(8,128)(2,1)S(1)}, u32[]{:S(2)}, u32[]{:S(2)}) collective-permute-start(bf16[8,128,256]{2,1,0:T(8,128)(2,1)S(1)} %all_to_all.25.refs_1_), channel_id=1, source_target_pairs={{0,1},{1,0},{2,3},{3,2},{4,5},{5,4},{6,7},{7,6},{8,9},{9,8},{10,11... | collective-permute-start | bytes 1572872 | tf_op jit(solution)/shard_map/ppermute | solution.py:186
  58.8 1.2 copy-start
  64.9 6.0 %copy-start.1 = (bf16[4096,128]{1,0:T(8,128)(2,1)S(1)}, bf16[4096,128]{1,0:T(8,128)(2,1)}, u32[]{:S(2)}) copy-start(bf16[4096,128]{1,0:T(8,128)(2,1)} %all-gather.3.cloned.1.call-done) | copy-start | bytes 3145732
  64.9 18.9 %all-to-all-start.2 = ((bf16[4,128,512]{2,1,0:T(8,128)(2,1)}), bf16[4,128,512]{2,1,0:T(8,128)(2,1)S(1)}, u32[]{:S(2)}, u32[]{:S(2)}) async-start(bf16[4,128,512]{2,1,0:T(8,128)(2,1)} %get-tuple-element.18.refs_2_), calls=%async_computation.2 | async-start | bytes 1048576 | tf_op jit(solution)/shard_map/all_to_all | solution.py:190
  71.8 1.0 copy-start.2
  72.7 3.8 %collective-permute-start.3 = (bf16[8,128,256]{2,1,0:T(8,128)(2,1)S(1)}, bf16[8,128,256]{2,1,0:T(8,128)(2,1)S(1)}, u32[]{:S(2)}, u32[]{:S(2)}) collective-permute-start(bf16[8,128,256]{2,1,0:T(8,128)(2,1)S(1)} %get-tuple-element.20.refs_3_), channel_id=1, source_target_pairs={{0,1},{1,0},{2,3},{3,2},{4,5},{5,4},{6,7},{7,6},{8,9},{9,8},{10,11... | collective-permute-start | bytes 1572872 | tf_op jit(solution)/shard_map/ppermute | solution.py:186
  83.8 1.2 copy-start.3
  85.9 5.6 %copy-start.7 = (bf16[128,512]{1,0:T(8,128)(2,1)S(1)}, bf16[128,512]{1,0:T(8,128)(2,1)}, u32[]{:S(2)}) copy-start(bf16[128,512]{1,0:T(8,128)(2,1)} %refs_1_.1) | copy-start | bytes 393220
  85.9 13.9 %all-to-all-start.3 = ((bf16[8,128,256]{2,1,0:T(8,128)(2,1)}), bf16[8,128,256]{2,1,0:T(8,128)(2,1)S(1)}, u32[]{:S(2)}, u32[]{:S(2)}) async-start(bf16[8,128,256]{2,1,0:T(8,128)(2,1)} %shard_map.115), calls=%async_computation.3 | async-start | bytes 1048576 | tf_op jit(solution)/shard_map/all_to_all | solution.py:190
  91.5 2.0 %copy-start.10 = (bf16[128,512]{1,0:T(8,128)(2,1)S(1)}, bf16[128,512]{1,0:T(8,128)(2,1)}, u32[]{:S(2)}) copy-start(bf16[128,512]{1,0:T(8,128)(2,1)} %copy-done.9) | copy-start | bytes 393220
  92.2 7.6 %collective-permute-start.5 = (bf16[128,512]{1,0:T(8,128)(2,1)S(1)}, bf16[128,512]{1,0:T(8,128)(2,1)S(1)}, u32[]{:S(2)}, u32[]{:S(2)}) collective-permute-start(bf16[128,512]{1,0:T(8,128)(2,1)S(1)} %get-tuple-element.23.refs_1_.refs_0_), channel_id=1, source_target_pairs={{16,0},{32,16},{48,32},{64,48},{80,64},{96,80},{112,96},{128,112},... | collective-permute-start | bytes 393224 | tf_op jit(solution)/shard_map/ppermute | solution.py:180
  100.5 22.1 %all-to-all-start.4 = ((bf16[32,32,128]{2,1,0:T(8,128)(2,1)}), bf16[32,32,128]{2,1,0:T(8,128)(2,1)S(1)}, u32[]{:S(2)}, u32[]{:S(2)}) async-start(bf16[32,32,128]{2,1,0:T(8,128)(2,1)} %shard_map.119), calls=%async_computation.4 | async-start | bytes 524288 | tf_op jit(solution)/shard_map/all_to_all | solution.py:269
  109.4 0.9 copy-start.4
  109.4 1.0 copy-start.5
  109.5 2.5 %collective-permute-start.4 = (bf16[128,256]{1,0:T(8,128)(2,1)S(1)}, bf16[128,256]{1,0:T(8,128)(2,1)S(1)}, u32[]{:S(2)}, u32[]{:S(2)}) collective-permute-start(bf16[128,256]{1,0:T(8,128)(2,1)S(1)} %reduce_sum.21), channel_id=1, source_target_pairs={{0,0},{1,1},{2,2},{3,3},{4,128},{5,129},{6,130},{7,131},{8,256},{9... | collective-permute-start | bytes 196616 | tf_op jit(solution)/shard_map/ppermute | solution.py:200
Sparse Core Ops, SparseCore 0:
  12.8 45.8 all-gather.2
  65.0 39.1 reduce-scatter.1

commit v7 on v6

--- a/solution.py
+++ b/solution.py
@@ -122,7 +122,11 @@
 
 
 def taps_body(taps_ref, out_ref):
-    taps = taps_ref[...].astype(BF16)
+    row, lane = iotas(128, 128)
+    flip = jnp.where(row + lane == 127, 1.0, 0.0).astype(BF16)
+    taps = lax.dot_general(
+        taps_ref[...].astype(BF16), flip, NN, preferred_element_type=F32
+    ).astype(BF16)
     for i in range(YS * ZS):
         out_ref[i] = taps
 
@@ -230,13 +234,6 @@
         position=at,
     )
     sums = exchange(shares, "row", Y_GROUPS)
-    gw8 = call(
-        grad_w_body,
-        shaped((ZS, 512, 128), BF16),
-        (mixed4, cot16),
-        flops=2 * 512 * 512 * 1024,
-        after=(shares,),
-    )
     keep, give = call(
         projected_body,
         [shaped((8, 128, 256), F32), shaped((8, 128, 256), BF16)],
@@ -244,10 +241,17 @@
         [pltpu.VMEM((COLS, 128, 256), F32)],
         flops=2 * 512 * 512 * 1024,
         position=at,
-        after=(gw8,),
+        after=(shares,),
+    )
+    gw8 = call(
+        grad_w_body,
+        shaped((ZS, 512, 128), BF16),
+        (mixed4, cot16),
+        flops=2 * 512 * 512 * 1024,
+        after=(give,),
     )
     pieces = call(pair_body, shaped((8, 128, 256), BF16), (keep, other_core(give)), after=(sums,))
-    grad_q, grad_conv = call(grad_conv_body, [tile, tile], (sums, q_proj, conv), after=(give,))
+    grad_q, grad_conv = call(grad_conv_body, [tile, tile], (sums, q_proj, conv), after=(gw8,))
     later = shift_row(grad_conv, -1)
     grad_taps = call(
         grad_filters_body,
@@ -267,7 +271,7 @@
     got = exchange(pieces, "col", CHIP_GROUPS)
     grad_taps = call(taps_body, shaped((YS * ZS, 32, 128), BF16), (grad_taps,), after=(got, later))
     grad_taps = jnp.sum(lax.all_to_all(grad_taps, "row", 0, 0, tiled=True).astype(F32), 0)
-    grad_filters = jnp.flip(grad_taps, 1).T
+    grad_filters = grad_taps.T
 
     projected = swap_pieces(jnp.sum(got.astype(F32), 0).astype(BF16))
     grad_w = lax.psum_scatter(gw8, "row", axis_index_groups=Z_GROUPS).astype(F32)

time: 131 us -> 136 us (1.038)
  waiting for transfers between devices: 33.1 us -> 35.5 us
    all_gather x1, waiting for transfers between devices: 5.91 us -> 8.04 us  [local(): w8 = lax.all_gather(w_out, 'row', axis_index_groups=Z_GROUPS)]
    unnamed x25 -> x33, local copies, waits for them, and re-layouts: 4.12 us -> 5.55 us
  transfers between devices with their start and end apart: 12 -> 12, of which waited for: 8 -> 7; matrix products, arithmetic and copies ran while one was open for 1% -> 1% of each run, Pallas kernels for 9% -> 8%
where the time goes in v7:
time: 136 us; the launch traced here: 135 us
  starting transfers between devices  43.6 us (32%)
  waiting for transfers between devices  35.5 us (26%)
  blocking collectives  19.6 us (14%)
  between operations  14.3 us (11%)
  Pallas kernels  13.1 us (10%)
  local copies, waits for them, and re-layouts  5.69 us (4%)
  other arithmetic  3.44 us (3%)
    all_to_all x3, starting transfers between devices, exchange(): lax.all_to_all(blocks, axis, 0, 0, axis_index_groups=groups, tiled=True)  23.3 us
    all_to_all x1, blocking collectives, exchange(): lax.all_to_all(blocks, axis, 0, 0, axis_index_groups=groups, tiled=True)  19.6 us
    pallas_call x11, Pallas kernels, call(): pl.pallas_call(run, out_shape=out_shape, in_specs=specs, scratch_shapes=l...  13.1 us
    all_to_all x1, starting transfers between devices, local(): lax.all_to_all(grad_taps, 'row', 0, 0, tiled=True).astype(F32)  9.26 us
    all_to_all x1, waiting for transfers between devices, local(): lax.all_to_all(grad_taps, 'row', 0, 0, tiled=True).astype(F32)  9.04 us
    all_to_all x3, waiting for transfers between devices, exchange(): lax.all_to_all(blocks, axis, 0, 0, axis_index_groups=groups, tiled=True)  8.72 us
    all_gather x1, waiting for transfers between devices, local(): w8 = lax.all_gather(w_out, 'row', axis_index_groups=Z_GROUPS)  8.04 us
    ppermute x2, waiting for transfers between devices, shift_row(): lax.ppermute(block, 'row', [(i, i + distance) for i in range(n) if 0 <= i...  5.91 us
  transfers between devices with their start and end apart: 12, of which 7 were waited for; matrix products, arithmetic and copies ran while one was open for 1% of the time, Pallas kernels for 8%

profile of v7, /device:TPU:2, one launch (start us, length us, event | category | flops | bytes accessed | tf_op | source)
XLA Modules:
  0.0 135.2 jit_solution(14378490978344059255)
XLA Ops:
  8.3 4.4 %collective-permute-start = (bf16[128,512]{1,0:T(8,128)(2,1)S(1)}, bf16[128,512]{1,0:T(8,128)(2,1)S(1)}, u32[]{:S(2)}, u32[]{:S(2)}) collective-permute-start(bf16[128,512]{1,0:T(8,128)(2,1)S(1)} %multiply_convert_fusion.refs_1_), channel_id=1, source_target_pairs={{0,16},{16,32},{32,48},{48,64},{64,80},{80,96},{96,112},{112,128},... | collective-permute-start | bytes 393224 | tf_op jit(solution)/shard_map/ppermute | solution.py:184
  13.6 1.8 %collective-permute-done.refs_2_ = bf16[128,512]{1,0:T(8,128)(2,1)S(1)} collective-permute-done((bf16[128,512]{1,0:T(8,128)(2,1)S(1)}, bf16[128,512]{1,0:T(8,128)(2,1)S(1)}, u32[]{:S(2)}, u32[]{:S(2)}) %collective-permute-start) | collective-permute-done | bytes 131104 | tf_op jit(solution)/shard_map/ppermute | solution.py:184
  15.4 1.6 %shard_map.109 = (f32[128,512]{1,0:T(8,128)S(1)}, bf16[128,512]{1,0:T(8,128)(2,1)S(1)}) custom-call(f32[32,128]{1,0:T(8,128)S(1)} %pad_maximum_fusion.refs_0_, bf16[128,512]{1,0:T(8,128)(2,1)S(1)} %multiply_convert_fusion.refs_1_, bf16[128,512]{1,0:T(8,128)(2,1)S(1)} %collective-permute-done.refs_2_, bf16[128,512]{1,0:T(8,128)(2,1)S(1)} %copy-done.10), custom_call_target="tpu_custom_call" | custom-call | flops 2147483648 | bytes 802816 | tf_op jit(solution)/shard_map/pallas_call | solution.py:36
  17.1 19.6 %all_to_all.25.refs_1_ = bf16[8,128,256]{2,1,0:T(8,128)(2,1)S(1)} all-to-all(bf16[8,128,256]{2,1,0:T(8,128)(2,1)S(1)} %shard_map.110), channel_id=1, replica_groups={{0,2,4,6,8,10,12,14},{1,3,5,7,9,11,13,15},{16,18,20,22,24,26,28,30},{17..., dimensions={0} | all-to-all | bytes 1048576 | tf_op jit(solution)/shard_map/all_to_all | solution.py:194
  37.6 11.4 %all-to-all-start.1 = ((bf16[4,128,512]{2,1,0:T(8,128)(2,1)}), bf16[4,128,512]{2,1,0:T(8,128)(2,1)S(1)}, u32[]{:S(2)}, u32[]{:S(2)}) async-start(bf16[4,128,512]{2,1,0:T(8,128)(2,1)} %shard_map.111), calls=%async_computation.1 | async-start | bytes 1048576 | tf_op jit(solution)/shard_map/all_to_all | solution.py:194
  49.1 1.9 %collective-permute-start.2 = (bf16[8,128,256]{2,1,0:T(8,128)(2,1)S(1)}, bf16[8,128,256]{2,1,0:T(8,128)(2,1)S(1)}, u32[]{:S(2)}, u32[]{:S(2)}) collective-permute-start(bf16[8,128,256]{2,1,0:T(8,128)(2,1)S(1)} %all_to_all.25.refs_1_), channel_id=1, source_target_pairs={{0,1},{1,0},{2,3},{3,2},{4,5},{5,4},{6,7},{7,6},{8,9},{9,8},{10,11... | collective-permute-start | bytes 1572872 | tf_op jit(solution)/shard_map/ppermute | solution.py:190
  51.0 1.9 %collective-permute-done.2.refs_2_ = bf16[8,128,256]{2,1,0:T(8,128)(2,1)S(1)} collective-permute-done((bf16[8,128,256]{2,1,0:T(8,128)(2,1)S(1)}, bf16[8,128,256]{2,1,0:T(8,128)(2,1)S(1)}, u32[]{:S(2)}, u32[]{:S(2)}) %collective-permute-start.2) | collective-permute-done | bytes 524320 | tf_op jit(solution)/shard_map/ppermute | solution.py:190
  53.6 8.0 %all-gather.3.cloned.1.call-done = bf16[4096,128]{1,0:T(8,128)(2,1)} async-done(((bf16[512,128]{1,0:T(8,128)(2,1)}), bf16[4096,128]{1,0:T(8,128)(2,1)}) %all-gather.3.cloned.1.call-update) | async-done | bytes 1048592 | tf_op jit(solution)/shard_map/all_gather | solution.py:210
  61.7 1.2 copy-done
  62.9 1.0 copy-done.5
  64.0 2.3 %shard_map.112 = (bf16[16,128,256]{2,1,0:T(8,128)(2,1)S(1)}, bf16[4,128,512]{2,1,0:T(8,128)(2,1)}) custom-call(s32[1]{0:T(128)} %bitcast.refs_0_, bf16[8,128,256]{2,1,0:T(8,128)(2,1)S(1)} %all_to_all.25.refs_1_, bf16[8,128,256]{2,1,0:T(8,128)(2,1)S(1)} %copy-done.5, bf16[8,512,128]{2,1,0:T(8,128)(2,1)S(1)} %bitcast.8), custom_call_target="tpu_custom_call" | custom-call | flops 536870912 | bytes 3670016 | tf_op jit(solution)/shard_map/pallas_call | solution.py:36
  68.1 1.7 %shard_map.115.refs_3_ = bf16[8,512,128]{2,1,0:T(8,128)(2,1)} custom-call(bf16[4,128,512]{2,1,0:T(8,128)(2,1)S(1)} %all-to-all-done.1.refs_1_.refs_0_, bf16[16,128,256]{2,1,0:T(8,128)(2,1)S(1)} %get-tuple-element.21.refs_1_, bf16[8,128,256]{2,1,0:T(8,128)(2,1)S(1)} %get-tuple-element.19.refs_2_), custom_call_target="tpu_custom_call" | custom-call | flops 536870912 | bytes 2621440 | tf_op jit(solution)/shard_map/pallas_call | solution.py:36
  70.6 6.9 %all-to-all-start.2 = ((bf16[4,128,512]{2,1,0:T(8,128)(2,1)}), bf16[4,128,512]{2,1,0:T(8,128)(2,1)S(1)}, u32[]{:S(2)}, u32[]{:S(2)}) async-start(bf16[4,128,512]{2,1,0:T(8,128)(2,1)} %get-tuple-element.17.refs_3_), calls=%async_computation.2 | async-start | bytes 1048576 | tf_op jit(solution)/shard_map/all_to_all | solution.py:194
  77.5 1.9 %collective-permute-start.3 = (bf16[8,128,256]{2,1,0:T(8,128)(2,1)S(1)}, bf16[8,128,256]{2,1,0:T(8,128)(2,1)S(1)}, u32[]{:S(2)}, u32[]{:S(2)}) collective-permute-start(bf16[8,128,256]{2,1,0:T(8,128)(2,1)S(1)} %copy-done.7), channel_id=1, source_target_pairs={{0,1},{1,0},{2,3},{3,2},{4,5},{5,4},{6,7},{7,6},{8,9},{9,8},{10,11... | collective-permute-start | bytes 1572872 | tf_op jit(solution)/shard_map/ppermute | solution.py:190
  79.4 1.9 %collective-permute-done.3.refs_1_ = bf16[8,128,256]{2,1,0:T(8,128)(2,1)S(1)} collective-permute-done((bf16[8,128,256]{2,1,0:T(8,128)(2,1)S(1)}, bf16[8,128,256]{2,1,0:T(8,128)(2,1)S(1)}, u32[]{:S(2)}, u32[]{:S(2)}) %collective-permute-start.3) | collective-permute-done | bytes 524320 | tf_op jit(solution)/shard_map/ppermute | solution.py:190
  81.3 8.7 %all-to-all-done.2.refs_2_.refs_0_ = bf16[4,128,512]{2,1,0:T(8,128)(2,1)S(1)} async-done(((bf16[4,128,512]{2,1,0:T(8,128)(2,1)}), bf16[4,128,512]{2,1,0:T(8,128)(2,1)S(1)}, u32[]{:S(2)}, u32[]{:S(2)}) %all-to-all-start.2) | async-done | bytes 524320 | tf_op jit(solution)/shard_map/all_to_all | solution.py:194
  90.9 5.0 %all-to-all-start.3 = ((bf16[8,128,256]{2,1,0:T(8,128)(2,1)}), bf16[8,128,256]{2,1,0:T(8,128)(2,1)S(1)}, u32[]{:S(2)}, u32[]{:S(2)}) async-start(bf16[8,128,256]{2,1,0:T(8,128)(2,1)} %shard_map.114), calls=%async_computation.3 | async-start | bytes 1048576 | tf_op jit(solution)/shard_map/all_to_all | solution.py:194
  96.6 1.3 collective-permute-start.5
  97.9 1.6 %shard_map.118.refs_0_ = f32[32,128]{1,0:T(8,128)S(1)} custom-call(bf16[128,512]{1,0:T(8,128)(2,1)S(1)} %get-tuple-element.23.refs_1_.refs_0_, bf16[128,512]{1,0:T(8,128)(2,1)S(1)} %multiply_convert_fusion.refs_1_, bf16[128,512]{1,0:T(8,128)(2,1)S(1)} %copy-done.14), custom_call_target="tpu_custom_call" | custom-call | flops 268435456 | bytes 409600 | tf_op jit(solution)/shard_map/pallas_call | solution.py:36
  99.5 4.1 %collective-permute-done.5.refs_2_ = bf16[128,512]{1,0:T(8,128)(2,1)S(1)} collective-permute-done((bf16[128,512]{1,0:T(8,128)(2,1)S(1)}, bf16[128,512]{1,0:T(8,128)(2,1)S(1)}, u32[]{:S(2)}, u32[]{:S(2)}) %collective-permute-start.5) | collective-permute-done | bytes 131104 | tf_op jit(solution)/shard_map/ppermute | solution.py:184
  104.5 9.3 %all-to-all-start.4 = ((bf16[32,32,128]{2,1,0:T(8,128)(2,1)}), bf16[32,32,128]{2,1,0:T(8,128)(2,1)S(1)}, u32[]{:S(2)}, u32[]{:S(2)}) async-start(bf16[32,32,128]{2,1,0:T(8,128)(2,1)} %shard_map.119), calls=%async_computation.4 | async-start | bytes 524288 | tf_op jit(solution)/shard_map/all_to_all | solution.py:273
  114.8 1.7 %shard_map.117 = (bf16[128,512]{1,0:T(8,128)(2,1)}, bf16[128,512]{1,0:T(8,128)(2,1)}) custom-call(f32[32,128]{1,0:T(8,128)S(1)} %bitcast.12, bf16[128,512]{1,0:T(8,128)(2,1)S(1)} %get-tuple-element.23.refs_1_.refs_0_, bf16[128,512]{1,0:T(8,128)(2,1)S(1)} %collective-permute-done.5.refs_2_, bf16[128,512]{1,0:T(8,128)(2,1)S(1)} %copy-done.9, ...), custom_call_target="tpu_custom_call" | custom-call | flops 1073741824 | bytes 802816 | tf_op jit(solution)/shard_map/pallas_call | solution.py:36
  116.4 1.6 %bitcast_convert_fusion = f32[512,128]{1,0:T(8,128)} fusion(bf16[1,512,128]{2,1,0:T(8,128)(2,1)} %reduce-scatter.2.cloned.1.call-done), kind=kLoop, calls=%fused_computation.2 | loop fusion | flops 65536 | bytes 393216 | tf_op jit(solution)/shard_map/convert_element_type | solution.py:277
  118.0 9.0 %all-to-all-done.4 = bf16[32,32,128]{2,1,0:T(8,128)(2,1)S(1)} async-done(((bf16[32,32,128]{2,1,0:T(8,128)(2,1)}), bf16[32,32,128]{2,1,0:T(8,128)(2,1)S(1)}, u32[]{:S(2)}, u32[]{:S(2)}) %all-to-all-start.4) | async-done | bytes 262176 | tf_op jit(solution)/shard_map/all_to_all | solution.py:273
  (54 shorter events, 11.0 us)
Async XLA Ops:
  7.2 5.5 %copy-start.15 = (bf16[128,256]{1,0:T(8,128)(2,1)S(1)}, bf16[128,256]{1,0:T(8,128)(2,1)}, u32[]{:S(2)}) copy-start(bf16[128,256]{1,0:T(8,128)(2,1)} %param.11) | copy-start | bytes 196612
  7.2 54.5 %all-gather.3.cloned.1.call-start = ((), (), s32[]{:S(2)}) async-start(), calls=%async_computation.7 | async-start | bytes 1179648 | tf_op jit(solution)/shard_map/all_gather | solution.py:210
  7.2 6.2 %copy-start.12 = (f32[128,32]{0,1:T(8,128)S(1)}, f32[128,32]{0,1:T(8,128)}, u32[]{:S(2)}) copy-start(f32[128,32]{0,1:T(8,128)} %param.9) | copy-start | bytes 49156
  8.2 7.2 %copy-start.10 = (bf16[128,512]{1,0:T(8,128)(2,1)S(1)}, bf16[128,512]{1,0:T(8,128)(2,1)}, u32[]{:S(2)}) copy-start(bf16[128,512]{1,0:T(8,128)(2,1)} %refs_1_.1) | copy-start | bytes 393220
  8.3 7.2 %collective-permute-start = (bf16[128,512]{1,0:T(8,128)(2,1)S(1)}, bf16[128,512]{1,0:T(8,128)(2,1)S(1)}, u32[]{:S(2)}, u32[]{:S(2)}) collective-permute-start(bf16[128,512]{1,0:T(8,128)(2,1)S(1)} %multiply_convert_fusion.refs_1_), channel_id=1, source_target_pairs={{0,16},{16,32},{32,48},{48,64},{64,80},{80,96},{96,112},{112,128},... | collective-permute-start | bytes 393224 | tf_op jit(solution)/shard_map/ppermute | solution.py:184
  12.7 4.4 %collective-permute-start.1 = (bf16[128,256]{1,0:T(8,128)(2,1)S(1)}, bf16[128,256]{1,0:T(8,128)(2,1)S(1)}, u32[]{:S(2)}, u32[]{:S(2)}) collective-permute-start(bf16[128,256]{1,0:T(8,128)(2,1)S(1)} %copy-done.15), channel_id=1, source_target_pairs={{0,0},{1,1},{2,2},{3,3},{4,128},{5,129},{6,130},{7,131},{8,256},{9... | collective-permute-start | bytes 196616 | tf_op jit(solution)/shard_map/ppermute | solution.py:204
  15.4 1.6 %copy-start.13 = (bf16[128,512]{1,0:T(8,128)(2,1)}, bf16[128,512]{1,0:T(8,128)(2,1)S(1)}, u32[]{:S(2)}) copy-start(bf16[128,512]{1,0:T(8,128)(2,1)S(1)} %collective-permute-done.refs_2_) | copy-start | bytes 393220
  37.6 28.6 %all-to-all-start.1 = ((bf16[4,128,512]{2,1,0:T(8,128)(2,1)}), bf16[4,128,512]{2,1,0:T(8,128)(2,1)S(1)}, u32[]{:S(2)}, u32[]{:S(2)}) async-start(bf16[4,128,512]{2,1,0:T(8,128)(2,1)} %shard_map.111), calls=%async_computation.1 | async-start | bytes 1048576 | tf_op jit(solution)/shard_map/all_to_all | solution.py:194
  49.1 67.4 %reduce-scatter.2.cloned.1.call-start = ((), (), s32[]{:S(2)}) async-start(), calls=%async_computation.6 | async-start | bytes 1179648 | tf_op jit(solution)/shard_map/reduce_scatter | solution.py:277
  49.1 3.8 %collective-permute-start.2 = (bf16[8,128,256]{2,1,0:T(8,128)(2,1)S(1)}, bf16[8,128,256]{2,1,0:T(8,128)(2,1)S(1)}, u32[]{:S(2)}, u32[]{:S(2)}) collective-permute-start(bf16[8,128,256]{2,1,0:T(8,128)(2,1)S(1)} %all_to_all.25.refs_1_), channel_id=1, source_target_pairs={{0,1},{1,0},{2,3},{3,2},{4,5},{5,4},{6,7},{7,6},{8,9},{9,8},{10,11... | collective-permute-start | bytes 1572872 | tf_op jit(solution)/shard_map/ppermute | solution.py:190
  61.7 1.2 copy-start
  62.9 1.0 copy-start.5
  64.0 2.3 %copy-start.1 = (bf16[4096,128]{1,0:T(8,128)(2,1)S(1)}, bf16[4096,128]{1,0:T(8,128)(2,1)}, u32[]{:S(2)}) copy-start(bf16[4096,128]{1,0:T(8,128)(2,1)} %all-gather.3.cloned.1.call-done) | copy-start | bytes 3145732
  67.1 1.0 copy-start.2
  70.6 19.4 %copy-start.3 = (f32[8,128,256]{2,1,0:T(8,128)S(1)}, f32[8,128,256]{2,1,0:T(8,128)}, u32[]{:S(2)}) copy-start(f32[8,128,256]{2,1,0:T(8,128)} %copy-done.2) | copy-start | bytes 3145732
  70.6 6.9 %copy-start.7 = (bf16[8,128,256]{2,1,0:T(8,128)(2,1)S(1)}, bf16[8,128,256]{2,1,0:T(8,128)(2,1)}, u32[]{:S(2)}) copy-start(bf16[8,128,256]{2,1,0:T(8,128)(2,1)} %copy-done.6) | copy-start | bytes 1572868
  70.6 19.4 %all-to-all-start.2 = ((bf16[4,128,512]{2,1,0:T(8,128)(2,1)}), bf16[4,128,512]{2,1,0:T(8,128)(2,1)S(1)}, u32[]{:S(2)}, u32[]{:S(2)}) async-start(bf16[4,128,512]{2,1,0:T(8,128)(2,1)} %get-tuple-element.17.refs_3_), calls=%async_computation.2 | async-start | bytes 1048576 | tf_op jit(solution)/shard_map/all_to_all | solution.py:194
  77.5 3.8 %collective-permute-start.3 = (bf16[8,128,256]{2,1,0:T(8,128)(2,1)S(1)}, bf16[8,128,256]{2,1,0:T(8,128)(2,1)S(1)}, u32[]{:S(2)}, u32[]{:S(2)}) collective-permute-start(bf16[8,128,256]{2,1,0:T(8,128)(2,1)S(1)} %copy-done.7), channel_id=1, source_target_pairs={{0,1},{1,0},{2,3},{3,2},{4,5},{5,4},{6,7},{7,6},{8,9},{9,8},{10,11... | collective-permute-start | bytes 1572872 | tf_op jit(solution)/shard_map/ppermute | solution.py:190
  90.9 5.0 %copy-start.11 = (bf16[128,512]{1,0:T(8,128)(2,1)S(1)}, bf16[128,512]{1,0:T(8,128)(2,1)}, u32[]{:S(2)}) copy-start(bf16[128,512]{1,0:T(8,128)(2,1)} %refs_1_.1) | copy-start | bytes 393220
  90.9 12.8 %all-to-all-start.3 = ((bf16[8,128,256]{2,1,0:T(8,128)(2,1)}), bf16[8,128,256]{2,1,0:T(8,128)(2,1)S(1)}, u32[]{:S(2)}, u32[]{:S(2)}) async-start(bf16[8,128,256]{2,1,0:T(8,128)(2,1)} %shard_map.114), calls=%async_computation.3 | async-start | bytes 1048576 | tf_op jit(solution)/shard_map/all_to_all | solution.py:194
  95.9 2.0 %copy-start.14 = (bf16[128,512]{1,0:T(8,128)(2,1)S(1)}, bf16[128,512]{1,0:T(8,128)(2,1)}, u32[]{:S(2)}) copy-start(bf16[128,512]{1,0:T(8,128)(2,1)} %copy-done.13) | copy-start | bytes 393220
  96.6 7.0 %collective-permute-start.5 = (bf16[128,512]{1,0:T(8,128)(2,1)S(1)}, bf16[128,512]{1,0:T(8,128)(2,1)S(1)}, u32[]{:S(2)}, u32[]{:S(2)}) collective-permute-start(bf16[128,512]{1,0:T(8,128)(2,1)S(1)} %get-tuple-element.23.refs_1_.refs_0_), channel_id=1, source_target_pairs={{16,0},{32,16},{48,32},{64,48},{80,64},{96,80},{112,96},{128,112},... | collective-permute-start | bytes 393224 | tf_op jit(solution)/shard_map/ppermute | solution.py:184
  104.5 22.6 %all-to-all-start.4 = ((bf16[32,32,128]{2,1,0:T(8,128)(2,1)}), bf16[32,32,128]{2,1,0:T(8,128)(2,1)S(1)}, u32[]{:S(2)}, u32[]{:S(2)}) async-start(bf16[32,32,128]{2,1,0:T(8,128)(2,1)} %shard_map.119), calls=%async_computation.4 | async-start | bytes 524288 | tf_op jit(solution)/shard_map/all_to_all | solution.py:273
  113.9 2.5 %collective-permute-start.4 = (bf16[128,256]{1,0:T(8,128)(2,1)S(1)}, bf16[128,256]{1,0:T(8,128)(2,1)S(1)}, u32[]{:S(2)}, u32[]{:S(2)}) collective-permute-start(bf16[128,256]{1,0:T(8,128)(2,1)S(1)} %reduce_sum.21), channel_id=1, source_target_pairs={{0,0},{1,1},{2,2},{3,3},{4,128},{5,129},{6,130},{7,131},{8,256},{9... | collective-permute-start | bytes 196616 | tf_op jit(solution)/shard_map/ppermute | solution.py:204
  (4 other events, 3.5 us)
Sparse Core Ops, SparseCore 0:
  13.5 48.1 all-gather.2
  70.7 41.2 reduce-scatter.1
